TPU v7x, 256 devices: a whole 4x4x8 slice. The times are simulated.
256 devices in a mesh: wide: 64 (over x, z_lo, y), slab: 4 (over z_hi, core).
Axes of the slice: x: 4, y: 4, z: 8 (z_hi: 2, z_lo: 4; z = z_hi * 4 + z_lo), core: 2. Of those that a mesh axis runs over, the one named last changes fastest.
Arguments:
- volume: bfloat16 [5, 8, 32768], P(None, 'slab', 'wide'), may hold values from -6 to 6
- back_proj: float32 [8, 32768], P('slab', 'wide'), may hold values from -6 to 6
- dual_state: bfloat16 [5, 8, 128, 1024], P(None, 'slab', 'wide'), may hold values from -6 to 6
- sinogram: bfloat16 [8, 128, 1024], P('slab', 'wide'), may hold values from -6 to 6
- offsets: int32 [64, 128], replicated, may hold values from 0 to 960
- primal_first: bfloat16 [3, 3, 3, 6, 32], replicated, may hold values from -0.5 to 0.5
- primal_second: bfloat16 [3, 3, 3, 32, 32], replicated, may hold values from -0.21875 to 0.21875
- primal_third: bfloat16 [3, 3, 3, 32, 5], replicated, may hold values from -0.21875 to 0.21875
- dual_first: bfloat16 [3, 3, 3, 7, 32], replicated, may hold values from -0.4375 to 0.4375
- dual_second: bfloat16 [3, 3, 3, 32, 32], replicated, may hold values from -0.21875 to 0.21875
- dual_third: bfloat16 [3, 3, 3, 32, 5], replicated, may hold values from -0.21875 to 0.21875
Outputs:
- new_volume: bfloat16 [5, 8, 32768], P(None, 'slab', 'wide')
- new_dual: bfloat16 [5, 8, 128, 1024], P(None, 'slab', 'wide')
- new_back: float32 [8, 32768], P('slab', 'wide')
Inputs may be any that keep to these rules, and one draw needn't show every extreme that they name: offsets[t, a] is where tile t's window of 64 bins begins on the detector at angle a.
All inputs are finite; a program needn't handle non-finite values.
Results may differ from a plain program's by a relative error of at most 0.005.
Values may be sent and summed in bfloat16 or wider, within the bound.
No kernel may reach another device: no remote copies, remote signals or barrier semaphores. Data moves between devices by JAX's collectives and lax.ppermute only.
A program may use at most 64 MiB of HBM per device.

v0:
```python
import math

import jax
import jax.numpy as jnp
from jax import lax
from jax.sharding import PartitionSpec as P

NY = 32
TX = 16


def extended(shard, sides, width):
    for axis, dim in sides:
        size, length = (lax.axis_size(axis), shard.shape[dim])
        up = [(i, (i + 1) % size) for i in range(size - 1)]
        down = [(j, i) for i, j in up]
        last = lax.slice_in_dim(shard, length - width, length, axis=dim)
        first = lax.slice_in_dim(shard, 0, width, axis=dim)
        before = lax.ppermute(last, axis, up)
        after = lax.ppermute(first, axis, down)
        shard = jnp.concatenate([before, shard, after], axis=dim)
    return shard


def make_table(angle_ids, angle_total, rows_x, cols_y):
    window_bins = cols_y + 2 * rows_x
    angle_value = angle_ids.astype(jnp.float32) * (math.pi / angle_total)
    pixels = jnp.arange(rows_x * cols_y, dtype=jnp.int32)
    centre_x = (pixels // cols_y).astype(jnp.float32) - (rows_x - 1) / 2.0
    centre_y = (pixels % cols_y).astype(jnp.float32) - (cols_y - 1) / 2.0
    positions = (
        centre_x[None, :] * jnp.cos(angle_value)[:, None]
        + centre_y[None, :] * jnp.sin(angle_value)[:, None]
        + window_bins / 2.0
    )
    detector = jnp.arange(window_bins, dtype=jnp.int32).astype(jnp.float32)
    return jnp.maximum(0.0, 1.0 - jnp.abs(positions[:, :, None] - detector)).astype(jnp.bfloat16)


def conv_core(framed, weights):
    slice_count = framed.shape[1] - 2
    across_count = framed.shape[2] - 2
    bin_count = framed.shape[3] - 2
    accumulated = jnp.zeros((weights.shape[4], slice_count, across_count, bin_count), jnp.float32)
    for tap_depth in range(3):
        for tap_across in range(3):
            for tap_bin in range(3):
                window = framed[
                    :,
                    tap_depth : tap_depth + slice_count,
                    tap_across : tap_across + across_count,
                    tap_bin : tap_bin + bin_count,
                ]
                accumulated = accumulated + jnp.einsum(
                    "czab,co->ozab",
                    window,
                    weights[tap_depth, tap_across, tap_bin],
                    preferred_element_type=jnp.float32,
                )
    return accumulated


def conv_valid(padded, weights):
    return conv_core(jnp.pad(padded, ((0, 0), (0, 0), (0, 0), (1, 1))), weights)


def volume_halo(field):
    return extended(field, (("wide", 2), ("slab", 1)), 1)


def angle_halo(field):
    return extended(field, (("wide", 2), ("slab", 1)), 1)


def selector_block(block_offsets, window_bins, bin_total):
    detector = jnp.arange(bin_total, dtype=jnp.int32)
    window_ids = jnp.arange(window_bins, dtype=jnp.int32)
    shifted = detector[None, None, None, :] - block_offsets[:, :, None, None]
    return (shifted == window_ids[None, None, :, None]).astype(jnp.bfloat16)


def tile_blocks(tile_offsets):
    tile_count = tile_offsets.shape[0]
    group_size = math.gcd(tile_count, 4)
    return (
        tile_offsets.reshape(tile_count // group_size, group_size, tile_offsets.shape[1]),
        group_size,
    )


def cut_tiles(by_angle, tile_offsets, window_bins):
    tile_count = tile_offsets.shape[0]
    bin_total = by_angle.shape[2]
    block_list, group_size = tile_blocks(tile_offsets)

    def cut_block(block_offsets):
        chooser = selector_block(block_offsets, window_bins, bin_total)
        return jnp.einsum(
            "azb,tajb->tazj", by_angle, chooser, preferred_element_type=jnp.float32
        ).astype(jnp.bfloat16)

    pieces = lax.map(cut_block, block_list)
    return pieces.reshape(tile_count, by_angle.shape[0], by_angle.shape[1], window_bins)


def place_tiles(arrived, tile_offsets, bin_total):
    tile_count = arrived.shape[0]
    window_bins = arrived.shape[3]
    block_list, group_size = tile_blocks(tile_offsets)
    arrived_blocks = arrived.reshape(
        tile_count // group_size, group_size, arrived.shape[1], arrived.shape[2], window_bins
    )

    def place_block(running, inputs):
        block_offsets, block_windows = inputs
        chooser = selector_block(block_offsets, window_bins, bin_total)
        term = jnp.einsum(
            "tazj,tajb->azb", block_windows, chooser, preferred_element_type=jnp.float32
        )
        return (running + term, None)

    start = jnp.zeros((arrived.shape[1], arrived.shape[2], bin_total), jnp.float32)
    return lax.scan(place_block, start, (block_list, arrived_blocks))[0]


def primal_update(volume, back_proj, primal_first, primal_second, primal_third):
    channels = volume.shape[0]
    slices = volume.shape[1]
    grid_view = volume.reshape(channels, slices, TX, NY)
    extra_channel = back_proj.astype(jnp.bfloat16).reshape(1, slices, TX, NY)
    stacked = jnp.concatenate([grid_view, extra_channel], axis=0)
    hidden = jax.nn.relu(conv_valid(volume_halo(stacked), primal_first)).astype(jnp.bfloat16)
    hidden = jax.nn.relu(conv_valid(volume_halo(hidden), primal_second)).astype(jnp.bfloat16)
    result = grid_view.astype(jnp.float32) + conv_valid(volume_halo(hidden), primal_third)
    return result.astype(jnp.bfloat16).reshape(channels, slices, TX * NY)


def dual_update(dual_state, projected, sinogram, dual_first, dual_second, dual_third):
    stacked = jnp.concatenate([dual_state, projected[None], sinogram[None]], axis=0)
    first_hidden = jax.nn.relu(conv_valid(angle_halo(stacked), dual_first)).astype(jnp.bfloat16)
    second_hidden = jax.nn.relu(conv_valid(angle_halo(first_hidden), dual_second)).astype(
        jnp.bfloat16
    )
    update = conv_valid(angle_halo(second_hidden), dual_third)
    return (dual_state.astype(jnp.float32) + update).astype(jnp.bfloat16)


def body(
    volume,
    back_proj,
    dual_state,
    sinogram,
    offsets,
    primal_first,
    primal_second,
    primal_third,
    dual_first,
    dual_second,
    dual_third,
):
    new_volume = primal_update(volume, back_proj, primal_first, primal_second, primal_third)
    slices = volume.shape[1]
    pixel_count = volume.shape[2]
    angles_here = dual_state.shape[2]
    bin_total = dual_state.shape[3]
    wide_count = lax.axis_size("wide")
    angle_total = angles_here * wide_count
    window_bins = NY + 2 * TX
    leading = new_volume[0]
    kept = make_table(jnp.arange(angle_total, dtype=jnp.int32), angle_total, TX, NY)
    windows = jnp.einsum("zp,apj->azj", leading, kept, preferred_element_type=jnp.float32)
    outgoing = windows.astype(jnp.bfloat16).reshape(wide_count, angles_here, slices, window_bins)
    arrived = lax.all_to_all(outgoing, "wide", split_axis=0, concat_axis=0, tiled=True)
    own_offsets = lax.dynamic_slice_in_dim(
        offsets, lax.axis_index("wide") * angles_here, angles_here, 1
    )
    placed = place_tiles(arrived, own_offsets, bin_total)
    projected = (placed * (1.0 / math.sqrt(NY))).transpose(1, 0, 2).astype(jnp.bfloat16)
    new_dual = dual_update(dual_state, projected, sinogram, dual_first, dual_second, dual_third)
    by_angle = new_dual[0].transpose(1, 0, 2)
    own_ids = lax.axis_index("wide") * angles_here + jnp.arange(angles_here, dtype=jnp.int32)
    own_table = make_table(own_ids, angle_total, TX, NY)
    tile_pieces = cut_tiles(by_angle, own_offsets, window_bins)
    part_sum = jnp.einsum(
        "tazj,apj->tzp", tile_pieces, own_table, preferred_element_type=jnp.float32
    )
    summed = lax.psum_scatter(
        part_sum.reshape(lax.axis_size("wide") * slices, pixel_count),
        "wide",
        scatter_dimension=0,
        tiled=True,
    )
    new_back = summed * (1.0 / math.sqrt(angle_total))
    return (new_volume, new_dual, new_back)


def solution(mesh):
    in_specs = (
        P(None, "slab", "wide"),
        P("slab", "wide"),
        P(None, "slab", "wide", None),
        P("slab", "wide", None),
        P(),
        P(),
        P(),
        P(),
        P(),
        P(),
        P(),
    )
    out_specs = (P(None, "slab", "wide"), P(None, "slab", "wide", None), P("slab", "wide"))
    return jax.shard_map(body, mesh=mesh, in_specs=in_specs, out_specs=out_specs, check_vma=False)
```

profile of v0, /device:TPU:2, one launch (start us, length us, event | category | flops | bytes accessed | tf_op | source)
XLA Modules:
  0.0 905.0 jit_solution(16854678839682925879)
XLA Ops:
  8.8 3.5 collective-permute-start
  12.3 7.4 collective-permute-start.1
  23.8 8.9 collective-permute-done.3
  42.4 9.0 collective-permute-start.5
  52.9 7.6 collective-permute-start.6
  61.9 2.3 collective-permute-done.7
  74.1 9.0 collective-permute-start.9
  84.6 8.7 collective-permute-start.10
  102.3 2.6 fusion.148
  105.8 13.2 %all-to-all-start = ((bf16[64,2,128]{2,1,0:T(2,128)(2,1)}), bf16[64,2,128]{2,1,0:T(2,128)(2,1)S(1)}, u32[]{:S(2)}, u32[]{:S(2)}) async-start(bf16[64,2,128]{2,1,0:T(2,128)(2,1)} %reshape.388), calls=%async_computation | async-start | bytes 65536 | tf_op jit(solution)/shard_map/all_to_all | solution.py:173
  119.5 8.6 all-to-all-done
  128.2 8.7 while.22
  137.0 2.5 collective-permute-start.12
  139.5 8.2 collective-permute-start.13
  149.4 6.9 collective-permute-start.14
  157.9 3.5 collective-permute-done.15
  171.4 9.0 collective-permute-start.17
  183.1 8.0 collective-permute-start.18
  192.5 2.3 collective-permute-done.19
  205.0 9.2 %collective-permute-start.21 = (bf16[32,2,1,1024]{3,0,2,1:T(8,128)(2,1)S(1)}, bf16[32,2,1,1024]{3,0,2,1:T(8,128)(2,1)S(1)}, u32[]{:S(2)}, u32[]{:S(2)}) collective-permute-start(bf16[32,2,1,1024]{3,0,2,1:T(8,128)(2,1)S(1)} %get-tuple-element.126), channel_id=1, source_target_pairs={{4,0},{8,4},{12,8},{16,12},{20,16},{24,20},{28,24},{32,28},{36,32}... | collective-permute-start | bytes 393224 | tf_op jit(solution)/shard_map/ppermute | solution.py:20
  216.8 9.7 %collective-permute-start.22 = (bf16[32,1,4,1024]{3,0,2,1:T(8,128)(2,1)S(1)}, bf16[32,1,4,1024]{3,0,2,1:T(8,128)(2,1)S(1)}, u32[]{:S(2)}, u32[]{:S(2)}) collective-permute-start(bf16[32,1,4,1024]{3,0,2,1:T(8,128)(2,1)S(1)} %get-tuple-element.113), channel_id=1, source_target_pairs={{0,1},{1,2},{2,3},{4,5},{5,6},{6,7},{8,9},{9,10},{10,11},{12,13},{... | collective-permute-start | bytes 786440 | tf_op jit(solution)/shard_map/ppermute | solution.py:19
  228.1 4.2 collective-permute-done.23
  237.8 10.0 %while.21 = (s32[]{:T(128)}, bf16[16,4,2,2,64]{4,1,0,3,2:T(4,128)(2,1)S(1)}, s32[16,4,2]{1,2,0:T(2,128)S(1)}, bf16[2,2,1024]{2,1,0:T(2,128)(2,1)S(1)}, s32[]{:T(128)}) while((s32[]{:T(128)}, bf16[16,4,2,2,64]{4,1,0,3,2:T(4,128)(2,1)S(1)}, s32[16,4,2]{1,2,0:T(2,128)S(1)}, bf16[2,2,1024]{2,1,0:T(2,128)(2,1)S(1)}, s32[]{:T(128)}) %tuple.125), condition=%wide.region_3.4_spmd, body=%wide.region_2.3_spmd.sunk | while | flops 2630658 | bytes 84133 | solution.py:102
  251.6 645.2 %all-reduce.9.cloned.1.call-done = f32[128,512]{1,0:T(8,128)} async-done(((f32[128,512]{1,0:T(8,128)}), f32[128,512]{1,0:T(8,128)}) %all-reduce.9.cloned.1.call-update) | async-done | bytes 262160
  (408 shorter events, 98.8 us)
Async XLA Ops:
  8.8 11.9 %collective-permute-start = (bf16[6,2,1,32]{3,0,2,1:T(8,128)(2,1)S(1)}, bf16[6,2,1,32]{3,0,2,1:T(8,128)(2,1)S(1)}, u32[]{:S(2)}, u32[]{:S(2)}) collective-permute-start(bf16[6,2,1,32]{3,0,2,1:T(8,128)(2,1)S(1)} %get-tuple-element.135), channel_id=1, source_target_pairs={{0,4},{4,8},{8,12},{12,16},{16,20},{20,24},{24,28},{28,32},{32,36}... | collective-permute-start | bytes 2312 | tf_op jit(solution)/shard_map/ppermute | solution.py:19
  12.3 8.7 collective-permute-start.1
  22.4 10.3 %collective-permute-start.3 = (bf16[6,1,18,32]{3,0,2,1:T(8,128)(2,1)S(1)}, bf16[6,1,18,32]{3,0,2,1:T(8,128)(2,1)S(1)}, u32[]{:S(2)}, u32[]{:S(2)}) collective-permute-start(bf16[6,1,18,32]{3,0,2,1:T(8,128)(2,1)S(1)} %get-tuple-element.138), channel_id=1, source_target_pairs={{1,0},{2,1},{3,2},{5,4},{6,5},{7,6},{9,8},{10,9},{11,10},{13,12},{... | collective-permute-start | bytes 20744 | tf_op jit(solution)/shard_map/ppermute | solution.py:20
  40.4 11.0 %collective-permute-start.4 = (bf16[32,2,1,32]{3,0,2,1:T(8,128)(2,1)S(1)}, bf16[32,2,1,32]{3,0,2,1:T(8,128)(2,1)S(1)}, u32[]{:S(2)}, u32[]{:S(2)}) collective-permute-start(bf16[32,2,1,32]{3,0,2,1:T(8,128)(2,1)S(1)} %get-tuple-element.131), channel_id=1, source_target_pairs={{0,4},{4,8},{8,12},{12,16},{16,20},{20,24},{24,28},{28,32},{32,36}... | collective-permute-start | bytes 12296 | tf_op jit(solution)/shard_map/ppermute | solution.py:19
  42.4 10.4 %collective-permute-start.5 = (bf16[32,2,1,32]{3,0,2,1:T(8,128)(2,1)S(1)}, bf16[32,2,1,32]{3,0,2,1:T(8,128)(2,1)S(1)}, u32[]{:S(2)}, u32[]{:S(2)}) collective-permute-start(bf16[32,2,1,32]{3,0,2,1:T(8,128)(2,1)S(1)} %get-tuple-element.132), channel_id=1, source_target_pairs={{4,0},{8,4},{12,8},{16,12},{20,16},{24,20},{28,24},{32,28},{36,32}... | collective-permute-start | bytes 12296 | tf_op jit(solution)/shard_map/ppermute | solution.py:20
  52.9 9.0 collective-permute-start.6
  60.5 3.6 collective-permute-start.7
  72.1 11.0 %collective-permute-start.8 = (bf16[32,2,1,32]{3,0,2,1:T(8,128)(2,1)S(1)}, bf16[32,2,1,32]{3,0,2,1:T(8,128)(2,1)S(1)}, u32[]{:S(2)}, u32[]{:S(2)}) collective-permute-start(bf16[32,2,1,32]{3,0,2,1:T(8,128)(2,1)S(1)} %get-tuple-element.129), channel_id=1, source_target_pairs={{0,4},{4,8},{8,12},{12,16},{16,20},{20,24},{24,28},{28,32},{32,36}... | collective-permute-start | bytes 12296 | tf_op jit(solution)/shard_map/ppermute | solution.py:19
  74.1 10.4 %collective-permute-start.9 = (bf16[32,2,1,32]{3,0,2,1:T(8,128)(2,1)S(1)}, bf16[32,2,1,32]{3,0,2,1:T(8,128)(2,1)S(1)}, u32[]{:S(2)}, u32[]{:S(2)}) collective-permute-start(bf16[32,2,1,32]{3,0,2,1:T(8,128)(2,1)S(1)} %get-tuple-element.130), channel_id=1, source_target_pairs={{4,0},{8,4},{12,8},{16,12},{20,16},{24,20},{28,24},{32,28},{36,32}... | collective-permute-start | bytes 12296 | tf_op jit(solution)/shard_map/ppermute | solution.py:20
  84.6 10.3 %collective-permute-start.10 = (bf16[32,1,18,32]{3,0,2,1:T(8,128)(2,1)S(1)}, bf16[32,1,18,32]{3,0,2,1:T(8,128)(2,1)S(1)}, u32[]{:S(2)}, u32[]{:S(2)}) collective-permute-start(bf16[32,1,18,32]{3,0,2,1:T(8,128)(2,1)S(1)} %get-tuple-element.119), channel_id=1, source_target_pairs={{0,1},{1,2},{2,3},{4,5},{5,6},{6,7},{8,9},{9,10},{10,11},{12,13},{... | collective-permute-start | bytes 110600 | tf_op jit(solution)/shard_map/ppermute | solution.py:19
  105.8 22.3 %all-to-all-start = ((bf16[64,2,128]{2,1,0:T(2,128)(2,1)}), bf16[64,2,128]{2,1,0:T(2,128)(2,1)S(1)}, u32[]{:S(2)}, u32[]{:S(2)}) async-start(bf16[64,2,128]{2,1,0:T(2,128)(2,1)} %reshape.388), calls=%async_computation | async-start | bytes 65536 | tf_op jit(solution)/shard_map/all_to_all | solution.py:173
  119.1 777.7 %all-reduce.9.cloned.1.call-start = ((), (), s32[]{:S(2)}) async-start(), calls=%async_computation.1 | async-start | bytes 524288
  137.0 10.7 %collective-permute-start.12 = (bf16[7,2,1,1024]{3,0,2,1:T(8,128)(2,1)S(1)}, bf16[7,2,1,1024]{3,0,2,1:T(8,128)(2,1)S(1)}, u32[]{:S(2)}, u32[]{:S(2)}) collective-permute-start(bf16[7,2,1,1024]{3,0,2,1:T(8,128)(2,1)S(1)} %get-tuple-element.139), channel_id=1, source_target_pairs={{0,4},{4,8},{8,12},{12,16},{16,20},{20,24},{24,28},{28,32},{32,36}... | collective-permute-start | bytes 86024 | tf_op jit(solution)/shard_map/ppermute | solution.py:19
  139.5 9.8 %collective-permute-start.13 = (bf16[7,2,1,1024]{3,0,2,1:T(8,128)(2,1)S(1)}, bf16[7,2,1,1024]{3,0,2,1:T(8,128)(2,1)S(1)}, u32[]{:S(2)}, u32[]{:S(2)}) collective-permute-start(bf16[7,2,1,1024]{3,0,2,1:T(8,128)(2,1)S(1)} %get-tuple-element.140), channel_id=1, source_target_pairs={{4,0},{8,4},{12,8},{16,12},{20,16},{24,20},{28,24},{32,28},{36,32}... | collective-permute-start | bytes 86024 | tf_op jit(solution)/shard_map/ppermute | solution.py:20
  149.4 8.5 collective-permute-start.14
  156.3 5.1 collective-permute-start.15
  169.3 12.0 %collective-permute-start.16 = (bf16[32,2,1,1024]{3,0,2,1:T(8,128)(2,1)S(1)}, bf16[32,2,1,1024]{3,0,2,1:T(8,128)(2,1)S(1)}, u32[]{:S(2)}, u32[]{:S(2)}) collective-permute-start(bf16[32,2,1,1024]{3,0,2,1:T(8,128)(2,1)S(1)} %get-tuple-element.127), channel_id=1, source_target_pairs={{0,4},{4,8},{8,12},{12,16},{16,20},{20,24},{24,28},{28,32},{32,36}... | collective-permute-start | bytes 393224 | tf_op jit(solution)/shard_map/ppermute | solution.py:19
  171.4 11.5 %collective-permute-start.17 = (bf16[32,2,1,1024]{3,0,2,1:T(8,128)(2,1)S(1)}, bf16[32,2,1,1024]{3,0,2,1:T(8,128)(2,1)S(1)}, u32[]{:S(2)}, u32[]{:S(2)}) collective-permute-start(bf16[32,2,1,1024]{3,0,2,1:T(8,128)(2,1)S(1)} %get-tuple-element.128), channel_id=1, source_target_pairs={{4,0},{8,4},{12,8},{16,12},{20,16},{24,20},{28,24},{32,28},{36,32}... | collective-permute-start | bytes 393224 | tf_op jit(solution)/shard_map/ppermute | solution.py:20
  183.1 9.5 %collective-permute-start.18 = (bf16[32,1,4,1024]{3,0,2,1:T(8,128)(2,1)S(1)}, bf16[32,1,4,1024]{3,0,2,1:T(8,128)(2,1)S(1)}, u32[]{:S(2)}, u32[]{:S(2)}) collective-permute-start(bf16[32,1,4,1024]{3,0,2,1:T(8,128)(2,1)S(1)} %get-tuple-element.117), channel_id=1, source_target_pairs={{0,1},{1,2},{2,3},{4,5},{5,6},{6,7},{8,9},{9,10},{10,11},{12,13},{... | collective-permute-start | bytes 786440 | tf_op jit(solution)/shard_map/ppermute | solution.py:19
  191.1 3.7 collective-permute-start.19
  203.1 12.1 %collective-permute-start.20 = (bf16[32,2,1,1024]{3,0,2,1:T(8,128)(2,1)S(1)}, bf16[32,2,1,1024]{3,0,2,1:T(8,128)(2,1)S(1)}, u32[]{:S(2)}, u32[]{:S(2)}) collective-permute-start(bf16[32,2,1,1024]{3,0,2,1:T(8,128)(2,1)S(1)} %get-tuple-element.125), channel_id=1, source_target_pairs={{0,4},{4,8},{8,12},{12,16},{16,20},{20,24},{24,28},{28,32},{32,36}... | collective-permute-start | bytes 393224 | tf_op jit(solution)/shard_map/ppermute | solution.py:19
  205.0 11.7 %collective-permute-start.21 = (bf16[32,2,1,1024]{3,0,2,1:T(8,128)(2,1)S(1)}, bf16[32,2,1,1024]{3,0,2,1:T(8,128)(2,1)S(1)}, u32[]{:S(2)}, u32[]{:S(2)}) collective-permute-start(bf16[32,2,1,1024]{3,0,2,1:T(8,128)(2,1)S(1)} %get-tuple-element.126), channel_id=1, source_target_pairs={{4,0},{8,4},{12,8},{16,12},{20,16},{24,20},{28,24},{32,28},{36,32}... | collective-permute-start | bytes 393224 | tf_op jit(solution)/shard_map/ppermute | solution.py:20
  216.8 11.4 %collective-permute-start.22 = (bf16[32,1,4,1024]{3,0,2,1:T(8,128)(2,1)S(1)}, bf16[32,1,4,1024]{3,0,2,1:T(8,128)(2,1)S(1)}, u32[]{:S(2)}, u32[]{:S(2)}) collective-permute-start(bf16[32,1,4,1024]{3,0,2,1:T(8,128)(2,1)S(1)} %get-tuple-element.113), channel_id=1, source_target_pairs={{0,1},{1,2},{2,3},{4,5},{5,6},{6,7},{8,9},{9,10},{10,11},{12,13},{... | collective-permute-start | bytes 786440 | tf_op jit(solution)/shard_map/ppermute | solution.py:19
  226.5 5.8 collective-permute-start.23
  (13 other events, 917.2 us)
Sparse Core Ops, SparseCore 0:
  249.0 647.7 all-reduce.8
where the time goes:
time: 921 us; the launch traced here: 905 us
  waiting for transfers between devices  686 us (74%)
  starting transfers between devices  129 us (14%)
  matrix products  59.7 us (6%)
  between operations  16.2 us (2%)
    unnamed x2, waiting for transfers between devices  645 us
    ppermute x12, starting transfers between devices, extended(): after = lax.ppermute(first, axis, down)  59.7 us
    ppermute x12, starting transfers between devices, extended(): before = lax.ppermute(last, axis, up)  56.2 us
    dot_general x162, matrix products, conv_core(): jnp.einsum('czab,co->ozab', window, weights[tap_depth, tap_across, tap_bi...  40.7 us
    ppermute x12, waiting for transfers between devices, extended(): after = lax.ppermute(first, axis, down)  30.7 us
  transfers between devices with their start and end apart: 26, of which 16 were waited for; matrix products, arithmetic and copies ran while one was open for 0% of the time, Pallas kernels for 0%

commit v1 on v0

v1 whole, which is shorter than its diff:
```python
import math

import jax
import jax.numpy as jnp
from jax import lax
from jax.experimental import pallas as pl
from jax.experimental.pallas import tpu as pltpu
from jax.sharding import PartitionSpec as P

NY = 32
TX = 16
BINS = NY + 2 * TX
HALO = 3
BF = jnp.bfloat16
F32 = jnp.float32
VMEM_BYTES = 48 * 1024 * 1024


def shifted(axis, delta, value):
    size = lax.axis_size(axis)
    return lax.ppermute(value, axis, [(i, i + delta) for i in range(size) if 0 <= i + delta < size])


def band(zo, zi_count):
    zi = jnp.arange(zi_count, dtype=jnp.int32)
    d = jnp.arange(3, dtype=jnp.int32)
    return ((zi[None, :, None] - zo[:, None, None] + 1) == d[None, None, :]).astype(BF)


def hidden_weights(w, nz):
    c, o = w.shape[3], w.shape[4]
    base = w.transpose(4, 1, 2, 0, 3).reshape(o, 9, 3 * c)
    width = nz * c
    wide = jnp.pad(base, ((0, 0), (0, 0), (width - c, width - 2 * c)))
    rows = [wide[:, :, (nz - zo) * c : (nz - zo) * c + width] for zo in range(nz)]
    return jnp.stack(rows).reshape(nz * o, 9 * width)


def table_kernel(angles, u_ref, u8_ref, t_ref, t8_ref):
    j = lax.broadcasted_iota(jnp.int32, (BINS, TX * NY), 0).astype(F32)

    def one(a, _):
        row = u_ref[pl.ds(a, 1), :]
        t_ref[pl.ds(pl.multiple_of(a * BINS, BINS), BINS), :] = jnp.maximum(0.0, 1.0 - jnp.abs(row - j)).astype(BF)
        return 0

    lax.fori_loop(0, angles, one, 0)
    for a in range(8):
        t8_ref[a * BINS : (a + 1) * BINS, :] = jnp.maximum(0.0, 1.0 - jnp.abs(u8_ref[a : a + 1, :] - j)).astype(BF)


def positions(angle_ids, angle_total):
    angle_value = angle_ids.astype(F32) * (math.pi / angle_total)
    pixels = jnp.arange(TX * NY, dtype=jnp.int32)
    centre_x = (pixels // NY).astype(F32) - (TX - 1) / 2.0
    centre_y = (pixels % NY).astype(F32) - (NY - 1) / 2.0
    return (
        centre_x[None, :] * jnp.cos(angle_value)[:, None]
        + centre_y[None, :] * jnp.sin(angle_value)[:, None]
        + BINS / 2.0
    )


def primal_kernel(nx, scal_ref, x_ref, w1_ref, w2_ref, w3_ref, own_ref, lead_ref, col1, col2):
    lanes = x_ref.shape[1]
    lane = lax.broadcasted_iota(jnp.int32, (1, lanes), 1)
    y = lane & (NY - 1)
    gx = (lane >> 5) - HALO + scal_ref[0] * TX
    inside = (gx >= 0) & (gx < nx)

    def fill(col, value):
        rows = value.shape[0]
        for dx in range(3):
            for dy in range(3):
                shift = NY * (dx - 1) + dy - 1
                moved = value if shift == 0 else pltpu.roll(value, (-shift) % lanes, 1)
                if dy == 0:
                    moved = jnp.where(y == 0, 0.0, moved)
                elif dy == 2:
                    moved = jnp.where(y == NY - 1, 0.0, moved)
                at = (dx * 3 + dy) * rows
                col[at : at + rows, :] = moved.astype(BF)

    x = x_ref[...].astype(F32)
    fill(col1, x)
    h = jnp.dot(w1_ref[...], col1[...], preferred_element_type=F32)
    h = jnp.where(inside, jnp.maximum(h, 0.0), 0.0)
    fill(col2, h)
    h = jnp.dot(w2_ref[...], col2[...], preferred_element_type=F32)
    h = jnp.where(inside, jnp.maximum(h, 0.0), 0.0).astype(BF)
    parts = jnp.dot(w3_ref[...], h, preferred_element_type=F32)
    rows = x.shape[0]
    total = x
    for dy in range(3):
        acc = jnp.zeros((rows, lanes), F32)
        for dx in range(3):
            at = (dx * 3 + dy) * rows
            part = parts[at : at + rows, :]
            if dx != 1:
                part = pltpu.roll(part, (-NY * (dx - 1)) % lanes, 1)
            acc = acc + part
        if dy == 0:
            acc = jnp.where(y == 0, 0.0, pltpu.roll(acc, 1, 1))
        elif dy == 2:
            acc = jnp.where(y == NY - 1, 0.0, pltpu.roll(acc, lanes - 1, 1))
        total = total + acc
    total = pltpu.roll(total, lanes - HALO * NY, 1)[:, : TX * NY]
    per = rows // 4
    lead_ref[...] = jnp.concatenate([total[i * per : i * per + 2] for i in range(4)], axis=0).astype(BF)
    own = jnp.zeros((per, TX * NY), F32)
    for i in range(4):
        own = jnp.where(scal_ref[1] == i, total[i * per : (i + 1) * per], own)
    own_ref[...] = own[: own_ref.shape[0]].astype(BF)


def dual_kernel(
    tiles, angles, scal_ref, off_ref, gv_ref, t8_ref, xk_ref, w1_ref, w2_ref, w3_ref, ds_ref,
    out_ref, piece_ref, win, pj, x1, h1, h2, parts, nd, pc,
):
    nb = x1.shape[2]
    blocks = nb // 128
    lane = lax.broadcasted_iota(jnp.int32, (8, 128), 1)
    big = lax.broadcasted_iota(jnp.int32, (1, nb), 1)
    first_angle = scal_ref[0] * 2 - HALO

    def before(v):
        return jnp.where(big == 0, 0.0, pltpu.roll(v, 1, 1))

    def after(v):
        return jnp.where(big == nb - 1, 0.0, pltpu.roll(v, nb - 1, 1))

    windows = lax.dot_general(
        gv_ref[...], t8_ref[...], (((1,), (1,)), ((), ())), preferred_element_type=F32
    )
    win[...] = windows.astype(BF).astype(F32)
    pj[...] = jnp.zeros(pj.shape, F32)

    def place(t, _):
        for a in range(8):
            off = off_ref[t, a]
            q = off >> 7
            r = off & 127
            v = win[pl.ds(pl.multiple_of(t * 8, 8), 8), (a // 2) * 128 : (a // 2) * 128 + 128]
            moved = pltpu.roll(v, (r + 64 * (a % 2)) & 127, 1)
            lo = jnp.where((lane >= r) & (lane < r + 64), moved, 0.0)
            hi = jnp.where(lane < r - 64, moved, 0.0)
            pj[a, q] += lo
            pj[a, q + 1] += hi
        return 0

    lax.fori_loop(0, tiles, place, 0)

    for a in range(8):
        valid = ((first_angle + a) >= 0) & ((first_angle + a) < angles)
        known = xk_ref[a].astype(F32)
        proj = jnp.concatenate([pj[a, b] for b in range(blocks)], axis=1) * (1.0 / math.sqrt(NY))
        proj = jnp.where(valid, proj, 0.0).astype(BF).astype(F32)
        x1[a] = jnp.concatenate(
            [before(known), known, after(known), before(proj), proj, after(proj), jnp.zeros((8, nb), F32)], axis=0
        ).astype(BF)

    k1 = x1.shape[1]
    for a in range(6):
        valid = ((first_angle + a + 1) >= 0) & ((first_angle + a + 1) < angles)
        h = jnp.dot(w1_ref[...], x1[a : a + 3].reshape(3 * k1, nb), preferred_element_type=F32)
        h = jnp.where(valid, jnp.maximum(h, 0.0), 0.0)
        rows = h.shape[0]
        h1[a, 0:rows] = before(h).astype(BF)
        h1[a, rows : 2 * rows] = h.astype(BF)
        h1[a, 2 * rows : 3 * rows] = after(h).astype(BF)

    k2 = h1.shape[1]
    for a in range(4):
        valid = ((first_angle + a + 2) >= 0) & ((first_angle + a + 2) < angles)
        h = jnp.dot(w2_ref[...], h1[a : a + 3].reshape(3 * k2, nb), preferred_element_type=F32)
        h2[a] = jnp.where(valid, jnp.maximum(h, 0.0), 0.0).astype(BF)
        parts[a] = jnp.dot(w3_ref[...], h2[a], preferred_element_type=F32)

    nd[...] = jnp.zeros(nd.shape, F32)
    for a in range(2):
        acc = []
        for db in range(3):
            acc.append(sum(parts[a + da, (da * 3 + db) * 16 : (da * 3 + db) * 16 + 16] for da in range(3)))
        result = before(acc[0]) + acc[1] + after(acc[2])
        result = (ds_ref[a].astype(F32) + result[:10]).astype(BF)
        out_ref[a] = result
        lead = result.astype(F32)[:2]
        lead = jnp.concatenate([lead] * 4, axis=0)
        for b in range(blocks):
            nd[a, b] = lead[:, b * 128 : (b + 1) * 128]

    sub = lax.broadcasted_iota(jnp.int32, (8, 128), 0) >> 1

    def cut(g, _):
        full = jnp.zeros((8, 128), F32)
        for i in range(4):
            got = []
            for a in range(2):
                off = off_ref[g * 4 + i, HALO + a]
                q = off >> 7
                r = off & 127
                v = jnp.where(lane >= r, nd[a, q], nd[a, q + 1])
                got.append(pltpu.roll(v, (64 * a + 128 - r) & 127, 1))
            full = jnp.where(sub == i, jnp.where(lane < 64, got[0], got[1]), full)
        pc[pl.ds(pl.multiple_of(g * 8, 8), 8), :] = full
        return 0

    lax.fori_loop(0, tiles // 4, cut, 0)
    piece_ref[...] = pc[...].astype(BF)


def back_kernel(scale, r_ref, t_ref, out_ref):
    r = r_ref[...].astype(F32)
    count = r.shape[0] // 2
    left = jnp.concatenate([r[2 * i : 2 * i + 2] for i in range(count)], axis=1).astype(BF)
    out_ref[...] = jnp.dot(left, t_ref[...], preferred_element_type=F32) * scale


def call(kernel, outs, scratch, args, smem):
    vm = pl.BlockSpec(memory_space=pltpu.VMEM)
    sm = pl.BlockSpec(memory_space=pltpu.SMEM)
    return pl.pallas_call(
        kernel,
        out_shape=outs,
        in_specs=[sm] * smem + [vm] * (len(args) - smem),
        out_specs=[vm] * len(outs),
        scratch_shapes=scratch,
        compiler_params=pltpu.CompilerParams(vmem_limit_bytes=VMEM_BYTES),
    )(*args)


def body(
    volume, back_proj, dual_state, sinogram, offsets,
    primal_first, primal_second, primal_third, dual_first, dual_second, dual_third,
):
    wide_count = lax.axis_size("wide")
    slab_count = lax.axis_size("slab")
    w = lax.axis_index("wide")
    s = lax.axis_index("slab")
    mem, zl, pix = volume.shape
    nz = zl * slab_count
    own_angles, nb = dual_state.shape[2], dual_state.shape[3]
    angles = own_angles * wide_count
    hid = primal_first.shape[4]
    scal = jnp.stack([w, s]).astype(jnp.int32)

    edge = HALO * NY
    xp = jnp.concatenate([volume, back_proj.astype(BF)[None]], axis=0).reshape((mem + 1) * zl, pix)
    from_low = shifted("wide", 1, xp[:, pix - edge :])
    from_high = shifted("wide", -1, xp[:, :edge])
    xp = jnp.concatenate([from_low, xp, from_high, jnp.zeros((xp.shape[0], 64), BF)], axis=1)
    xg = lax.all_gather(xp, "slab").reshape(-1, xp.shape[1])

    xd = jnp.concatenate([dual_state, sinogram[None]], axis=0).transpose(2, 0, 1, 3)
    xd = xd.reshape(own_angles, (mem + 1) * zl, nb)
    xd, xp = lax.optimization_barrier((xd, xp))
    xd = jnp.concatenate(
        [
            shifted("wide", 2, xd[1:]),
            shifted("wide", 1, xd),
            xd,
            shifted("wide", -1, xd),
            shifted("wide", -2, xd[:1]),
        ],
        axis=0,
    )
    xk = lax.all_gather(xd, "slab").transpose(1, 0, 2, 3).reshape(8, nz * (mem + 1), nb)

    all_z = jnp.arange(nz, dtype=jnp.int32)
    e = band(all_z, nz)
    e_slab = band(s * zl + jnp.arange(zl, dtype=jnp.int32), nz)

    def first_known(wt):
        t = jnp.einsum("yzd,dabco->yoabzc", e, wt)
        t = t.reshape(nz, hid, 3, 3, slab_count, zl, wt.shape[3]).transpose(0, 1, 2, 3, 4, 6, 5)
        return t.reshape(nz * hid, 3, 3 * nz * wt.shape[3])

    pw1 = first_known(primal_first).reshape(nz * hid, -1)
    pw2 = hidden_weights(primal_second, nz)
    third = jnp.pad(primal_third, ((0, 0),) * 4 + ((0, 1),))
    pw3 = jnp.einsum("yzd,dabco->abyozc", e, third)
    pw3 = pw3.reshape(9, slab_count, zl, mem + 1, nz * hid).transpose(0, 1, 3, 2, 4)
    pw3 = pw3.reshape(9 * nz * (mem + 1), nz * hid)

    state_sino = jnp.concatenate([dual_first[:, :, :, :mem], dual_first[:, :, :, mem + 1 :]], axis=3)
    dw1a = first_known(state_sino)
    dw1b = jnp.einsum("yzd,dabo->yoabz", e, dual_first[:, :, :, mem]).reshape(nz * hid, 3, 3 * nz)
    dw1 = jnp.concatenate([dw1a, dw1b, jnp.zeros((nz * hid, 3, 8), BF)], axis=2).reshape(nz * hid, -1)
    dw2 = hidden_weights(dual_second, nz)
    dw3 = jnp.einsum("yzd,dabco->aboyzc", e_slab, dual_third).reshape(9, mem * zl, nz * hid)
    dw3 = jnp.pad(dw3, ((0, 0), (0, 16 - mem * zl), (0, 0))).reshape(9 * 16, nz * hid)

    near_ids = w * own_angles - HALO + jnp.arange(8, dtype=jnp.int32)
    u = positions(jnp.arange(angles, dtype=jnp.int32), angles)
    u8 = positions(near_ids, angles)
    table, table8 = call(
        lambda *refs: table_kernel(angles, *refs),
        [jax.ShapeDtypeStruct((angles * BINS, pix), BF), jax.ShapeDtypeStruct((8 * BINS, pix), BF)],
        [], (u, u8), 0,
    )
    off8 = jnp.take(offsets, jnp.clip(near_ids, 0, angles - 1), axis=1)

    own, lead = call(
        lambda *refs: primal_kernel(wide_count * TX, *refs),
        [jax.ShapeDtypeStruct((mem * zl, pix), BF), jax.ShapeDtypeStruct((nz, pix), BF)],
        [
            pltpu.VMEM((9 * xg.shape[0], xg.shape[1]), BF),
            pltpu.VMEM((9 * nz * hid, xg.shape[1]), BF),
        ],
        (scal, xg, pw1, pw2, pw3), 1,
    )

    sent = jnp.broadcast_to(lead[None], (wide_count, nz, pix))
    gv = lax.all_to_all(sent, "wide", split_axis=0, concat_axis=0, tiled=True)

    k1 = dw1.shape[1] // 3
    blocks = nb // 128
    ds = dual_state.transpose(2, 0, 1, 3).reshape(own_angles, mem * zl, nb)
    nd, pieces = call(
        lambda *refs: dual_kernel(wide_count, angles, *refs),
        [
            jax.ShapeDtypeStruct((own_angles, mem * zl, nb), BF),
            jax.ShapeDtypeStruct((wide_count * zl, 128), BF),
        ],
        [
            pltpu.VMEM((wide_count * nz, 8 * BINS), F32),
            pltpu.VMEM((8, blocks + 1, 8, 128), F32),
            pltpu.VMEM((8, k1, nb), BF),
            pltpu.VMEM((6, 3 * nz * hid, nb), BF),
            pltpu.VMEM((4, nz * hid, nb), BF),
            pltpu.VMEM((4, 9 * 16, nb), F32),
            pltpu.VMEM((own_angles, blocks + 1, 8, 128), F32),
            pltpu.VMEM((wide_count * zl, 128), F32),
        ],
        (scal, off8, gv.reshape(wide_count * nz, pix), table8, xk, dw1, dw2, dw3, ds), 2,
    )
    arrived = lax.all_to_all(
        pieces.reshape(wide_count, zl, 128), "wide", split_axis=0, concat_axis=0, tiled=True
    )
    (new_back,) = call(
        lambda *refs: back_kernel(1.0 / math.sqrt(angles), *refs),
        [jax.ShapeDtypeStruct((zl, pix), F32)],
        [], (arrived.reshape(wide_count * zl, 128), table), 0,
    )
    new_dual = nd.reshape(own_angles, mem, zl, nb).transpose(1, 2, 0, 3)
    return (own.reshape(mem, zl, pix), new_dual, new_back)


def solution(mesh):
    in_specs = (
        P(None, "slab", "wide"),
        P("slab", "wide"),
        P(None, "slab", "wide", None),
        P("slab", "wide", None),
    ) + (P(),) * 7
    out_specs = (P(None, "slab", "wide"), P(None, "slab", "wide", None), P("slab", "wide"))
    return jax.shard_map(body, mesh=mesh, in_specs=in_specs, out_specs=out_specs, check_vma=False)
```

time: 921 us -> 147 us (0.16); the launches traced: 905 us -> 145 us
  waiting for transfers between devices: 686 us -> 7.03 us
  starting transfers between devices: 129 us -> 45.1 us
  matrix products: 59.7 us -> 2.46 us
  Pallas kernels: 0 us -> 33.2 us
  blocking collectives: 0 us -> 27.4 us
  local copies, waits for them, and re-layouts: 5.29 us -> 25.7 us
  between operations: 16.2 us -> 1.23 us
    unnamed x2 -> x0, waiting for transfers between devices: 645 us -> none
    ppermute x24 -> x6, starting transfers between devices: 116 us -> 27.6 us  [shifted(): lax.ppermute(value, axis, [(i, i + delta) for i in range(size) if 0 <= i...]
    dot_general x196 -> x5, matrix products: 59.7 us -> 2.46 us  [the longest x1 0.93 us: body(): jnp.einsum('yzd,dabco->aboyzc', e_slab, dual_third)]
    pallas_call x0 -> x4, Pallas kernels: none -> 33.2 us  [call(): pl.pallas_call(kernel, out_shape=outs, in_specs=[sm] * smem + [vm] * (len...]
    ppermute x24 -> x6, waiting for transfers between devices: 32.3 us -> 0.02 us  [shifted(): lax.ppermute(value, axis, [(i, i + delta) for i in range(size) if 0 <= i...]
    all_gather x0 -> x2, blocking collectives: none -> 27.4 us  [the longest x1 16.8 us: body(): lax.all_gather(xd, 'slab').transpose(1, 0, 2, 3)]
  transfers between devices with their start and end apart: 26 -> 8, of which waited for: 16 -> 1; matrix products, arithmetic and copies ran while one was open for 0% -> 19% of each run, Pallas kernels for 0% -> 4%
where the time goes in v1:
time: 147 us; the launch traced here: 145 us
  starting transfers between devices  45.1 us (31%)
  Pallas kernels  33.2 us (23%)
  blocking collectives  27.4 us (19%)
  local copies, waits for them, and re-layouts  25.7 us (17%)
  waiting for transfers between devices  7.03 us (5%)
  other arithmetic  2.97 us (2%)
  matrix products  2.46 us (2%)
    pallas_call x4, Pallas kernels, call(): pl.pallas_call(kernel, out_shape=outs, in_specs=[sm] * smem + [vm] * (len...  33.2 us
    ppermute x6, starting transfers between devices, shifted(): lax.ppermute(value, axis, [(i, i + delta) for i in range(size) if 0 <= i...  27.6 us
    all_gather x1, blocking collectives, body(): lax.all_gather(xd, 'slab').transpose(1, 0, 2, 3)  16.8 us
    all_to_all x1, starting transfers between devices, body(): lax.all_to_all(pieces.reshape(wide_count, zl, 128), 'wide', split_axis=0,...  11.6 us
    all_gather x1, blocking collectives, body(): xg = lax.all_gather(xp, 'slab').reshape(-1, xp.shape[1])  10.6 us
    unnamed x43, local copies, waits for them, and re-layouts  10.1 us
    all_to_all x1, waiting for transfers between devices, body(): lax.all_to_all(pieces.reshape(wide_count, zl, 128), 'wide', split_axis=0,...  7.01 us
    all_to_all x1, starting transfers between devices, body(): gv = lax.all_to_all(sent, 'wide', split_axis=0, concat_axis=0, tiled=True)  5.84 us
  transfers between devices with their start and end apart: 8, of which 1 were waited for; matrix products, arithmetic and copies ran while one was open for 19% of the time, Pallas kernels for 4%

profile of v1, /device:TPU:2, one launch (start us, length us, event | category | flops | bytes accessed | tf_op | source)
XLA Modules:
  0.0 145.0 jit_solution(9812060830872049419)
XLA Ops:
  2.2 3.5 %collective-permute-start = (bf16[12,96]{1,0:T(8,128)(2,1)S(1)}, bf16[12,96]{1,0:T(8,128)(2,1)S(1)}, u32[]{:S(2)}, u32[]{:S(2)}) collective-permute-start(bf16[12,96]{1,0:T(8,128)(2,1)S(1)} %get-tuple-element.21), channel_id=1, source_target_pairs={{0,4},{4,8},{8,12},{12,16},{16,20},{20,24},{24,28},{28,32},{32,36}... | collective-permute-start | bytes 6920 | tf_op jit(solution)/shard_map/ppermute | solution.py:21
  5.7 7.4 %collective-permute-start.1 = (bf16[12,96]{1,0:T(8,128)(2,1)S(1)}, bf16[12,96]{1,0:T(8,128)(2,1)S(1)}, u32[]{:S(2)}, u32[]{:S(2)}) collective-permute-start(bf16[12,96]{1,0:T(8,128)(2,1)S(1)} %get-tuple-element.22), channel_id=1, source_target_pairs={{4,0},{8,4},{12,8},{16,12},{20,16},{24,20},{28,24},{32,28},{36,32}... | collective-permute-start | bytes 6920 | tf_op jit(solution)/shard_map/ppermute | solution.py:21
  13.3 0.9 fusion.74
  15.1 0.8 copy.108
  15.9 0.8 copy.86
  20.6 0.9 fusion.1
  27.4 0.9 convolution_bitcast_fusion.1
  31.4 2.1 %copy.82 = bf16[8,32,9,256]{3,2,1,0:T(8,128)(2,1)S(1)} copy(bf16[8,32,9,256]{3,1,2,0:T(8,128)(2,1)} %fusion.15) | data formatting | bytes 2359296 | tf_op jit(solution)/shard_map/stack | solution.py:36
  34.2 10.6 %all-gather.2 = bf16[4,12,768]{2,1,0:T(8,128)(2,1)S(1)} all-gather(bf16[1,12,768]{2,1,0:T(8,128)(2,1)S(1)} %fusion.77), channel_id=2, replica_groups=mesh['wide'=64,'slab'=4] {'slab'}, dimensions={0}, use_global_device_ids=true | all-gather | bytes 92160 | tf_op jit(solution)/shard_map/all_gather | solution.py:252
  44.8 3.1 %shard_map.130 = (bf16[10,512]{1,0:T(8,128)(2,1)S(1)}, bf16[8,512]{1,0:T(8,128)(2,1)S(1)}) custom-call(s32[2]{0:T(128)S(1)} %pad_add_fusion.refs_0_, bf16[48,768]{1,0:T(8,128)(2,1)S(1)} %reshape.225.refs_1_, bf16[256,432]{1,0:T(8,128)(2,1)S(1)} %copy.85.refs_2_, bf16[256,2304]{1,0:T(8,128)(2,1)S(1)} %bitcast.185, bf16[432,256]{1,0:T(8,128)(2,1)S(1)} %reshape.196.refs_4_), custom_call_target="tpu_custom_call" | custom-call | tf_op jit(solution)/shard_map/pallas_call | solution.py:222
  47.9 0.9 broadcast_in_dim.24
  48.8 5.8 %all-to-all-start = ((bf16[64,8,512]{2,1,0:T(8,128)(2,1)}), bf16[64,8,512]{2,1,0:T(8,128)(2,1)S(1)}, u32[]{:S(2)}, u32[]{:S(2)}) async-start(bf16[64,8,512]{2,1,0:T(8,128)(2,1)} %broadcast_in_dim.24), calls=%async_computation | async-start | bytes 1048576 | tf_op jit(solution)/shard_map/all_to_all | solution.py:314
  54.9 7.3 %collective-permute-start.4 = (bf16[2,12,1024]{2,0,1:T(2,128)(2,1)S(1)}, bf16[2,12,1024]{2,0,1:T(2,128)(2,1)}, u32[]{:S(2)}, u32[]{:S(2)}) collective-permute-start(bf16[2,12,1024]{2,0,1:T(2,128)(2,1)S(1)} %bitcast.200), channel_id=1, source_target_pairs={{4,0},{8,4},{12,8},{16,12},{20,16},{24,20},{28,24},{32,28},{36,32}... | collective-permute-start | bytes 147464 | tf_op jit(solution)/shard_map/ppermute | solution.py:21
  62.2 1.9 %collective-permute-start.3 = (bf16[2,12,1024]{2,0,1:T(2,128)(2,1)S(1)}, bf16[2,12,1024]{2,0,1:T(2,128)(2,1)}, u32[]{:S(2)}, u32[]{:S(2)}) collective-permute-start(bf16[2,12,1024]{2,0,1:T(2,128)(2,1)S(1)} %bitcast.201), channel_id=1, source_target_pairs={{0,4},{4,8},{8,12},{12,16},{16,20},{20,24},{24,28},{28,32},{32,36}... | collective-permute-start | bytes 147464 | tf_op jit(solution)/shard_map/ppermute | solution.py:21
  64.8 4.2 %collective-permute-start.5 = (bf16[1,12,1024]{2,0,1:T(2,128)(2,1)}, bf16[1,12,1024]{2,0,1:T(2,128)(2,1)}, u32[]{:S(2)}, u32[]{:S(2)}) collective-permute-start(bf16[1,12,1024]{2,0,1:T(2,128)(2,1)} %get-tuple-element.19), channel_id=1, source_target_pairs={{8,0},{12,4},{16,8},{20,12},{24,16},{28,20},{32,24},{36,28},{40,32... | collective-permute-start | bytes 73736 | tf_op jit(solution)/shard_map/ppermute | solution.py:21
  69.0 3.3 %collective-permute-start.2 = (bf16[1,12,1024]{2,0,1:T(2,128)(2,1)}, bf16[1,12,1024]{2,0,1:T(2,128)(2,1)}, u32[]{:S(2)}, u32[]{:S(2)}) collective-permute-start(bf16[1,12,1024]{2,0,1:T(2,128)(2,1)} %get-tuple-element.20), channel_id=1, source_target_pairs={{0,8},{4,12},{8,16},{12,20},{16,24},{20,28},{24,32},{28,36},{32,40... | collective-permute-start | bytes 73736 | tf_op jit(solution)/shard_map/ppermute | solution.py:21
  74.3 6.5 %shard_map.131 = (bf16[8192,512]{1,0:T(8,128)(2,1)}, bf16[512,512]{1,0:T(8,128)(2,1)S(1)}) custom-call(f32[128,512]{1,0:T(8,128)S(1)} %add_add_fusion.refs_0_, f32[8,512]{1,0:T(8,128)S(1)} %add_add_fusion.1.refs_1_), custom_call_target="tpu_custom_call" | custom-call | tf_op jit(solution)/shard_map/pallas_call | solution.py:222
  80.9 1.8 %concatenate.21 = bf16[8,12,1024]{2,0,1:T(8,128)(2,1)} concatenate(bf16[1,12,1024]{2,0,1:T(2,128)(2,1)} %collective-permute-done.2, bf16[2,12,1024]{2,0,1:T(2,128)(2,1)} %collective-permute-done.3, bf16[2,12,1024]{2,0,1:T(2,128)(2,1)S(1)} %bitcast.203, bf16[2,12,1024]{2,0,1:T(2,128)(2,1)} %collective-permute-done.4, bf16[1,12,1024]{2,0,1:T(2,128)(2,1)} %collective-permute-done.5), dimensions={0} | concatenate | bytes 393216 | tf_op jit(solution)/shard_map/concatenate | solution.py:257
  82.7 16.8 %all-gather.1 = bf16[32,12,1024]{2,0,1:T(8,128)(2,1)S(1)} all-gather(bf16[8,12,1024]{2,0,1:T(8,128)(2,1)} %concatenate.21), channel_id=3, replica_groups=mesh['wide'=64,'slab'=4] {'slab'}, dimensions={0}, use_global_device_ids=true | all-gather | bytes 983040 | tf_op jit(solution)/shard_map/all_gather | solution.py:267
  100.0 18.5 %shard_map.132 = (bf16[2,10,1024]{2,1,0:T(8,128)(2,1)S(1)}, bf16[128,128]{1,0:T(8,128)(2,1)}) custom-call(s32[2]{0:T(128)S(1)} %pad_add_fusion.refs_0_, s32[64,8]{1,0:T(8,128)S(1)} %bitcast.188, bf16[512,512]{1,0:T(8,128)(2,1)S(1)} %bitcast.186, bf16[512,512]{1,0:T(8,128)(2,1)S(1)} %get-tuple-element.12.refs_3_, bf16[8,48,1024]{2,1,0:T(8,128)(2,1)S(1)} %copy.98.refs_4_, ...), custom_call_target="tpu_custom_call" | custom-call | tf_op jit(solution)/shard_map/pallas_call | solution.py:222
  119.1 11.6 %all-to-all-start.1 = ((bf16[64,2,128]{2,1,0:T(2,128)(2,1)}), bf16[64,2,128]{2,1,0:T(2,128)(2,1)S(1)}, u32[]{:S(2)}, u32[]{:S(2)}) async-start(bf16[64,2,128]{2,1,0:T(2,128)(2,1)} %bitcast.63), calls=%async_computation.1 | async-start | bytes 65536 | tf_op jit(solution)/shard_map/all_to_all | solution.py:337
  131.4 1.5 %copy.101 = bf16[2,10,1024]{2,0,1:T(2,128)(2,1)} copy(bf16[2,10,1024]{2,1,0:T(8,128)(2,1)} %copy-done) | data formatting | bytes 81920 | tf_op jit(solution)/shard_map/pallas_call | solution.py:222
  132.9 7.0 %all-to-all-done.1 = bf16[64,2,128]{2,1,0:T(2,128)(2,1)S(1)} async-done(((bf16[64,2,128]{2,1,0:T(2,128)(2,1)}), bf16[64,2,128]{2,1,0:T(2,128)(2,1)S(1)}, u32[]{:S(2)}, u32[]{:S(2)}) %all-to-all-start.1) | async-done | bytes 32800 | tf_op jit(solution)/shard_map/all_to_all | solution.py:337
  139.9 5.2 %shard_map.133 = f32[2,512]{1,0:T(2,128)} custom-call(bf16[128,128]{1,0:T(8,128)(2,1)S(1)} %bitcast.189, bf16[8192,512]{1,0:T(8,128)(2,1)} %get-tuple-element.16.refs_1_), custom_call_target="tpu_custom_call" | custom-call | tf_op jit(solution)/shard_map/pallas_call | solution.py:222
  (103 shorter events, 20.4 us)
Async XLA Ops:
  0.6 16.6 %copy-start.5 = (bf16[3,3,3,32,32]{4,3,2,1,0:T(8,128)(2,1)S(1)}, bf16[3,3,3,32,32]{4,3,2,1,0:T(8,128)(2,1)}, u32[]{:S(2)}) copy-start(bf16[3,3,3,32,32]{4,3,2,1,0:T(8,128)(2,1)} %param.17) | copy-start | bytes 165892
  0.6 17.0 %copy-start.6 = (bf16[3,3,3,32,32]{4,3,2,1,0:T(8,128)(2,1)S(1)}, bf16[3,3,3,32,32]{4,3,2,1,0:T(8,128)(2,1)}, u32[]{:S(2)}) copy-start(bf16[3,3,3,32,32]{4,3,2,1,0:T(8,128)(2,1)} %param.20) | copy-start | bytes 165892
  2.2 31.9 %collective-permute-start = (bf16[12,96]{1,0:T(8,128)(2,1)S(1)}, bf16[12,96]{1,0:T(8,128)(2,1)S(1)}, u32[]{:S(2)}, u32[]{:S(2)}) collective-permute-start(bf16[12,96]{1,0:T(8,128)(2,1)S(1)} %get-tuple-element.21), channel_id=1, source_target_pairs={{0,4},{4,8},{8,12},{12,16},{16,20},{20,24},{24,28},{28,32},{32,36}... | collective-permute-start | bytes 6920 | tf_op jit(solution)/shard_map/ppermute | solution.py:21
  5.7 28.4 %collective-permute-start.1 = (bf16[12,96]{1,0:T(8,128)(2,1)S(1)}, bf16[12,96]{1,0:T(8,128)(2,1)S(1)}, u32[]{:S(2)}, u32[]{:S(2)}) collective-permute-start(bf16[12,96]{1,0:T(8,128)(2,1)S(1)} %get-tuple-element.22), channel_id=1, source_target_pairs={{4,0},{8,4},{12,8},{16,12},{20,16},{24,20},{28,24},{32,28},{36,32}... | collective-permute-start | bytes 6920 | tf_op jit(solution)/shard_map/ppermute | solution.py:21
  18.6 1.0 copy-start.8
  20.6 6.8 %copy-start.9 = (bf16[3,3,3,32,5]{3,2,4,1,0:T(4,128)(2,1)S(1)}, bf16[3,3,3,32,5]{3,2,4,1,0:T(4,128)(2,1)}, u32[]{:S(2)}) copy-start(bf16[3,3,3,32,5]{3,2,4,1,0:T(4,128)(2,1)} %param.21) | copy-start | bytes 25924
  20.6 6.0 %copy-start.1 = (bf16[8,32,9,256]{3,1,2,0:T(8,128)(2,1)}, bf16[8,32,9,256]{3,1,2,0:T(8,128)(2,1)S(1)}, u32[]{:S(2)}) copy-start(bf16[8,32,9,256]{3,1,2,0:T(8,128)(2,1)S(1)} %fusion.27) | copy-start | bytes 3538948
  47.9 6.8 %copy-start.7 = (bf16[5,2,2,1024]{3,2,1,0:T(2,128)(2,1)S(1)}, bf16[5,2,2,1024]{3,2,1,0:T(2,128)(2,1)}, u32[]{:S(2)}) copy-start(bf16[5,2,2,1024]{3,2,1,0:T(2,128)(2,1)} %param.13) | copy-start | bytes 122884
  47.9 6.8 %copy-start.10 = (bf16[2,2,1024]{2,1,0:T(2,128)(2,1)S(1)}, bf16[2,2,1024]{2,1,0:T(2,128)(2,1)}, u32[]{:S(2)}) copy-start(bf16[2,2,1024]{2,1,0:T(2,128)(2,1)} %param.14) | copy-start | bytes 24580
  47.9 6.9 %copy-start.2 = (bf16[8,32,9,256]{3,1,2,0:T(8,128)(2,1)S(1)}, bf16[8,32,9,256]{3,1,2,0:T(8,128)(2,1)}, u32[]{:S(2)}) copy-start(bf16[8,32,9,256]{3,1,2,0:T(8,128)(2,1)} %copy-done.1) | copy-start | bytes 3538948
  47.9 24.6 %copy-start.4 = (bf16[3,3,5,2,8,32]{5,4,2,1,0,3:T(8,128)(2,1)S(1)}, bf16[3,3,5,2,8,32]{5,4,2,1,0,3:T(8,128)(2,1)}, u32[]{:S(2)}) copy-start(bf16[3,3,5,2,8,32]{5,4,2,1,0,3:T(8,128)(2,1)} %convolution_bitcast_fusion.1) | copy-start | bytes 138244
  48.8 23.9 %copy-start.3 = (bf16[256,3,176]{0,2,1:T(8,128)(2,1)S(1)}, bf16[256,3,176]{0,2,1:T(8,128)(2,1)}, u32[]{:S(2)}) copy-start(bf16[256,3,176]{0,2,1:T(8,128)(2,1)} %maximum_maximum_fusion) | copy-start | bytes 811012
  48.8 51.2 %all-to-all-start = ((bf16[64,8,512]{2,1,0:T(8,128)(2,1)}), bf16[64,8,512]{2,1,0:T(8,128)(2,1)S(1)}, u32[]{:S(2)}, u32[]{:S(2)}) async-start(bf16[64,8,512]{2,1,0:T(8,128)(2,1)} %broadcast_in_dim.24), calls=%async_computation | async-start | bytes 1048576 | tf_op jit(solution)/shard_map/all_to_all | solution.py:314
  54.9 26.0 %collective-permute-start.4 = (bf16[2,12,1024]{2,0,1:T(2,128)(2,1)S(1)}, bf16[2,12,1024]{2,0,1:T(2,128)(2,1)}, u32[]{:S(2)}, u32[]{:S(2)}) collective-permute-start(bf16[2,12,1024]{2,0,1:T(2,128)(2,1)S(1)} %bitcast.200), channel_id=1, source_target_pairs={{4,0},{8,4},{12,8},{16,12},{20,16},{24,20},{28,24},{32,28},{36,32}... | collective-permute-start | bytes 147464 | tf_op jit(solution)/shard_map/ppermute | solution.py:21
  62.2 18.7 %collective-permute-start.3 = (bf16[2,12,1024]{2,0,1:T(2,128)(2,1)S(1)}, bf16[2,12,1024]{2,0,1:T(2,128)(2,1)}, u32[]{:S(2)}, u32[]{:S(2)}) collective-permute-start(bf16[2,12,1024]{2,0,1:T(2,128)(2,1)S(1)} %bitcast.201), channel_id=1, source_target_pairs={{0,4},{4,8},{8,12},{12,16},{16,20},{20,24},{24,28},{28,32},{32,36}... | collective-permute-start | bytes 147464 | tf_op jit(solution)/shard_map/ppermute | solution.py:21
  64.8 16.1 %collective-permute-start.5 = (bf16[1,12,1024]{2,0,1:T(2,128)(2,1)}, bf16[1,12,1024]{2,0,1:T(2,128)(2,1)}, u32[]{:S(2)}, u32[]{:S(2)}) collective-permute-start(bf16[1,12,1024]{2,0,1:T(2,128)(2,1)} %get-tuple-element.19), channel_id=1, source_target_pairs={{8,0},{12,4},{16,8},{20,12},{24,16},{28,20},{32,24},{36,28},{40,32... | collective-permute-start | bytes 73736 | tf_op jit(solution)/shard_map/ppermute | solution.py:21
  69.0 11.9 %collective-permute-start.2 = (bf16[1,12,1024]{2,0,1:T(2,128)(2,1)}, bf16[1,12,1024]{2,0,1:T(2,128)(2,1)}, u32[]{:S(2)}, u32[]{:S(2)}) collective-permute-start(bf16[1,12,1024]{2,0,1:T(2,128)(2,1)} %get-tuple-element.20), channel_id=1, source_target_pairs={{0,8},{4,12},{8,16},{12,20},{16,24},{20,28},{24,32},{28,36},{32,40... | collective-permute-start | bytes 73736 | tf_op jit(solution)/shard_map/ppermute | solution.py:21
  118.5 0.6 copy-start
  119.1 20.8 %all-to-all-start.1 = ((bf16[64,2,128]{2,1,0:T(2,128)(2,1)}), bf16[64,2,128]{2,1,0:T(2,128)(2,1)S(1)}, u32[]{:S(2)}, u32[]{:S(2)}) async-start(bf16[64,2,128]{2,1,0:T(2,128)(2,1)} %bitcast.63), calls=%async_computation.1 | async-start | bytes 65536 | tf_op jit(solution)/shard_map/all_to_all | solution.py:337

commit v2 on v1

v2 whole, which is shorter than its diff:
```python
import math

import jax
import jax.numpy as jnp
from jax import lax
from jax.experimental import pallas as pl
from jax.experimental.pallas import tpu as pltpu
from jax.sharding import PartitionSpec as P

NY = 32
TX = 16
BINS = NY + 2 * TX
HALO = 3
BF = jnp.bfloat16
F32 = jnp.float32


def shifted(axis, delta, value):
    size = lax.axis_size(axis)
    return lax.ppermute(value, axis, [(i, i + delta) for i in range(size) if 0 <= i + delta < size])


def band(zo, zi):
    d = jnp.arange(3, dtype=jnp.int32)
    return ((zi[None, :, None] - zo[:, None, None] + 1) == d[None, None, :]).astype(BF)


def swapped(value, mask):
    size = lax.axis_size("slab")
    return lax.ppermute(value, "slab", [(i, i ^ mask) for i in range(size)])


def hidden_base(w):
    c, o = w.shape[3], w.shape[4]
    base = w.transpose(1, 2, 4, 0, 3).reshape(9, o, 3 * c)
    return jnp.pad(base, ((0, 0), (0, 0), (0, 128 - 3 * c)))


def weights_kernel(nz, scal_ref, p_ref, d_ref, pout_ref, dout_ref):
    o = p_ref.shape[1]
    width = pout_ref.shape[1] // 9
    c = width // nz
    lane = lax.broadcasted_iota(jnp.int32, (1, width), 1)
    for tap in range(9):
        base = p_ref[tap].astype(F32)
        base = jnp.concatenate([base, jnp.zeros((o, width - base.shape[1]), F32)], axis=1)
        for zo in range(nz):
            moved = pltpu.roll(base, (c * (zo - 1)) % width, 1)
            if zo == 0:
                moved = jnp.where(lane < 2 * c, moved, 0.0)
            elif zo == nz - 1:
                moved = jnp.where(lane >= c * (zo - 1), moved, 0.0)
            pout_ref[zo * o : (zo + 1) * o, tap * width : (tap + 1) * width] = moved.astype(BF)
    count = dout_ref.shape[0] // o
    span = (count + 2) * c
    first = scal_ref[1] * 2 - 1
    for zo in range(count):
        inside = (first + zo >= 0) & (first + zo < nz)
        pieces = []
        for tap in range(9):
            base = d_ref[tap].astype(F32)
            base = jnp.concatenate([base, jnp.zeros((o, width - base.shape[1]), F32)], axis=1)
            pieces.append(pltpu.roll(base, c * zo, 1)[:, :span])
        row = jnp.where(inside, jnp.concatenate(pieces, axis=1), 0.0)
        dout_ref[zo * o : (zo + 1) * o, :] = row.astype(BF)


def table_kernel(u_ref, t_ref):
    j = lax.broadcasted_iota(jnp.int32, (BINS, TX * NY), 0).astype(F32)

    def one(a, _):
        row = u_ref[pl.ds(a, 1), :]
        t_ref[pl.ds(pl.multiple_of(a * BINS, BINS), BINS), :] = jnp.maximum(0.0, 1.0 - jnp.abs(row - j)).astype(BF)
        return 0

    lax.fori_loop(0, u_ref.shape[0], one, 0)


def positions(angle_ids, angle_total):
    angle_value = angle_ids.astype(F32) * (math.pi / angle_total)
    pixels = jnp.arange(TX * NY, dtype=jnp.int32)
    centre_x = (pixels // NY).astype(F32) - (TX - 1) / 2.0
    centre_y = (pixels % NY).astype(F32) - (NY - 1) / 2.0
    return (
        centre_x[None, :] * jnp.cos(angle_value)[:, None]
        + centre_y[None, :] * jnp.sin(angle_value)[:, None]
        + BINS / 2.0
    )


def primal_kernel(nx, scal_ref, x_ref, w1_ref, w2_ref, w3_ref, own_ref, lead_ref, col1, col2):
    lanes = x_ref.shape[1]
    lane = lax.broadcasted_iota(jnp.int32, (1, lanes), 1)
    y = lane & (NY - 1)
    gx = (lane >> 5) - HALO + scal_ref[0] * TX
    inside = (gx >= 0) & (gx < nx)

    def fill(col, value):
        rows = value.shape[0]
        for dx in range(3):
            for dy in range(3):
                shift = NY * (dx - 1) + dy - 1
                moved = value if shift == 0 else pltpu.roll(value, (-shift) % lanes, 1)
                if dy == 0:
                    moved = jnp.where(y == 0, 0.0, moved)
                elif dy == 2:
                    moved = jnp.where(y == NY - 1, 0.0, moved)
                at = (dx * 3 + dy) * rows
                col[at : at + rows, :] = moved.astype(BF)

    x = x_ref[...].astype(F32)
    fill(col1, x)
    h = jnp.dot(w1_ref[...], col1[...], preferred_element_type=F32)
    h = jnp.where(inside, jnp.maximum(h, 0.0), 0.0)
    fill(col2, h)
    h = jnp.dot(w2_ref[...], col2[...], preferred_element_type=F32)
    h = jnp.where(inside, jnp.maximum(h, 0.0), 0.0).astype(BF)
    parts = jnp.dot(w3_ref[...], h, preferred_element_type=F32)
    rows = x.shape[0]
    total = x
    for dy in range(3):
        acc = jnp.zeros((rows, lanes), F32)
        for dx in range(3):
            at = (dx * 3 + dy) * rows
            part = parts[at : at + rows, :]
            if dx != 1:
                part = pltpu.roll(part, (-NY * (dx - 1)) % lanes, 1)
            acc = acc + part
        if dy == 0:
            acc = jnp.where(y == 0, 0.0, pltpu.roll(acc, 1, 1))
        elif dy == 2:
            acc = jnp.where(y == NY - 1, 0.0, pltpu.roll(acc, lanes - 1, 1))
        total = total + acc
    total = pltpu.roll(total, lanes - HALO * NY, 1)[:, : TX * NY]
    per = rows // 4
    lead_ref[...] = jnp.concatenate([total[i * per : i * per + 2] for i in range(4)], axis=0).astype(BF)
    own_ref[...] = total[: own_ref.shape[0]].astype(BF)


def before(v):
    bins = lax.broadcasted_iota(jnp.int32, (1, v.shape[1]), 1)
    return jnp.where(bins == 0, 0.0, pltpu.roll(v, 1, 1))


def after(v):
    bins = lax.broadcasted_iota(jnp.int32, (1, v.shape[1]), 1)
    return jnp.where(bins == v.shape[1] - 1, 0.0, pltpu.roll(v, v.shape[1] - 1, 1))


def known_kernel(x0_ref, x1_ref, w_ref, out_ref, col, part, sems):
    nb = col.shape[2]
    for a in range(8):
        at = slice(a * nb, (a + 1) * nb)
        known = jnp.concatenate([x0_ref[:, at].astype(F32), x1_ref[:, at].astype(F32)], axis=0)
        col[a] = jnp.concatenate([before(known), known, after(known)], axis=0).astype(BF)
    for a in range(6):
        part[a] = jnp.dot(w_ref[...], col[a : a + 3].reshape(-1, nb), preferred_element_type=F32)
        pltpu.make_async_copy(part.at[a], out_ref.at[a], sems.at[a]).start()
    for a in range(6):
        pltpu.make_async_copy(part.at[a], out_ref.at[a], sems.at[a]).wait()


def dual_kernel(tiles, angles, *refs):
    (scal_ref, off_ref, gv_ref, t8_ref, known_ref, w1_ref, w2_ref, w3_ref, ds_ref, out_ref, piece_ref) = refs[:11]
    (win, x1, h1, h2, parts, nd, pc, known, sem) = refs[11:20]
    pj = refs[20:]
    fetch = pltpu.make_async_copy(known_ref, known, sem)
    fetch.start()
    nb = x1.shape[2]
    blocks = nb // 128
    lane = lax.broadcasted_iota(jnp.int32, (8, 128), 1)
    first_angle = scal_ref[0] * 2 - HALO

    windows = lax.dot_general(
        gv_ref[...], t8_ref[...], (((1,), (1,)), ((), ())), preferred_element_type=F32
    )
    win[...] = windows.astype(BF).astype(F32)
    for ref in pj:
        ref[...] = jnp.zeros(ref.shape, F32)

    def place(t, _):
        found = []
        for a in range(8):
            off = off_ref[t, a]
            q = off >> 7
            r = off & 127
            v = win[pl.ds(pl.multiple_of(t * 8, 8), 8), (a // 2) * 128 : (a // 2) * 128 + 128]
            moved = pltpu.roll(v, (r + 64 * (a % 2)) & 127, 1)
            lo = jnp.where((lane >= r) & (lane < r + 64), moved, 0.0)
            hi = jnp.where(lane < r - 64, moved, 0.0)
            found.append((q, pj[a][q] + lo, pj[a][q + 1] + hi))
        for a, (q, lo, hi) in enumerate(found):
            pj[a][q] = lo
            pj[a][q + 1] = hi
        return 0

    lax.fori_loop(0, tiles, place, 0)

    for a in range(8):
        valid = ((first_angle + a) >= 0) & ((first_angle + a) < angles)
        proj = jnp.concatenate([pj[a][b] for b in range(blocks)], axis=1) * (1.0 / math.sqrt(NY))
        proj = jnp.where(valid, proj, 0.0).astype(BF).astype(F32)
        x1[a] = jnp.concatenate([before(proj), proj, after(proj), jnp.zeros((8, nb), F32)], axis=0).astype(BF)

    fetch.wait()
    k1 = x1.shape[1]
    for a in range(6):
        valid = ((first_angle + a + 1) >= 0) & ((first_angle + a + 1) < angles)
        h = jnp.dot(w1_ref[...], x1[a : a + 3].reshape(3 * k1, nb), preferred_element_type=F32)
        h = jnp.where(valid, jnp.maximum(h + known[a], 0.0), 0.0)
        rows = h.shape[0]
        h1[a, 0:rows] = before(h).astype(BF)
        h1[a, rows : 2 * rows] = h.astype(BF)
        h1[a, 2 * rows : 3 * rows] = after(h).astype(BF)

    k2 = h1.shape[1]
    for a in range(4):
        valid = ((first_angle + a + 2) >= 0) & ((first_angle + a + 2) < angles)
        h = jnp.dot(w2_ref[...], h1[a : a + 3].reshape(3 * k2, nb), preferred_element_type=F32)
        h2[a] = jnp.where(valid, jnp.maximum(h, 0.0), 0.0).astype(BF)
        parts[a] = jnp.dot(w3_ref[...], h2[a], preferred_element_type=F32)

    nd[...] = jnp.zeros(nd.shape, F32)
    for a in range(2):
        acc = []
        for db in range(3):
            acc.append(sum(parts[a + da, (da * 3 + db) * 16 : (da * 3 + db) * 16 + 16] for da in range(3)))
        result = before(acc[0]) + acc[1] + after(acc[2])
        result = (ds_ref[a].astype(F32) + result[:10]).astype(BF)
        out_ref[a] = result
        lead = result.astype(F32)[:2]
        lead = jnp.concatenate([lead] * 4, axis=0)
        for b in range(blocks):
            nd[a, b] = lead[:, b * 128 : (b + 1) * 128]

    sub = lax.broadcasted_iota(jnp.int32, (8, 128), 0) >> 1

    def cut(g, _):
        full = jnp.zeros((8, 128), F32)
        for i in range(4):
            got = []
            for a in range(2):
                off = off_ref[g * 4 + i, HALO + a]
                q = off >> 7
                r = off & 127
                v = jnp.where(lane >= r, nd[a, q], nd[a, q + 1])
                got.append(pltpu.roll(v, (64 * a + 128 - r) & 127, 1))
            full = jnp.where(sub == i, jnp.where(lane < 64, got[0], got[1]), full)
        pc[pl.ds(pl.multiple_of(g * 8, 8), 8), :] = full
        return 0

    lax.fori_loop(0, tiles // 4, cut, 0)
    piece_ref[...] = pc[...].astype(BF)


def back_kernel(scale, r_ref, u_ref, out_ref):
    j = lax.broadcasted_iota(jnp.int32, (BINS, TX * NY), 0).astype(F32)
    total = jnp.zeros((8, TX * NY), F32)
    zeros = jnp.zeros((6, 128), F32)
    for i in range(r_ref.shape[0] // 4):
        r = r_ref[4 * i : 4 * i + 4, :].astype(F32)
        left = jnp.concatenate(
            [jnp.concatenate([r[0:2], zeros], axis=0), jnp.concatenate([r[2:4], zeros], axis=0)], axis=1
        ).astype(BF)
        right = jnp.concatenate(
            [jnp.maximum(0.0, 1.0 - jnp.abs(u_ref[4 * i + a : 4 * i + a + 1, :] - j)).astype(BF) for a in range(4)],
            axis=0,
        )
        total = total + jnp.dot(left, right, preferred_element_type=F32)
    out_ref[...] = total[0:2] * scale


def call(kernel, outs, scratch, args, smem, hbm_in=(), hbm_out=False, mib=24):
    vm = pl.BlockSpec(memory_space=pltpu.VMEM)
    sm = pl.BlockSpec(memory_space=pltpu.SMEM)
    hb = pl.BlockSpec(memory_space=pltpu.HBM)
    return pl.pallas_call(
        kernel,
        out_shape=outs,
        in_specs=[sm if i < smem else hb if i in hbm_in else vm for i in range(len(args))],
        out_specs=[hb if hbm_out else vm] * len(outs),
        scratch_shapes=scratch,
        compiler_params=pltpu.CompilerParams(vmem_limit_bytes=mib * 1024 * 1024),
    )(*args)


def body(
    volume, back_proj, dual_state, sinogram, offsets,
    primal_first, primal_second, primal_third, dual_first, dual_second, dual_third,
):
    wide_count = lax.axis_size("wide")
    slab_count = lax.axis_size("slab")
    w = lax.axis_index("wide")
    s = lax.axis_index("slab")
    mem, zl, pix = volume.shape
    nz = zl * slab_count
    own_angles, nb = dual_state.shape[2], dual_state.shape[3]
    angles = own_angles * wide_count
    hid = primal_first.shape[4]
    scal = jnp.stack([w, s]).astype(jnp.int32)

    rows = (mem + 1) * zl
    xp = jnp.concatenate([volume, back_proj.astype(BF)[None]], axis=0).reshape(rows, pix)
    xd = jnp.concatenate([dual_state, sinogram[None]], axis=0).transpose(0, 1, 2, 3)
    xd = xd.reshape(rows, own_angles * nb)
    both = jnp.concatenate([xp, xd], axis=1)
    both = jnp.concatenate([both, swapped(both, 2)], axis=0)
    xp, xd = both[:, :pix], both[:, pix:]
    edge = HALO * NY
    from_low = shifted("wide", 1, xp[:, pix - edge :])
    from_high = shifted("wide", -1, xp[:, :edge])
    xg = jnp.concatenate([from_low, xp, from_high, jnp.zeros((xp.shape[0], 64), BF)], axis=1)
    xg = jnp.concatenate([xg, swapped(xg, 1)], axis=0)

    all_z = jnp.arange(nz, dtype=jnp.int32)
    seen = (s ^ jnp.array([0, 2, 1, 3], jnp.int32))[:, None] * zl + jnp.arange(zl, dtype=jnp.int32)[None]
    seen = seen.reshape(nz)
    e = band(all_z, seen)
    e_out = band(seen, all_z)

    def first_known(wt, e):
        t = jnp.einsum("ypzd,dabco->yoabpcz", e.reshape(-1, slab_count, zl, 3), wt)
        return t.reshape(e.shape[0] * hid, 3, 3 * nz * wt.shape[3])

    pw1 = first_known(primal_first, e).reshape(nz * hid, -1)
    third = jnp.pad(primal_third, ((0, 0),) * 4 + ((0, 1),))
    pw3 = jnp.einsum("pyzd,dabco->abpoyzc", e_out.reshape(slab_count, zl, nz, 3), third)
    pw3 = pw3.reshape(9 * nz * (mem + 1), nz * hid)
    one, two = (zl + 4) * hid, (zl + 2) * hid
    pw2, dw2 = call(
        lambda *refs: weights_kernel(nz, *refs),
        [jax.ShapeDtypeStruct((nz * hid, 9 * nz * hid), BF), jax.ShapeDtypeStruct((two, 9 * one), BF)],
        [], (scal, hidden_base(primal_second), hidden_base(dual_second)), 1,
    )
    own, lead = call(
        lambda *refs: primal_kernel(wide_count * TX, *refs),
        [jax.ShapeDtypeStruct((mem * zl, pix), BF), jax.ShapeDtypeStruct((nz, pix), BF)],
        [
            pltpu.VMEM((9 * xg.shape[0], xg.shape[1]), BF),
            pltpu.VMEM((9 * nz * hid, xg.shape[1]), BF),
        ],
        (scal, xg, pw1, pw2, pw3), 1,
    )

    sent = jnp.broadcast_to(lead[None], (wide_count, nz, pix))
    gv = lax.all_to_all(sent, "wide", split_axis=0, concat_axis=0, tiled=True)

    xd, _ = lax.optimization_barrier((xd, lead))
    xk = jnp.concatenate(
        [
            shifted("wide", 2, xd[:, nb:]),
            shifted("wide", 1, xd),
            xd,
            shifted("wide", -1, xd),
            shifted("wide", -2, xd[:, :nb]),
        ],
        axis=1,
    )
    xk = (xk, swapped(xk, 1))
    z_one = s * zl - 2 + jnp.arange(zl + 4, dtype=jnp.int32)
    z_two = s * zl - 1 + jnp.arange(zl + 2, dtype=jnp.int32)
    z_own = s * zl + jnp.arange(zl, dtype=jnp.int32)
    def inside_z(z):
        return ((z >= 0) & (z < nz)).astype(BF)[:, None, None]

    e_one = band(z_one, seen) * inside_z(z_one)
    state_sino = jnp.concatenate([dual_first[:, :, :, :mem], dual_first[:, :, :, mem + 1 :]], axis=3)
    dw1a = first_known(state_sino, e_one).reshape(one, -1)
    dw1b = jnp.einsum("yzd,dabo->yoabz", e_one, dual_first[:, :, :, mem]).reshape(one, 3, 3 * nz)
    dw1b = jnp.pad(dw1b, ((0, 0), (0, 0), (0, 8))).reshape(one, -1)
    dw3 = jnp.einsum("yzd,dabco->aboyzc", band(z_own, z_two), dual_third).reshape(9, mem * zl, two)
    dw3 = jnp.pad(dw3, ((0, 0), (0, 16 - mem * zl), (0, 0))).reshape(9 * 16, two)
    (known,) = call(
        known_kernel, [jax.ShapeDtypeStruct((6, one, nb), F32)],
        [pltpu.VMEM((8, 3 * nz * (mem + 1), nb), BF), pltpu.VMEM((6, one, nb), F32), pltpu.SemaphoreType.DMA((6,))],
        (*xk, dw1a), 0, hbm_out=True, mib=60,
    )

    near_ids = w * own_angles - HALO + jnp.arange(8, dtype=jnp.int32)
    (table8,) = call(
        table_kernel, [jax.ShapeDtypeStruct((8 * BINS, pix), BF)], [], (positions(near_ids, angles),), 0
    )
    off8 = jnp.take(offsets, jnp.clip(near_ids, 0, angles - 1), axis=1)

    blocks = nb // 128
    ds = dual_state.transpose(2, 0, 1, 3).reshape(own_angles, mem * zl, nb)
    nd, pieces = call(
        lambda *refs: dual_kernel(wide_count, angles, *refs),
        [
            jax.ShapeDtypeStruct((own_angles, mem * zl, nb), BF),
            jax.ShapeDtypeStruct((wide_count * zl, 128), BF),
        ],
        [
            pltpu.VMEM((wide_count * nz, 8 * BINS), F32),
            pltpu.VMEM((8, 4 * 8, nb), BF),
            pltpu.VMEM((6, 3 * one, nb), BF),
            pltpu.VMEM((4, two, nb), BF),
            pltpu.VMEM((4, 9 * 16, nb), F32),
            pltpu.VMEM((own_angles, blocks + 1, 8, 128), F32),
            pltpu.VMEM((wide_count * zl, 128), F32),
            pltpu.VMEM((6, one, nb), F32),
            pltpu.SemaphoreType.DMA,
        ]
        + [pltpu.VMEM((blocks + 1, 8, 128), F32)] * 8,
        (scal, off8, gv.reshape(wide_count * nz, pix), table8, known, dw1b, dw2, dw3, ds), 2, hbm_in=(4,), mib=60,
    )
    arrived = lax.all_to_all(
        pieces.reshape(wide_count, zl, 128), "wide", split_axis=0, concat_axis=0, tiled=True
    )
    (new_back,) = call(
        lambda *refs: back_kernel(1.0 / math.sqrt(angles), *refs), [jax.ShapeDtypeStruct((zl, pix), F32)],
        [], (arrived.reshape(wide_count * zl, 128), positions(jnp.arange(angles, dtype=jnp.int32), angles)), 0,
    )
    new_dual = nd.reshape(own_angles, mem, zl, nb).transpose(1, 2, 0, 3)
    return (own.reshape(mem, zl, pix), new_dual, new_back)


def solution(mesh):
    in_specs = (
        P(None, "slab", "wide"),
        P("slab", "wide"),
        P(None, "slab", "wide", None),
        P("slab", "wide", None),
    ) + (P(),) * 7
    out_specs = (P(None, "slab", "wide"), P(None, "slab", "wide", None), P("slab", "wide"))
    return jax.shard_map(body, mesh=mesh, in_specs=in_specs, out_specs=out_specs, check_vma=False)
```

time: 147 us -> 116 us (0.79)
  blocking collectives: 27.4 us -> 0 us
  waiting for transfers between devices: 7.03 us -> 17.9 us
  local copies, waits for them, and re-layouts: 25.7 us -> 15 us
  Pallas kernels: 33.2 us -> 24.7 us
  starting transfers between devices: 45.1 us -> 50.6 us
    all_gather x2 -> x0, blocking collectives: 27.4 us -> none  [the longest x1 16.8 us: body(): lax.all_gather(xd, 'slab').transpose(1, 0, 2, 3)]
    pallas_call x4 -> x6, Pallas kernels: 33.2 us -> 24.7 us  [call(): pl.pallas_call(kernel, out_shape=outs, in_specs=[sm if i < smem else hb i...]
    all_to_all x1, waiting for transfers between devices: 0.01 us -> 8.29 us  [body(): gv = lax.all_to_all(sent, 'wide', split_axis=0, concat_axis=0, tiled=True)]
    ppermute x0 -> x3, starting transfers between devices: none -> 7.64 us  [swapped(): return lax.ppermute(value, 'slab', [(i, i ^ mask) for i in range(size)])]
    unnamed x43 -> x35, local copies, waits for them, and re-layouts: 10.1 us -> 2.63 us
    all_to_all x1, starting transfers between devices: 11.6 us -> 7.46 us  [body(): lax.all_to_all(pieces.reshape(wide_count, zl, 128), 'wide', split_axis=0,...]
    another operation x6 -> x4, local copies, waits for them, and re-layouts: 4.49 us -> 2.04 us  [the longest x2 1.3 us: body(): dw1a = first_known(state_sino, e_one).reshape(one, -1)]
    transpose x5 -> x7, local copies, waits for them, and re-layouts: 0.52 us -> 2.82 us  [the longest x2 2.27 us: hidden_base(): base = w.transpose(1, 2, 4, 0, 3).reshape(9, o, 3 * c)]
  transfers between devices with their start and end apart: 8 -> 11, of which waited for: 1 -> 5; matrix products, arithmetic and copies ran while one was open for 19% -> 14% of each run, Pallas kernels for 4% -> 4%
where the time goes in v2:
time: 116 us; the launch traced here: 115 us
  starting transfers between devices  50.6 us (44%)
  Pallas kernels  24.7 us (21%)
  waiting for transfers between devices  17.9 us (15%)
  local copies, waits for them, and re-layouts  15 us (13%)
  other arithmetic  4.16 us (4%)
  matrix products  1.79 us (2%)
  between operations  1.28 us (1%)
    ppermute x6, starting transfers between devices, shifted(): lax.ppermute(value, axis, [(i, i + delta) for i in range(size) if 0 <= i...  28.3 us
    pallas_call x6, Pallas kernels, call(): pl.pallas_call(kernel, out_shape=outs, in_specs=[sm if i < smem else hb i...  24.7 us
    all_to_all x1, waiting for transfers between devices, body(): gv = lax.all_to_all(sent, 'wide', split_axis=0, concat_axis=0, tiled=True)  8.29 us
    ppermute x3, starting transfers between devices, swapped(): return lax.ppermute(value, 'slab', [(i, i ^ mask) for i in range(size)])  7.64 us
    all_to_all x1, starting transfers between devices, body(): lax.all_to_all(pieces.reshape(wide_count, zl, 128), 'wide', split_axis=0,...  7.46 us
    all_to_all x1, starting transfers between devices, body(): gv = lax.all_to_all(sent, 'wide', split_axis=0, concat_axis=0, tiled=True)  7.19 us
    all_to_all x1, waiting for transfers between devices, body(): lax.all_to_all(pieces.reshape(wide_count, zl, 128), 'wide', split_axis=0,...  6.9 us
    unnamed x35, local copies, waits for them, and re-layouts  2.63 us
  transfers between devices with their start and end apart: 11, of which 5 were waited for; matrix products, arithmetic and copies ran while one was open for 14% of the time, Pallas kernels for 4%

profile of v2, /device:TPU:2, one launch (start us, length us, event | category | flops | bytes accessed | tf_op | source)
XLA Modules:
  0.0 115.5 jit_solution(8388376241340752653)
XLA Ops:
  0.7 0.9 pad_maximum_fusion.2
  3.1 7.3 %collective-permute-start = (bf16[12,2560]{1,0:T(8,128)(2,1)S(1)}, bf16[12,2560]{1,0:T(8,128)(2,1)S(1)}, u32[]{:S(2)}, u32[]{:S(2)}) collective-permute-start(bf16[12,2560]{1,0:T(8,128)(2,1)S(1)} %constant_dynamic-update-slice_fusion), channel_id=1, source_target_pairs={{0,2},{1,3},{2,0},{3,1},{4,6},{5,7},{6,4},{7,5},{8,10},{9,11},{10,... | collective-permute-start | bytes 184328 | tf_op jit(solution)/shard_map/ppermute | solution.py:30
  11.4 1.1 copy.56
  12.7 1.1 copy.57
  17.4 1.0 shard_map.139
  19.3 3.5 %collective-permute-start.1 = (bf16[24,96]{1,0:T(8,128)(2,1)S(1)}, bf16[24,96]{1,0:T(8,128)(2,1)S(1)}, u32[]{:S(2)}, u32[]{:S(2)}) collective-permute-start(bf16[24,96]{1,0:T(8,128)(2,1)S(1)} %get-tuple-element.17), channel_id=1, source_target_pairs={{0,4},{4,8},{8,12},{12,16},{16,20},{20,24},{24,28},{28,32},{32,36}... | collective-permute-start | bytes 13832 | tf_op jit(solution)/shard_map/ppermute | solution.py:20
  22.8 7.2 %collective-permute-start.2 = (bf16[24,96]{1,0:T(8,128)(2,1)S(1)}, bf16[24,96]{1,0:T(8,128)(2,1)S(1)}, u32[]{:S(2)}, u32[]{:S(2)}) collective-permute-start(bf16[24,96]{1,0:T(8,128)(2,1)S(1)} %get-tuple-element.18), channel_id=1, source_target_pairs={{4,0},{8,4},{12,8},{16,12},{20,16},{24,20},{28,24},{32,28},{36,32}... | collective-permute-start | bytes 13832 | tf_op jit(solution)/shard_map/ppermute | solution.py:20
  30.0 1.3 %collective-permute-done.2 = bf16[24,96]{1,0:T(8,128)(2,1)S(1)} collective-permute-done((bf16[24,96]{1,0:T(8,128)(2,1)S(1)}, bf16[24,96]{1,0:T(8,128)(2,1)S(1)}, u32[]{:S(2)}, u32[]{:S(2)}) %collective-permute-start.2) | collective-permute-done | bytes 4640 | tf_op jit(solution)/shard_map/ppermute | solution.py:20
  31.5 1.2 %collective-permute-done.3 = bf16[24,768]{1,0:T(8,128)(2,1)S(1)} collective-permute-done((bf16[24,768]{1,0:T(8,128)(2,1)S(1)}, bf16[24,768]{1,0:T(8,128)(2,1)S(1)}, u32[]{:S(2)}, u32[]{:S(2)}) %collective-permute-start.3) | collective-permute-done | bytes 36896 | tf_op jit(solution)/shard_map/ppermute | solution.py:30
  32.8 3.2 %shard_map.140 = (bf16[10,512]{1,0:T(8,128)(2,1)S(1)}, bf16[8,512]{1,0:T(8,128)(2,1)S(1)}) custom-call(s32[2]{0:T(128)S(1)} %pad_add_fusion.refs_0_, bf16[48,768]{1,0:T(8,128)(2,1)S(1)} %pad_maximum_fusion.1.refs_1_, bf16[256,432]{1,0:T(8,128)(2,1)S(1)} %copy.60.refs_2_, bf16[256,2304]{1,0:T(8,128)(2,1)S(1)} %get-tuple-element.10.refs_3_, ...), custom_call_target="tpu_custom_call" | custom-call | tf_op jit(solution)/shard_map/pallas_call | solution.py:277
  36.0 1.9 %collective-permute-start.4 = (bf16[24,1024]{1,0:T(8,128)(2,1)S(1)}, bf16[24,1024]{1,0:T(8,128)(2,1)S(1)}, u32[]{:S(2)}, u32[]{:S(2)}) collective-permute-start(bf16[24,1024]{1,0:T(8,128)(2,1)S(1)} %get-tuple-element.20), channel_id=1, source_target_pairs={{0,8},{4,12},{8,16},{12,20},{16,24},{20,28},{24,32},{28,36},{32,40... | collective-permute-start | bytes 147464 | tf_op jit(solution)/shard_map/ppermute | solution.py:20
  40.5 0.8 copy-done.1
  42.7 4.0 %collective-permute-start.5 = (bf16[24,2048]{1,0:T(8,128)(2,1)S(1)}, bf16[24,2048]{1,0:T(8,128)(2,1)S(1)}, u32[]{:S(2)}, u32[]{:S(2)}) collective-permute-start(bf16[24,2048]{1,0:T(8,128)(2,1)S(1)} %pad_maximum_fusion), channel_id=1, source_target_pairs={{0,4},{4,8},{8,12},{12,16},{16,20},{20,24},{24,28},{28,32},{32,36}... | collective-permute-start | bytes 294920 | tf_op jit(solution)/shard_map/ppermute | solution.py:20
  46.7 6.9 %collective-permute-start.6 = (bf16[24,2048]{1,0:T(8,128)(2,1)S(1)}, bf16[24,2048]{1,0:T(8,128)(2,1)S(1)}, u32[]{:S(2)}, u32[]{:S(2)}) collective-permute-start(bf16[24,2048]{1,0:T(8,128)(2,1)S(1)} %pad_maximum_fusion), channel_id=1, source_target_pairs={{4,0},{8,4},{12,8},{16,12},{20,16},{24,20},{28,24},{32,28},{36,32}... | collective-permute-start | bytes 294920 | tf_op jit(solution)/shard_map/ppermute | solution.py:20
  53.7 4.8 %collective-permute-start.7 = (bf16[24,1024]{1,0:T(8,128)(2,1)S(1)}, bf16[24,1024]{1,0:T(8,128)(2,1)S(1)}, u32[]{:S(2)}, u32[]{:S(2)}) collective-permute-start(bf16[24,1024]{1,0:T(8,128)(2,1)S(1)} %get-tuple-element.19), channel_id=1, source_target_pairs={{8,0},{12,4},{16,8},{20,12},{24,16},{28,20},{32,24},{36,28},{40,32... | collective-permute-start | bytes 147464 | tf_op jit(solution)/shard_map/ppermute | solution.py:20
  58.5 0.8 broadcast_in_dim.20
  59.3 7.2 %all-to-all-start = ((bf16[64,8,512]{2,1,0:T(8,128)(2,1)}), bf16[64,8,512]{2,1,0:T(8,128)(2,1)S(1)}, u32[]{:S(2)}, u32[]{:S(2)}) async-start(bf16[64,8,512]{2,1,0:T(8,128)(2,1)} %broadcast_in_dim.20), calls=%async_computation | async-start | bytes 1048576 | tf_op jit(solution)/shard_map/all_to_all | solution.py:346
  69.4 3.8 %shard_map.142.refs_4_ = f32[6,192,1024]{2,1,0:T(8,128)} custom-call(bf16[24,8192]{1,0:T(8,128)(2,1)} %copy-done.5, bf16[24,8192]{1,0:T(8,128)(2,1)} %copy-done.6, bf16[192,432]{1,0:T(8,128)(2,1)} %copy.66.w_ref), custom_call_target="tpu_custom_call" | custom-call | tf_op jit(solution)/shard_map/pallas_call | solution.py:277
  73.2 8.3 %all-to-all-done = bf16[64,8,512]{2,1,0:T(8,128)(2,1)S(1)} async-done(((bf16[64,8,512]{2,1,0:T(8,128)(2,1)}), bf16[64,8,512]{2,1,0:T(8,128)(2,1)S(1)}, u32[]{:S(2)}, u32[]{:S(2)}) %all-to-all-start) | async-done | bytes 524320 | tf_op jit(solution)/shard_map/all_to_all | solution.py:346
  82.3 13.4 %shard_map.143 = (bf16[2,10,1024]{2,1,0:T(8,128)(2,1)}, bf16[128,128]{1,0:T(8,128)(2,1)}) custom-call(s32[2]{0:T(128)} %copy-done.3, s32[64,8]{1,0:T(8,128)} %bitcast.100, bf16[512,512]{1,0:T(8,128)(2,1)} %bitcast.91, bf16[512,512]{1,0:T(8,128)(2,1)} %copy-done.1, f32[6,192,1024]{2,1,0:T(8,128)} %shard_map.142.refs_4_, bf16[192,96]{1,0:T(8,128)(2,1)} %copy.71.refs_5_, ...), custom_call_target="tpu_custom_call" | custom-call | tf_op jit(solution)/shard_map/pallas_call | solution.py:277
  95.7 7.5 %all-to-all-start.1 = ((bf16[64,2,128]{2,1,0:T(2,128)(2,1)}), bf16[64,2,128]{2,1,0:T(2,128)(2,1)S(1)}, u32[]{:S(2)}, u32[]{:S(2)}) async-start(bf16[64,2,128]{2,1,0:T(2,128)(2,1)} %bitcast.103), calls=%async_computation.1 | async-start | bytes 65536 | tf_op jit(solution)/shard_map/all_to_all | solution.py:407
  103.9 1.5 %copy.73 = bf16[2,10,1024]{2,0,1:T(2,128)(2,1)} copy(bf16[2,10,1024]{2,1,0:T(8,128)(2,1)} %get-tuple-element.15) | data formatting | bytes 81920 | tf_op jit(solution)/shard_map/pallas_call | solution.py:277
  105.4 6.9 %all-to-all-done.1 = bf16[64,2,128]{2,1,0:T(2,128)(2,1)S(1)} async-done(((bf16[64,2,128]{2,1,0:T(2,128)(2,1)}), bf16[64,2,128]{2,1,0:T(2,128)(2,1)S(1)}, u32[]{:S(2)}, u32[]{:S(2)}) %all-to-all-start.1) | async-done | bytes 32800 | tf_op jit(solution)/shard_map/all_to_all | solution.py:407
  112.3 3.2 %shard_map.144 = f32[2,512]{1,0:T(2,128)} custom-call(bf16[128,128]{1,0:T(8,128)(2,1)S(1)} %bitcast.90, f32[128,512]{1,0:T(8,128)S(1)} %add_add_fusion.refs_1_), custom_call_target="tpu_custom_call" | custom-call | tf_op jit(solution)/shard_map/pallas_call | solution.py:277
  (107 shorter events, 15.5 us)
Async XLA Ops:
  0.6 13.4 %copy-start = (bf16[3,3,3,6,32]{4,3,2,1,0:T(8,128)(2,1)S(1)}, bf16[3,3,3,6,32]{4,3,2,1,0:T(8,128)(2,1)}, u32[]{:S(2)}) copy-start(bf16[3,3,3,6,32]{4,3,2,1,0:T(8,128)(2,1)} %param.17) | copy-start | bytes 31108
  0.6 14.8 %copy-start.9 = (bf16[3,3,3,32,5]{3,2,4,1,0:T(4,128)(2,1)S(1)}, bf16[3,3,3,32,5]{3,2,4,1,0:T(4,128)(2,1)}, u32[]{:S(2)}) copy-start(bf16[3,3,3,32,5]{3,2,4,1,0:T(4,128)(2,1)} %param.19) | copy-start | bytes 25924
  3.1 16.1 %collective-permute-start = (bf16[12,2560]{1,0:T(8,128)(2,1)S(1)}, bf16[12,2560]{1,0:T(8,128)(2,1)S(1)}, u32[]{:S(2)}, u32[]{:S(2)}) collective-permute-start(bf16[12,2560]{1,0:T(8,128)(2,1)S(1)} %constant_dynamic-update-slice_fusion), channel_id=1, source_target_pairs={{0,2},{1,3},{2,0},{3,1},{4,6},{5,7},{6,4},{7,5},{8,10},{9,11},{10,... | collective-permute-start | bytes 184328 | tf_op jit(solution)/shard_map/ppermute | solution.py:30
  12.7 4.1 %copy-start.8 = (bf16[3,3,3,7,32]{4,3,2,1,0:T(8,128)(2,1)S(1)}, bf16[3,3,3,7,32]{4,3,2,1,0:T(8,128)(2,1)}, u32[]{:S(2)}) copy-start(bf16[3,3,3,7,32]{4,3,2,1,0:T(8,128)(2,1)} %param.20) | copy-start | bytes 36292
  12.7 4.4 %copy-start.10 = (bf16[3,3,3,32,5]{3,2,4,1,0:T(4,128)(2,1)S(1)}, bf16[3,3,3,32,5]{3,2,4,1,0:T(4,128)(2,1)}, u32[]{:S(2)}) copy-start(bf16[3,3,3,32,5]{3,2,4,1,0:T(4,128)(2,1)} %param.22) | copy-start | bytes 25924
  16.7 25.4 %copy-start.11 = (s32[64,128]{1,0:T(8,128)S(1)}, s32[64,128]{1,0:T(8,128)}, u32[]{:S(2)}) copy-start(s32[64,128]{1,0:T(8,128)} %param.16) | copy-start | bytes 98308
  17.1 25.7 %copy-start.3 = (s32[2]{0:T(128)}, s32[2]{0:T(128)S(1)}, u32[]{:S(2)}) copy-start(s32[2]{0:T(128)S(1)} %pad_add_fusion.refs_0_) | copy-start | bytes 28
  18.4 17.6 %copy-start.2 = (bf16[128,1728]{1,0:T(8,128)(2,1)}, bf16[128,1728]{1,0:T(8,128)(2,1)S(1)}, u32[]{:S(2)}) copy-start(bf16[128,1728]{1,0:T(8,128)(2,1)S(1)} %get-tuple-element.14.refs_6_) | copy-start | bytes 1327108
  19.3 10.7 %collective-permute-start.1 = (bf16[24,96]{1,0:T(8,128)(2,1)S(1)}, bf16[24,96]{1,0:T(8,128)(2,1)S(1)}, u32[]{:S(2)}, u32[]{:S(2)}) collective-permute-start(bf16[24,96]{1,0:T(8,128)(2,1)S(1)} %get-tuple-element.17), channel_id=1, source_target_pairs={{0,4},{4,8},{8,12},{12,16},{16,20},{20,24},{24,28},{28,32},{32,36}... | collective-permute-start | bytes 13832 | tf_op jit(solution)/shard_map/ppermute | solution.py:20
  22.8 8.5 %collective-permute-start.2 = (bf16[24,96]{1,0:T(8,128)(2,1)S(1)}, bf16[24,96]{1,0:T(8,128)(2,1)S(1)}, u32[]{:S(2)}, u32[]{:S(2)}) collective-permute-start(bf16[24,96]{1,0:T(8,128)(2,1)S(1)} %get-tuple-element.18), channel_id=1, source_target_pairs={{4,0},{8,4},{12,8},{16,12},{20,16},{24,20},{28,24},{32,28},{36,32}... | collective-permute-start | bytes 13832 | tf_op jit(solution)/shard_map/ppermute | solution.py:20
  31.4 1.3 %collective-permute-start.3 = (bf16[24,768]{1,0:T(8,128)(2,1)S(1)}, bf16[24,768]{1,0:T(8,128)(2,1)S(1)}, u32[]{:S(2)}, u32[]{:S(2)}) collective-permute-start(bf16[24,768]{1,0:T(8,128)(2,1)S(1)} %pad_maximum_fusion.3), channel_id=1, source_target_pairs={{0,1},{1,0},{2,3},{3,2},{4,5},{5,4},{6,7},{7,6},{8,9},{9,8},{10,11... | collective-permute-start | bytes 110600 | tf_op jit(solution)/shard_map/ppermute | solution.py:30
  32.7 35.0 %copy-start.7 = (bf16[5,2,2,1024]{3,2,1,0:T(2,128)(2,1)S(1)}, bf16[5,2,2,1024]{3,2,1,0:T(2,128)(2,1)}, u32[]{:S(2)}) copy-start(bf16[5,2,2,1024]{3,2,1,0:T(2,128)(2,1)} %param.14) | copy-start | bytes 122884
  36.0 30.6 %collective-permute-start.4 = (bf16[24,1024]{1,0:T(8,128)(2,1)S(1)}, bf16[24,1024]{1,0:T(8,128)(2,1)S(1)}, u32[]{:S(2)}, u32[]{:S(2)}) collective-permute-start(bf16[24,1024]{1,0:T(8,128)(2,1)S(1)} %get-tuple-element.20), channel_id=1, source_target_pairs={{0,8},{4,12},{8,16},{12,20},{16,24},{20,28},{24,32},{28,36},{32,40... | collective-permute-start | bytes 147464 | tf_op jit(solution)/shard_map/ppermute | solution.py:20
  40.5 0.8 copy-start.1
  42.7 23.8 %collective-permute-start.5 = (bf16[24,2048]{1,0:T(8,128)(2,1)S(1)}, bf16[24,2048]{1,0:T(8,128)(2,1)S(1)}, u32[]{:S(2)}, u32[]{:S(2)}) collective-permute-start(bf16[24,2048]{1,0:T(8,128)(2,1)S(1)} %pad_maximum_fusion), channel_id=1, source_target_pairs={{0,4},{4,8},{8,12},{12,16},{16,20},{20,24},{24,28},{28,32},{32,36}... | collective-permute-start | bytes 294920 | tf_op jit(solution)/shard_map/ppermute | solution.py:20
  46.7 19.9 %collective-permute-start.6 = (bf16[24,2048]{1,0:T(8,128)(2,1)S(1)}, bf16[24,2048]{1,0:T(8,128)(2,1)S(1)}, u32[]{:S(2)}, u32[]{:S(2)}) collective-permute-start(bf16[24,2048]{1,0:T(8,128)(2,1)S(1)} %pad_maximum_fusion), channel_id=1, source_target_pairs={{4,0},{8,4},{12,8},{16,12},{20,16},{24,20},{28,24},{32,28},{36,32}... | collective-permute-start | bytes 294920 | tf_op jit(solution)/shard_map/ppermute | solution.py:20
  53.7 13.0 %collective-permute-start.7 = (bf16[24,1024]{1,0:T(8,128)(2,1)S(1)}, bf16[24,1024]{1,0:T(8,128)(2,1)S(1)}, u32[]{:S(2)}, u32[]{:S(2)}) collective-permute-start(bf16[24,1024]{1,0:T(8,128)(2,1)S(1)} %get-tuple-element.19), channel_id=1, source_target_pairs={{8,0},{12,4},{16,8},{20,12},{24,16},{28,20},{32,24},{36,28},{40,32... | collective-permute-start | bytes 147464 | tf_op jit(solution)/shard_map/ppermute | solution.py:20
  59.3 22.2 %all-to-all-start = ((bf16[64,8,512]{2,1,0:T(8,128)(2,1)}), bf16[64,8,512]{2,1,0:T(8,128)(2,1)S(1)}, u32[]{:S(2)}, u32[]{:S(2)}) async-start(bf16[64,8,512]{2,1,0:T(8,128)(2,1)} %broadcast_in_dim.20), calls=%async_computation | async-start | bytes 1048576 | tf_op jit(solution)/shard_map/all_to_all | solution.py:346
  66.6 2.0 %copy-start.5 = (bf16[24,8192]{1,0:T(8,128)(2,1)}, bf16[24,8192]{1,0:T(8,128)(2,1)S(1)}, u32[]{:S(2)}) copy-start(bf16[24,8192]{1,0:T(8,128)(2,1)S(1)} %constant_dynamic-update-slice_fusion.2.x0_ref) | copy-start | bytes 1179652
  66.7 2.0 %collective-permute-start.8 = (bf16[24,8192]{1,0:T(8,128)(2,1)S(1)}, bf16[24,8192]{1,0:T(8,128)(2,1)S(1)}, u32[]{:S(2)}, u32[]{:S(2)}) collective-permute-start(bf16[24,8192]{1,0:T(8,128)(2,1)S(1)} %constant_dynamic-update-slice_fusion.2.x0_ref), channel_id=1, source_target_pairs={{0,1},{1,0},{2,3},{3,2},{4,5},{5,4},{6,7},{7,6},{8,9},{9,8},{10,11... | collective-permute-start | bytes 1179656 | tf_op jit(solution)/shard_map/ppermute | solution.py:30
  68.6 0.7 copy-start.6
  81.5 0.8 copy-start.4
  95.7 16.6 %all-to-all-start.1 = ((bf16[64,2,128]{2,1,0:T(2,128)(2,1)}), bf16[64,2,128]{2,1,0:T(2,128)(2,1)S(1)}, u32[]{:S(2)}, u32[]{:S(2)}) async-start(bf16[64,2,128]{2,1,0:T(2,128)(2,1)} %bitcast.103), calls=%async_computation.1 | async-start | bytes 65536 | tf_op jit(solution)/shard_map/all_to_all | solution.py:407

commit v3 on v2

--- a/solution.py
+++ b/solution.py
@@ -36,7 +36,7 @@
     return jnp.pad(base, ((0, 0), (0, 0), (0, 128 - 3 * c)))
 
 
-def weights_kernel(nz, scal_ref, p_ref, d_ref, pout_ref, dout_ref):
+def primal_weights_kernel(nz, p_ref, pout_ref):
     o = p_ref.shape[1]
     width = pout_ref.shape[1] // 9
     c = width // nz
@@ -51,6 +51,12 @@
             elif zo == nz - 1:
                 moved = jnp.where(lane >= c * (zo - 1), moved, 0.0)
             pout_ref[zo * o : (zo + 1) * o, tap * width : (tap + 1) * width] = moved.astype(BF)
+
+
+def dual_weights_kernel(nz, scal_ref, d_ref, dout_ref):
+    o = d_ref.shape[1]
+    c = dout_ref.shape[1] // 9 // (dout_ref.shape[0] // o + 2)
+    width = 256
     count = dout_ref.shape[0] // o
     span = (count + 2) * c
     first = scal_ref[1] * 2 - 1
@@ -76,9 +82,9 @@
     lax.fori_loop(0, u_ref.shape[0], one, 0)
 
 
-def positions(angle_ids, angle_total):
+def positions(angle_ids, angle_total, first_pixel=0):
     angle_value = angle_ids.astype(F32) * (math.pi / angle_total)
-    pixels = jnp.arange(TX * NY, dtype=jnp.int32)
+    pixels = (jnp.arange(TX * NY, dtype=jnp.int32) + first_pixel) % (TX * NY)
     centre_x = (pixels // NY).astype(F32) - (TX - 1) / 2.0
     centre_y = (pixels % NY).astype(F32) - (NY - 1) / 2.0
     return (
@@ -133,7 +139,10 @@
         total = total + acc
     total = pltpu.roll(total, lanes - HALO * NY, 1)[:, : TX * NY]
     per = rows // 4
-    lead_ref[...] = jnp.concatenate([total[i * per : i * per + 2] for i in range(4)], axis=0).astype(BF)
+    lead = jnp.concatenate([total[i * per : i * per + 2] for i in range(4)], axis=0)
+    lead = jnp.where((scal_ref[1] & 1) == 0, lead, pltpu.roll(lead, 4, 0))
+    half = TX * NY // 2
+    lead_ref[...] = jnp.where((scal_ref[1] & 1) == 0, lead[:, :half], lead[:, half:]).astype(BF)
     own_ref[...] = total[: own_ref.shape[0]].astype(BF)
 
 
@@ -147,32 +156,19 @@
     return jnp.where(bins == v.shape[1] - 1, 0.0, pltpu.roll(v, v.shape[1] - 1, 1))
 
 
-def known_kernel(x0_ref, x1_ref, w_ref, out_ref, col, part, sems):
-    nb = col.shape[2]
-    for a in range(8):
-        at = slice(a * nb, (a + 1) * nb)
-        known = jnp.concatenate([x0_ref[:, at].astype(F32), x1_ref[:, at].astype(F32)], axis=0)
-        col[a] = jnp.concatenate([before(known), known, after(known)], axis=0).astype(BF)
-    for a in range(6):
-        part[a] = jnp.dot(w_ref[...], col[a : a + 3].reshape(-1, nb), preferred_element_type=F32)
-        pltpu.make_async_copy(part.at[a], out_ref.at[a], sems.at[a]).start()
-    for a in range(6):
-        pltpu.make_async_copy(part.at[a], out_ref.at[a], sems.at[a]).wait()
-
-
 def dual_kernel(tiles, angles, *refs):
-    (scal_ref, off_ref, gv_ref, t8_ref, known_ref, w1_ref, w2_ref, w3_ref, ds_ref, out_ref, piece_ref) = refs[:11]
-    (win, x1, h1, h2, parts, nd, pc, known, sem) = refs[11:20]
+    (scal_ref, off_ref, g0_ref, g1_ref, t8_ref, xa_ref, xb_ref, w1_ref, w2_ref, w3_ref, ds_ref, out_ref, piece_ref) = refs[:13]
+    (win, x1, h1, h2, parts, nd, pc) = refs[13:20]
     pj = refs[20:]
-    fetch = pltpu.make_async_copy(known_ref, known, sem)
-    fetch.start()
     nb = x1.shape[2]
     blocks = nb // 128
     lane = lax.broadcasted_iota(jnp.int32, (8, 128), 1)
     first_angle = scal_ref[0] * 2 - HALO
 
-    windows = lax.dot_general(
-        gv_ref[...], t8_ref[...], (((1,), (1,)), ((), ())), preferred_element_type=F32
+    half = g0_ref.shape[1]
+    windows = sum(
+        lax.dot_general(ref[...], t8_ref[:, at : at + half], (((1,), (1,)), ((), ())), preferred_element_type=F32)
+        for ref, at in ((g0_ref, 0), (g1_ref, half))
     )
     win[...] = windows.astype(BF).astype(F32)
     for ref in pj:
@@ -200,14 +196,17 @@
         valid = ((first_angle + a) >= 0) & ((first_angle + a) < angles)
         proj = jnp.concatenate([pj[a][b] for b in range(blocks)], axis=1) * (1.0 / math.sqrt(NY))
         proj = jnp.where(valid, proj, 0.0).astype(BF).astype(F32)
-        x1[a] = jnp.concatenate([before(proj), proj, after(proj), jnp.zeros((8, nb), F32)], axis=0).astype(BF)
-
-    fetch.wait()
+        at = slice(a * nb, (a + 1) * nb)
+        known = jnp.concatenate([xa_ref[:, at].astype(F32), xb_ref[:, at].astype(F32)], axis=0)
+        x1[a] = jnp.concatenate(
+            [before(known), known, after(known), before(proj), proj, after(proj), jnp.zeros((8, nb), F32)], axis=0
+        ).astype(BF)
+
     k1 = x1.shape[1]
     for a in range(6):
         valid = ((first_angle + a + 1) >= 0) & ((first_angle + a + 1) < angles)
         h = jnp.dot(w1_ref[...], x1[a : a + 3].reshape(3 * k1, nb), preferred_element_type=F32)
-        h = jnp.where(valid, jnp.maximum(h + known[a], 0.0), 0.0)
+        h = jnp.where(valid, jnp.maximum(h, 0.0), 0.0)
         rows = h.shape[0]
         h1[a, 0:rows] = before(h).astype(BF)
         h1[a, rows : 2 * rows] = h.astype(BF)
@@ -270,15 +269,14 @@
     out_ref[...] = total[0:2] * scale
 
 
-def call(kernel, outs, scratch, args, smem, hbm_in=(), hbm_out=False, mib=24):
+def call(kernel, outs, scratch, args, smem, mib=24):
     vm = pl.BlockSpec(memory_space=pltpu.VMEM)
     sm = pl.BlockSpec(memory_space=pltpu.SMEM)
-    hb = pl.BlockSpec(memory_space=pltpu.HBM)
     return pl.pallas_call(
         kernel,
         out_shape=outs,
-        in_specs=[sm if i < smem else hb if i in hbm_in else vm for i in range(len(args))],
-        out_specs=[hb if hbm_out else vm] * len(outs),
+        in_specs=[sm] * smem + [vm] * (len(args) - smem),
+        out_specs=[vm] * len(outs),
         scratch_shapes=scratch,
         compiler_params=pltpu.CompilerParams(vmem_limit_bytes=mib * 1024 * 1024),
     )(*args)
@@ -313,8 +311,12 @@
     xg = jnp.concatenate([xg, swapped(xg, 1)], axis=0)
 
     all_z = jnp.arange(nz, dtype=jnp.int32)
-    seen = (s ^ jnp.array([0, 2, 1, 3], jnp.int32))[:, None] * zl + jnp.arange(zl, dtype=jnp.int32)[None]
-    seen = seen.reshape(nz)
+    def z_order(slab):
+        slabs = slab ^ jnp.array([0, 2, 1, 3], jnp.int32)
+        return (slabs[:, None] * zl + jnp.arange(zl, dtype=jnp.int32)[None]).reshape(nz)
+
+    seen = z_order(s)
+    lead_z = z_order(s & 2)
     e = band(all_z, seen)
     e_out = band(seen, all_z)
 
@@ -327,14 +329,13 @@
     pw3 = jnp.einsum("pyzd,dabco->abpoyzc", e_out.reshape(slab_count, zl, nz, 3), third)
     pw3 = pw3.reshape(9 * nz * (mem + 1), nz * hid)
     one, two = (zl + 4) * hid, (zl + 2) * hid
-    pw2, dw2 = call(
-        lambda *refs: weights_kernel(nz, *refs),
-        [jax.ShapeDtypeStruct((nz * hid, 9 * nz * hid), BF), jax.ShapeDtypeStruct((two, 9 * one), BF)],
-        [], (scal, hidden_base(primal_second), hidden_base(dual_second)), 1,
+    (pw2,) = call(
+        lambda *refs: primal_weights_kernel(nz, *refs),
+        [jax.ShapeDtypeStruct((nz * hid, 9 * nz * hid), BF)], [], (hidden_base(primal_second),), 0,
     )
     own, lead = call(
         lambda *refs: primal_kernel(wide_count * TX, *refs),
-        [jax.ShapeDtypeStruct((mem * zl, pix), BF), jax.ShapeDtypeStruct((nz, pix), BF)],
+        [jax.ShapeDtypeStruct((mem * zl, pix), BF), jax.ShapeDtypeStruct((nz, pix // 2), BF)],
         [
             pltpu.VMEM((9 * xg.shape[0], xg.shape[1]), BF),
             pltpu.VMEM((9 * nz * hid, xg.shape[1]), BF),
@@ -342,8 +343,9 @@
         (scal, xg, pw1, pw2, pw3), 1,
     )
 
-    sent = jnp.broadcast_to(lead[None], (wide_count, nz, pix))
+    sent = jnp.broadcast_to(lead[None], (wide_count, nz, pix // 2))
     gv = lax.all_to_all(sent, "wide", split_axis=0, concat_axis=0, tiled=True)
+    gv = gv.reshape(wide_count * nz, pix // 2)
 
     xd, _ = lax.optimization_barrier((xd, lead))
     xk = jnp.concatenate(
@@ -356,7 +358,13 @@
         ],
         axis=1,
     )
-    xk = (xk, swapped(xk, 1))
+    xk, dual_first, dual_second, dual_third, w, offsets = lax.optimization_barrier(
+        (xk, dual_first, dual_second, dual_third, w, offsets)
+    )
+    (dw2,) = call(
+        lambda *refs: dual_weights_kernel(nz, *refs),
+        [jax.ShapeDtypeStruct((two, 9 * one), BF)], [], (scal, hidden_base(dual_second)), 1,
+    )
     z_one = s * zl - 2 + jnp.arange(zl + 4, dtype=jnp.int32)
     z_two = s * zl - 1 + jnp.arange(zl + 2, dtype=jnp.int32)
     z_own = s * zl + jnp.arange(zl, dtype=jnp.int32)
@@ -365,25 +373,25 @@
 
     e_one = band(z_one, seen) * inside_z(z_one)
     state_sino = jnp.concatenate([dual_first[:, :, :, :mem], dual_first[:, :, :, mem + 1 :]], axis=3)
-    dw1a = first_known(state_sino, e_one).reshape(one, -1)
-    dw1b = jnp.einsum("yzd,dabo->yoabz", e_one, dual_first[:, :, :, mem]).reshape(one, 3, 3 * nz)
-    dw1b = jnp.pad(dw1b, ((0, 0), (0, 0), (0, 8))).reshape(one, -1)
+    dw1a = first_known(state_sino, e_one)
+    e_lead = band(z_one, lead_z) * inside_z(z_one)
+    dw1b = jnp.einsum("yzd,dabo->yoabz", e_lead, dual_first[:, :, :, mem]).reshape(one, 3, 3 * nz)
+    dw1 = jnp.concatenate([dw1a, dw1b, jnp.zeros((one, 3, 8), BF)], axis=2).reshape(one, -1)
     dw3 = jnp.einsum("yzd,dabco->aboyzc", band(z_own, z_two), dual_third).reshape(9, mem * zl, two)
     dw3 = jnp.pad(dw3, ((0, 0), (0, 16 - mem * zl), (0, 0))).reshape(9 * 16, two)
-    (known,) = call(
-        known_kernel, [jax.ShapeDtypeStruct((6, one, nb), F32)],
-        [pltpu.VMEM((8, 3 * nz * (mem + 1), nb), BF), pltpu.VMEM((6, one, nb), F32), pltpu.SemaphoreType.DMA((6,))],
-        (*xk, dw1a), 0, hbm_out=True, mib=60,
-    )
-
     near_ids = w * own_angles - HALO + jnp.arange(8, dtype=jnp.int32)
     (table8,) = call(
-        table_kernel, [jax.ShapeDtypeStruct((8 * BINS, pix), BF)], [], (positions(near_ids, angles),), 0
+        table_kernel, [jax.ShapeDtypeStruct((8 * BINS, pix), BF)], [], (positions(near_ids, angles, (s & 1) * (pix // 2)),), 0
     )
     off8 = jnp.take(offsets, jnp.clip(near_ids, 0, angles - 1), axis=1)
 
     blocks = nb // 128
     ds = dual_state.transpose(2, 0, 1, 3).reshape(own_angles, mem * zl, nb)
+    gv, xk, off8, table8, dw1, dw2, dw3, ds = lax.optimization_barrier(
+        (gv, xk, off8, table8, dw1, dw2, dw3, ds)
+    )
+    gv = (gv, swapped(gv, 1))
+    xk = (xk, swapped(xk, 1))
     nd, pieces = call(
         lambda *refs: dual_kernel(wide_count, angles, *refs),
         [
@@ -392,17 +400,15 @@
         ],
         [
             pltpu.VMEM((wide_count * nz, 8 * BINS), F32),
-            pltpu.VMEM((8, 4 * 8, nb), BF),
+            pltpu.VMEM((8, dw1.shape[1] // 3, nb), BF),
             pltpu.VMEM((6, 3 * one, nb), BF),
             pltpu.VMEM((4, two, nb), BF),
             pltpu.VMEM((4, 9 * 16, nb), F32),
             pltpu.VMEM((own_angles, blocks + 1, 8, 128), F32),
             pltpu.VMEM((wide_count * zl, 128), F32),
-            pltpu.VMEM((6, one, nb), F32),
-            pltpu.SemaphoreType.DMA,
         ]
         + [pltpu.VMEM((blocks + 1, 8, 128), F32)] * 8,
-        (scal, off8, gv.reshape(wide_count * nz, pix), table8, known, dw1b, dw2, dw3, ds), 2, hbm_in=(4,), mib=60,
+        (scal, off8, *gv, table8, *xk, dw1, dw2, dw3, ds), 2, mib=32,
     )
     arrived = lax.all_to_all(
         pieces.reshape(wide_count, zl, 128), "wide", split_axis=0, concat_axis=0, tiled=True

time: 116 us -> 104 us (0.90)
  local copies, waits for them, and re-layouts: 15 us -> 6.93 us
  Pallas kernels: 24.7 us -> 21.5 us
    pallas_call x6, Pallas kernels: 24.7 us -> 21.5 us  [call(): pl.pallas_call(kernel, out_shape=outs, in_specs=[sm] * smem + [vm] * (len...]
    all_to_all x1, waiting for transfers between devices: 8.29 us -> 5.86 us  [body(): gv = lax.all_to_all(sent, 'wide', split_axis=0, concat_axis=0, tiled=True)]
    unnamed x35 -> x24, local copies, waits for them, and re-layouts: 2.63 us -> 0.33 us
    transpose x2, local copies, waits for them, and re-layouts: 2.27 us -> 0.4 us  [hidden_base(): base = w.transpose(1, 2, 4, 0, 3).reshape(9, o, 3 * c)]
    another operation x2 -> x0, local copies, waits for them, and re-layouts: 1.3 us -> none  [body(): dw1a = first_known(state_sino, e_one).reshape(one, -1)]
    all_to_all x1, starting transfers between devices: 7.46 us -> 6.29 us  [body(): lax.all_to_all(pieces.reshape(wide_count, zl, 128), 'wide', split_axis=0,...]
    ppermute x3 -> x4, waiting for transfers between devices: 1.41 us -> 2.49 us  [swapped(): return lax.ppermute(value, 'slab', [(i, i ^ mask) for i in range(size)])]
    ppermute x3 -> x4, starting transfers between devices: 7.64 us -> 7.88 us  [swapped(): return lax.ppermute(value, 'slab', [(i, i ^ mask) for i in range(size)])]
  transfers between devices with their start and end apart: 11 -> 12, of which waited for: 5 -> 5; matrix products, arithmetic and copies ran while one was open for 14% -> 10% of each run, Pallas kernels for 4% -> 1%
where the time goes in v3:
time: 104 us; the launch traced here: 103 us
  starting transfers between devices  49.6 us (48%)
  Pallas kernels  21.5 us (21%)
  waiting for transfers between devices  17.4 us (17%)
  local copies, waits for them, and re-layouts  6.93 us (7%)
  other arithmetic  4.32 us (4%)
  matrix products  1.83 us (2%)
  between operations  1.31 us (1%)
    ppermute x6, starting transfers between devices, shifted(): lax.ppermute(value, axis, [(i, i + delta) for i in range(size) if 0 <= i...  28.3 us
    pallas_call x6, Pallas kernels, call(): pl.pallas_call(kernel, out_shape=outs, in_specs=[sm] * smem + [vm] * (len...  21.5 us
    ppermute x4, starting transfers between devices, swapped(): return lax.ppermute(value, 'slab', [(i, i ^ mask) for i in range(size)])  7.88 us
    all_to_all x1, waiting for transfers between devices, body(): lax.all_to_all(pieces.reshape(wide_count, zl, 128), 'wide', split_axis=0,...  7.74 us
    all_to_all x1, starting transfers between devices, body(): gv = lax.all_to_all(sent, 'wide', split_axis=0, concat_axis=0, tiled=True)  7.19 us
    all_to_all x1, starting transfers between devices, body(): lax.all_to_all(pieces.reshape(wide_count, zl, 128), 'wide', split_axis=0,...  6.29 us
    all_to_all x1, waiting for transfers between devices, body(): gv = lax.all_to_all(sent, 'wide', split_axis=0, concat_axis=0, tiled=True)  5.86 us
    ppermute x4, waiting for transfers between devices, swapped(): return lax.ppermute(value, 'slab', [(i, i ^ mask) for i in range(size)])  2.49 us
  transfers between devices with their start and end apart: 12, of which 5 were waited for; matrix products, arithmetic and copies ran while one was open for 10% of the time, Pallas kernels for 1%

profile of v3, /device:TPU:2, one launch (start us, length us, event | category | flops | bytes accessed | tf_op | source)
XLA Modules:
  0.0 102.9 jit_solution(7584680932184901805)
XLA Ops:
  0.6 0.9 pad_maximum_fusion.2
  1.6 0.7 convert_bitcast_fusion
  2.3 0.7 pad_maximum_fusion.5
  3.1 7.3 %collective-permute-start = (bf16[12,2560]{1,0:T(8,128)(2,1)S(1)}, bf16[12,2560]{1,0:T(8,128)(2,1)S(1)}, u32[]{:S(2)}, u32[]{:S(2)}) collective-permute-start(bf16[12,2560]{1,0:T(8,128)(2,1)S(1)} %constant_dynamic-update-slice_fusion), channel_id=1, source_target_pairs={{0,2},{1,3},{2,0},{3,1},{4,6},{5,7},{6,4},{7,5},{8,10},{9,11},{10,... | collective-permute-start | bytes 184328 | tf_op jit(solution)/shard_map/ppermute | solution.py:30
  10.3 0.7 xor_multiply_fusion
  15.1 3.5 %collective-permute-start.1 = (bf16[24,96]{1,0:T(8,128)(2,1)S(1)}, bf16[24,96]{1,0:T(8,128)(2,1)S(1)}, u32[]{:S(2)}, u32[]{:S(2)}) collective-permute-start(bf16[24,96]{1,0:T(8,128)(2,1)S(1)} %get-tuple-element.41), channel_id=1, source_target_pairs={{0,4},{4,8},{8,12},{12,16},{16,20},{20,24},{24,28},{28,32},{32,36}... | collective-permute-start | bytes 13832 | tf_op jit(solution)/shard_map/ppermute | solution.py:20
  18.6 7.2 %collective-permute-start.2 = (bf16[24,96]{1,0:T(8,128)(2,1)S(1)}, bf16[24,96]{1,0:T(8,128)(2,1)S(1)}, u32[]{:S(2)}, u32[]{:S(2)}) collective-permute-start(bf16[24,96]{1,0:T(8,128)(2,1)S(1)} %get-tuple-element.42), channel_id=1, source_target_pairs={{4,0},{8,4},{12,8},{16,12},{20,16},{24,20},{28,24},{32,28},{36,32}... | collective-permute-start | bytes 13832 | tf_op jit(solution)/shard_map/ppermute | solution.py:20
  25.8 1.3 %collective-permute-done.2 = bf16[24,96]{1,0:T(8,128)(2,1)S(1)} collective-permute-done((bf16[24,96]{1,0:T(8,128)(2,1)S(1)}, bf16[24,96]{1,0:T(8,128)(2,1)S(1)}, u32[]{:S(2)}, u32[]{:S(2)}) %collective-permute-start.2) | collective-permute-done | bytes 4640 | tf_op jit(solution)/shard_map/ppermute | solution.py:20
  27.3 1.2 %collective-permute-done.3 = bf16[24,768]{1,0:T(8,128)(2,1)S(1)} collective-permute-done((bf16[24,768]{1,0:T(8,128)(2,1)S(1)}, bf16[24,768]{1,0:T(8,128)(2,1)S(1)}, u32[]{:S(2)}, u32[]{:S(2)}) %collective-permute-start.3) | collective-permute-done | bytes 36896 | tf_op jit(solution)/shard_map/ppermute | solution.py:30
  28.6 3.1 %shard_map.149 = (bf16[10,512]{1,0:T(8,128)(2,1)S(1)}, bf16[8,256]{1,0:T(8,128)(2,1)S(1)}) custom-call(s32[2]{0:T(128)S(1)} %pad_add_fusion.refs_0_, bf16[48,768]{1,0:T(8,128)(2,1)S(1)} %pad_maximum_fusion.1.refs_1_, bf16[256,432]{1,0:T(8,128)(2,1)S(1)} %copy.57.refs_2_, bf16[256,2304]{1,0:T(8,128)(2,1)S(1)} %shard_map.148.refs_3_, ...), custom_call_target="tpu_custom_call" | custom-call | tf_op jit(solution)/shard_map/pallas_call | solution.py:275
  31.8 1.9 %collective-permute-start.4 = (bf16[24,1024]{1,0:T(8,128)(2,1)S(1)}, bf16[24,1024]{1,0:T(8,128)(2,1)S(1)}, u32[]{:S(2)}, u32[]{:S(2)}) collective-permute-start(bf16[24,1024]{1,0:T(8,128)(2,1)S(1)} %get-tuple-element.44), channel_id=1, source_target_pairs={{0,8},{4,12},{8,16},{12,20},{16,24},{20,28},{24,32},{28,36},{32,40... | collective-permute-start | bytes 147464 | tf_op jit(solution)/shard_map/ppermute | solution.py:20
  33.8 4.0 %collective-permute-start.5 = (bf16[24,2048]{1,0:T(8,128)(2,1)S(1)}, bf16[24,2048]{1,0:T(8,128)(2,1)S(1)}, u32[]{:S(2)}, u32[]{:S(2)}) collective-permute-start(bf16[24,2048]{1,0:T(8,128)(2,1)S(1)} %pad_maximum_fusion), channel_id=1, source_target_pairs={{0,4},{4,8},{8,12},{12,16},{16,20},{20,24},{24,28},{28,32},{32,36}... | collective-permute-start | bytes 294920 | tf_op jit(solution)/shard_map/ppermute | solution.py:20
  37.8 6.9 %collective-permute-start.6 = (bf16[24,2048]{1,0:T(8,128)(2,1)S(1)}, bf16[24,2048]{1,0:T(8,128)(2,1)S(1)}, u32[]{:S(2)}, u32[]{:S(2)}) collective-permute-start(bf16[24,2048]{1,0:T(8,128)(2,1)S(1)} %pad_maximum_fusion), channel_id=1, source_target_pairs={{4,0},{8,4},{12,8},{16,12},{20,16},{24,20},{28,24},{32,28},{36,32}... | collective-permute-start | bytes 294920 | tf_op jit(solution)/shard_map/ppermute | solution.py:20
  44.7 4.8 %collective-permute-start.7 = (bf16[24,1024]{1,0:T(8,128)(2,1)S(1)}, bf16[24,1024]{1,0:T(8,128)(2,1)S(1)}, u32[]{:S(2)}, u32[]{:S(2)}) collective-permute-start(bf16[24,1024]{1,0:T(8,128)(2,1)S(1)} %get-tuple-element.43), channel_id=1, source_target_pairs={{8,0},{12,4},{16,8},{20,12},{24,16},{28,20},{32,24},{36,28},{40,32... | collective-permute-start | bytes 147464 | tf_op jit(solution)/shard_map/ppermute | solution.py:20
  49.6 0.7 broadcast_in_dim.20
  50.3 7.2 %all-to-all-start = ((bf16[64,8,256]{2,1,0:T(8,128)(2,1)}), bf16[64,8,256]{2,1,0:T(8,128)(2,1)S(1)}, u32[]{:S(2)}, u32[]{:S(2)}) async-start(bf16[64,8,256]{2,1,0:T(8,128)(2,1)} %broadcast_in_dim.20), calls=%async_computation | async-start | bytes 524288 | tf_op jit(solution)/shard_map/all_to_all | solution.py:347
  59.9 0.8 shard_map.151.refs_8_
  62.4 5.9 %all-to-all-done = bf16[64,8,256]{2,1,0:T(8,128)(2,1)S(1)} async-done(((bf16[64,8,256]{2,1,0:T(8,128)(2,1)}), bf16[64,8,256]{2,1,0:T(8,128)(2,1)S(1)}, u32[]{:S(2)}, u32[]{:S(2)}) %all-to-all-start) | async-done | bytes 262176 | tf_op jit(solution)/shard_map/all_to_all | solution.py:347
  69.0 1.3 %collective-permute-done.8.refs_3_ = bf16[512,256]{1,0:T(8,128)(2,1)S(1)} collective-permute-done((bf16[512,256]{1,0:T(8,128)(2,1)S(1)}, bf16[512,256]{1,0:T(8,128)(2,1)S(1)}, u32[]{:S(2)}, u32[]{:S(2)}) %collective-permute-start.8) | collective-permute-done | bytes 262176 | tf_op jit(solution)/shard_map/ppermute | solution.py:30
  70.3 14.0 %shard_map.152 = (bf16[2,10,1024]{2,1,0:T(8,128)(2,1)S(1)}, bf16[128,128]{1,0:T(8,128)(2,1)}) custom-call(s32[2]{0:T(128)S(1)} %pad_add_fusion.refs_0_, s32[64,8]{1,0:T(8,128)S(1)} %bitcast.92, bf16[512,256]{1,0:T(8,128)(2,1)S(1)} %bitcast.90, bf16[512,256]{1,0:T(8,128)(2,1)S(1)} %collective-permute-done.8.refs_3_, bf16[512,512]{1,0:T(8,128)(2,1)S(1)} %shard_map.150.refs_4_, ...), custom_call_target="tpu_custom_call" | custom-call | tf_op jit(solution)/shard_map/pallas_call | solution.py:275
  84.3 6.3 %all-to-all-start.1 = ((bf16[64,2,128]{2,1,0:T(2,128)(2,1)}), bf16[64,2,128]{2,1,0:T(2,128)(2,1)S(1)}, u32[]{:S(2)}, u32[]{:S(2)}) async-start(bf16[64,2,128]{2,1,0:T(2,128)(2,1)} %bitcast.39), calls=%async_computation.1 | async-start | bytes 65536 | tf_op jit(solution)/shard_map/all_to_all | solution.py:413
  91.4 0.7 copy.69
  92.0 7.7 %all-to-all-done.1 = bf16[64,2,128]{2,1,0:T(2,128)(2,1)S(1)} async-done(((bf16[64,2,128]{2,1,0:T(2,128)(2,1)}), bf16[64,2,128]{2,1,0:T(2,128)(2,1)S(1)}, u32[]{:S(2)}, u32[]{:S(2)}) %all-to-all-start.1) | async-done | bytes 32800 | tf_op jit(solution)/shard_map/all_to_all | solution.py:413
  99.8 3.2 %shard_map.153 = f32[2,512]{1,0:T(2,128)} custom-call(bf16[128,128]{1,0:T(8,128)(2,1)S(1)} %bitcast.93, f32[128,512]{1,0:T(8,128)S(1)} %add_add_fusion.refs_1_), custom_call_target="tpu_custom_call" | custom-call | tf_op jit(solution)/shard_map/pallas_call | solution.py:275
  (104 shorter events, 9.7 us)
Async XLA Ops:
  0.6 10.6 %copy-start = (bf16[3,3,3,6,32]{4,3,2,1,0:T(8,128)(2,1)S(1)}, bf16[3,3,3,6,32]{4,3,2,1,0:T(8,128)(2,1)}, u32[]{:S(2)}) copy-start(bf16[3,3,3,6,32]{4,3,2,1,0:T(8,128)(2,1)} %param.18) | copy-start | bytes 31108
  3.1 12.0 %collective-permute-start = (bf16[12,2560]{1,0:T(8,128)(2,1)S(1)}, bf16[12,2560]{1,0:T(8,128)(2,1)S(1)}, u32[]{:S(2)}, u32[]{:S(2)}) collective-permute-start(bf16[12,2560]{1,0:T(8,128)(2,1)S(1)} %constant_dynamic-update-slice_fusion), channel_id=1, source_target_pairs={{0,2},{1,3},{2,0},{3,1},{4,6},{5,7},{6,4},{7,5},{8,10},{9,11},{10,... | collective-permute-start | bytes 184328 | tf_op jit(solution)/shard_map/ppermute | solution.py:30
  11.9 0.8 copy-start.5
  13.1 0.9 copy-start.1
  15.1 10.7 %collective-permute-start.1 = (bf16[24,96]{1,0:T(8,128)(2,1)S(1)}, bf16[24,96]{1,0:T(8,128)(2,1)S(1)}, u32[]{:S(2)}, u32[]{:S(2)}) collective-permute-start(bf16[24,96]{1,0:T(8,128)(2,1)S(1)} %get-tuple-element.41), channel_id=1, source_target_pairs={{0,4},{4,8},{8,12},{12,16},{16,20},{20,24},{24,28},{28,32},{32,36}... | collective-permute-start | bytes 13832 | tf_op jit(solution)/shard_map/ppermute | solution.py:20
  18.6 8.5 %collective-permute-start.2 = (bf16[24,96]{1,0:T(8,128)(2,1)S(1)}, bf16[24,96]{1,0:T(8,128)(2,1)S(1)}, u32[]{:S(2)}, u32[]{:S(2)}) collective-permute-start(bf16[24,96]{1,0:T(8,128)(2,1)S(1)} %get-tuple-element.42), channel_id=1, source_target_pairs={{4,0},{8,4},{12,8},{16,12},{20,16},{24,20},{28,24},{32,28},{36,32}... | collective-permute-start | bytes 13832 | tf_op jit(solution)/shard_map/ppermute | solution.py:20
  27.2 1.3 %collective-permute-start.3 = (bf16[24,768]{1,0:T(8,128)(2,1)S(1)}, bf16[24,768]{1,0:T(8,128)(2,1)S(1)}, u32[]{:S(2)}, u32[]{:S(2)}) collective-permute-start(bf16[24,768]{1,0:T(8,128)(2,1)S(1)} %pad_maximum_fusion.3), channel_id=1, source_target_pairs={{0,1},{1,0},{2,3},{3,2},{4,5},{5,4},{6,7},{7,6},{8,9},{9,8},{10,11... | collective-permute-start | bytes 110600 | tf_op jit(solution)/shard_map/ppermute | solution.py:30
  31.7 25.9 %copy-start.3 = (bf16[3,3,3,7,32]{4,3,2,1,0:T(8,128)(2,1)S(1)}, bf16[3,3,3,7,32]{4,3,2,1,0:T(8,128)(2,1)}, u32[]{:S(2)}) copy-start(bf16[3,3,3,7,32]{4,3,2,1,0:T(8,128)(2,1)} %param.21) | copy-start | bytes 36292
  31.8 25.7 %collective-permute-start.4 = (bf16[24,1024]{1,0:T(8,128)(2,1)S(1)}, bf16[24,1024]{1,0:T(8,128)(2,1)S(1)}, u32[]{:S(2)}, u32[]{:S(2)}) collective-permute-start(bf16[24,1024]{1,0:T(8,128)(2,1)S(1)} %get-tuple-element.44), channel_id=1, source_target_pairs={{0,8},{4,12},{8,16},{12,20},{16,24},{20,28},{24,32},{28,36},{32,40... | collective-permute-start | bytes 147464 | tf_op jit(solution)/shard_map/ppermute | solution.py:20
  33.8 23.7 %collective-permute-start.5 = (bf16[24,2048]{1,0:T(8,128)(2,1)S(1)}, bf16[24,2048]{1,0:T(8,128)(2,1)S(1)}, u32[]{:S(2)}, u32[]{:S(2)}) collective-permute-start(bf16[24,2048]{1,0:T(8,128)(2,1)S(1)} %pad_maximum_fusion), channel_id=1, source_target_pairs={{0,4},{4,8},{8,12},{12,16},{16,20},{20,24},{24,28},{28,32},{32,36}... | collective-permute-start | bytes 294920 | tf_op jit(solution)/shard_map/ppermute | solution.py:20
  37.8 19.7 %collective-permute-start.6 = (bf16[24,2048]{1,0:T(8,128)(2,1)S(1)}, bf16[24,2048]{1,0:T(8,128)(2,1)S(1)}, u32[]{:S(2)}, u32[]{:S(2)}) collective-permute-start(bf16[24,2048]{1,0:T(8,128)(2,1)S(1)} %pad_maximum_fusion), channel_id=1, source_target_pairs={{4,0},{8,4},{12,8},{16,12},{20,16},{24,20},{28,24},{32,28},{36,32}... | collective-permute-start | bytes 294920 | tf_op jit(solution)/shard_map/ppermute | solution.py:20
  44.7 12.8 %collective-permute-start.7 = (bf16[24,1024]{1,0:T(8,128)(2,1)S(1)}, bf16[24,1024]{1,0:T(8,128)(2,1)S(1)}, u32[]{:S(2)}, u32[]{:S(2)}) collective-permute-start(bf16[24,1024]{1,0:T(8,128)(2,1)S(1)} %get-tuple-element.43), channel_id=1, source_target_pairs={{8,0},{12,4},{16,8},{20,12},{24,16},{28,20},{32,24},{36,28},{40,32... | collective-permute-start | bytes 147464 | tf_op jit(solution)/shard_map/ppermute | solution.py:20
  50.3 17.9 %all-to-all-start = ((bf16[64,8,256]{2,1,0:T(8,128)(2,1)}), bf16[64,8,256]{2,1,0:T(8,128)(2,1)S(1)}, u32[]{:S(2)}, u32[]{:S(2)}) async-start(bf16[64,8,256]{2,1,0:T(8,128)(2,1)} %broadcast_in_dim.20), calls=%async_computation | async-start | bytes 524288 | tf_op jit(solution)/shard_map/all_to_all | solution.py:347
  58.4 1.0 copy-start.2
  59.3 1.7 %copy-start.7 = (bf16[3,3,3,32,5]{3,2,4,1,0:T(4,128)(2,1)S(1)}, bf16[3,3,3,32,5]{3,2,4,1,0:T(4,128)(2,1)}, u32[]{:S(2)}) copy-start(bf16[3,3,3,32,5]{3,2,4,1,0:T(4,128)(2,1)} %param.23) | copy-start | bytes 25924
  59.5 1.9 %copy-start.6 = (s32[64,128]{1,0:T(8,128)S(1)}, s32[64,128]{1,0:T(8,128)}, u32[]{:S(2)}) copy-start(s32[64,128]{1,0:T(8,128)} %param.17) | copy-start | bytes 98308
  60.8 8.2 %copy-start.4 = (bf16[5,2,2,1024]{3,2,1,0:T(2,128)(2,1)S(1)}, bf16[5,2,2,1024]{3,2,1,0:T(2,128)(2,1)}, u32[]{:S(2)}) copy-start(bf16[5,2,2,1024]{3,2,1,0:T(2,128)(2,1)} %param.15) | copy-start | bytes 122884
  68.2 2.1 %collective-permute-start.9 = (bf16[24,8192]{1,0:T(8,128)(2,1)S(1)}, bf16[24,8192]{1,0:T(8,128)(2,1)S(1)}, u32[]{:S(2)}, u32[]{:S(2)}) collective-permute-start(bf16[24,8192]{1,0:T(8,128)(2,1)S(1)} %constant_dynamic-update-slice_fusion.2.refs_5_), channel_id=1, source_target_pairs={{0,1},{1,0},{2,3},{3,2},{4,5},{5,4},{6,7},{7,6},{8,9},{9,8},{10,11... | collective-permute-start | bytes 1179656 | tf_op jit(solution)/shard_map/ppermute | solution.py:30
  68.2 2.1 %collective-permute-start.8 = (bf16[512,256]{1,0:T(8,128)(2,1)S(1)}, bf16[512,256]{1,0:T(8,128)(2,1)S(1)}, u32[]{:S(2)}, u32[]{:S(2)}) collective-permute-start(bf16[512,256]{1,0:T(8,128)(2,1)S(1)} %bitcast.89), channel_id=1, source_target_pairs={{0,1},{1,0},{2,3},{3,2},{4,5},{5,4},{6,7},{7,6},{8,9},{9,8},{10,11... | collective-permute-start | bytes 786440 | tf_op jit(solution)/shard_map/ppermute | solution.py:30
  84.3 15.4 %all-to-all-start.1 = ((bf16[64,2,128]{2,1,0:T(2,128)(2,1)}), bf16[64,2,128]{2,1,0:T(2,128)(2,1)S(1)}, u32[]{:S(2)}, u32[]{:S(2)}) async-start(bf16[64,2,128]{2,1,0:T(2,128)(2,1)} %bitcast.39), calls=%async_computation.1 | async-start | bytes 65536 | tf_op jit(solution)/shard_map/all_to_all | solution.py:413

commit v4 on v3

--- a/solution.py
+++ b/solution.py
@@ -23,6 +23,17 @@
 def band(zo, zi):
     d = jnp.arange(3, dtype=jnp.int32)
     return ((zi[None, :, None] - zo[:, None, None] + 1) == d[None, None, :]).astype(BF)
+
+
+def from_sides(value, distance):
+    wide, slab = lax.axis_size("wide"), lax.axis_size("slab")
+    pairs = []
+    for i in range(wide):
+        for j in range(slab):
+            to = i - distance if j % 2 else i + distance
+            if 0 <= to < wide:
+                pairs.append((i * slab + j, to * slab + j))
+    return lax.ppermute(value, ("wide", "slab"), pairs)
 
 
 def swapped(value, mask):
@@ -157,9 +168,9 @@
 
 
 def dual_kernel(tiles, angles, *refs):
-    (scal_ref, off_ref, g0_ref, g1_ref, t8_ref, xa_ref, xb_ref, w1_ref, w2_ref, w3_ref, ds_ref, out_ref, piece_ref) = refs[:13]
-    (win, x1, h1, h2, parts, nd, pc) = refs[13:20]
-    pj = refs[20:]
+    (scal_ref, off_ref, g0_ref, g1_ref, t8_ref, xo_ref, xa_ref, xb_ref, w1_ref, w2_ref, w3_ref, ds_ref, out_ref, piece_ref) = refs[:14]
+    (win, x1, h1, h2, parts, nd, pc) = refs[14:21]
+    pj = refs[21:]
     nb = x1.shape[2]
     blocks = nb // 128
     lane = lax.broadcasted_iota(jnp.int32, (8, 128), 1)
@@ -192,12 +203,19 @@
 
     lax.fori_loop(0, tiles, place, 0)
 
+    low_core = (scal_ref[1] & 1) == 0
     for a in range(8):
         valid = ((first_angle + a) >= 0) & ((first_angle + a) < angles)
         proj = jnp.concatenate([pj[a][b] for b in range(blocks)], axis=1) * (1.0 / math.sqrt(NY))
         proj = jnp.where(valid, proj, 0.0).astype(BF).astype(F32)
-        at = slice(a * nb, (a + 1) * nb)
-        known = jnp.concatenate([xa_ref[:, at].astype(F32), xb_ref[:, at].astype(F32)], axis=0)
+        if a in (3, 4):
+            known = xo_ref[:, (a - 3) * nb : (a - 2) * nb].astype(F32)
+        else:
+            at = {0: 2, 1: 0, 2: 1, 5: 0, 6: 1, 7: 2}[a] * nb
+            mine = xa_ref[:, at : at + nb].astype(F32)
+            theirs = xb_ref[:, at : at + nb].astype(F32)
+            theirs = jnp.concatenate([theirs[theirs.shape[0] // 2 :], theirs[: theirs.shape[0] // 2]], axis=0)
+            known = jnp.where(low_core, mine, theirs) if a < 3 else jnp.where(low_core, theirs, mine)
         x1[a] = jnp.concatenate(
             [before(known), known, after(known), before(proj), proj, after(proj), jnp.zeros((8, nb), F32)], axis=0
         ).astype(BF)
@@ -304,6 +322,7 @@
     both = jnp.concatenate([xp, xd], axis=1)
     both = jnp.concatenate([both, swapped(both, 2)], axis=0)
     xp, xd = both[:, :pix], both[:, pix:]
+    xd = jnp.concatenate([xd, swapped(xd, 1)], axis=0)
     edge = HALO * NY
     from_low = shifted("wide", 1, xp[:, pix - edge :])
     from_high = shifted("wide", -1, xp[:, :edge])
@@ -348,16 +367,8 @@
     gv = gv.reshape(wide_count * nz, pix // 2)
 
     xd, _ = lax.optimization_barrier((xd, lead))
-    xk = jnp.concatenate(
-        [
-            shifted("wide", 2, xd[:, nb:]),
-            shifted("wide", 1, xd),
-            xd,
-            shifted("wide", -1, xd),
-            shifted("wide", -2, xd[:, :nb]),
-        ],
-        axis=1,
-    )
+    end = jnp.where((s & 1) == 0, xd[:, nb:], xd[:, :nb])
+    xk = jnp.concatenate([from_sides(xd, 1), from_sides(end, 2)], axis=1)
     xk, dual_first, dual_second, dual_third, w, offsets = lax.optimization_barrier(
         (xk, dual_first, dual_second, dual_third, w, offsets)
     )
@@ -408,7 +419,7 @@
             pltpu.VMEM((wide_count * zl, 128), F32),
         ]
         + [pltpu.VMEM((blocks + 1, 8, 128), F32)] * 8,
-        (scal, off8, *gv, table8, *xk, dw1, dw2, dw3, ds), 2, mib=32,
+        (scal, off8, *gv, table8, xd, *xk, dw1, dw2, dw3, ds), 2, mib=32,
     )
     arrived = lax.all_to_all(
         pieces.reshape(wide_count, zl, 128), "wide", split_axis=0, concat_axis=0, tiled=True

time: 104 us -> 98.7 us (0.949)
  starting transfers between devices: 49.6 us -> 43.1 us
  waiting for transfers between devices: 17.4 us -> 18.5 us
    ppermute x6 -> x2, starting transfers between devices: 28.3 us -> 10.6 us  [shifted(): lax.ppermute(value, axis, [(i, i + delta) for i in range(size) if 0 <= i...]
    ppermute x0 -> x2, starting transfers between devices: none -> 6.54 us  [from_sides(): return lax.ppermute(value, ('wide', 'slab'), pairs)]
    all_to_all x1, starting transfers between devices: 7.19 us -> 11 us  [body(): gv = lax.all_to_all(sent, 'wide', split_axis=0, concat_axis=0, tiled=True)]
    all_to_all x1, waiting for transfers between devices: 5.86 us -> 7.69 us  [body(): gv = lax.all_to_all(sent, 'wide', split_axis=0, concat_axis=0, tiled=True)]
    ppermute x4 -> x5, waiting for transfers between devices: 2.49 us -> 1.77 us  [swapped(): return lax.ppermute(value, 'slab', [(i, i ^ mask) for i in range(size)])]
    ppermute x4 -> x5, starting transfers between devices: 7.88 us -> 8.46 us  [swapped(): return lax.ppermute(value, 'slab', [(i, i ^ mask) for i in range(size)])]
  transfers between devices with their start and end apart: 12 -> 11, of which waited for: 5 -> 5; matrix products, arithmetic and copies ran while one was open for 10% -> 11% of each run, Pallas kernels for 1% -> 4%
where the time goes in v4:
time: 98.7 us; the launch traced here: 97.6 us
  starting transfers between devices  43.1 us (44%)
  Pallas kernels  21.7 us (22%)
  waiting for transfers between devices  18.5 us (19%)
  local copies, waits for them, and re-layouts  6.89 us (7%)
  other arithmetic  4.37 us (4%)
  matrix products  1.83 us (2%)
  between operations  1.26 us (1%)
    pallas_call x6, Pallas kernels, call(): pl.pallas_call(kernel, out_shape=outs, in_specs=[sm] * smem + [vm] * (len...  21.7 us
    all_to_all x1, starting transfers between devices, body(): gv = lax.all_to_all(sent, 'wide', split_axis=0, concat_axis=0, tiled=True)  11 us
    ppermute x2, starting transfers between devices, shifted(): lax.ppermute(value, axis, [(i, i + delta) for i in range(size) if 0 <= i...  10.6 us
    ppermute x5, starting transfers between devices, swapped(): return lax.ppermute(value, 'slab', [(i, i ^ mask) for i in range(size)])  8.46 us
    all_to_all x1, waiting for transfers between devices, body(): lax.all_to_all(pieces.reshape(wide_count, zl, 128), 'wide', split_axis=0,...  7.74 us
    all_to_all x1, waiting for transfers between devices, body(): gv = lax.all_to_all(sent, 'wide', split_axis=0, concat_axis=0, tiled=True)  7.69 us
    ppermute x2, starting transfers between devices, from_sides(): return lax.ppermute(value, ('wide', 'slab'), pairs)  6.54 us
    all_to_all x1, starting transfers between devices, body(): lax.all_to_all(pieces.reshape(wide_count, zl, 128), 'wide', split_axis=0,...  6.48 us
  transfers between devices with their start and end apart: 11, of which 5 were waited for; matrix products, arithmetic and copies ran while one was open for 11% of the time, Pallas kernels for 4%

profile of v4, /device:TPU:2, one launch (start us, length us, event | category | flops | bytes accessed | tf_op | source)
XLA Modules:
  0.0 97.6 jit_solution(1118440154515602934)
XLA Ops:
  0.6 0.9 pad_maximum_fusion.4
  1.6 0.7 convert_bitcast_fusion
  2.3 0.7 pad_maximum_fusion.7
  3.1 7.3 %collective-permute-start = (bf16[12,2560]{1,0:T(8,128)(2,1)S(1)}, bf16[12,2560]{1,0:T(8,128)(2,1)S(1)}, u32[]{:S(2)}, u32[]{:S(2)}) collective-permute-start(bf16[12,2560]{1,0:T(8,128)(2,1)S(1)} %constant_dynamic-update-slice_fusion), channel_id=1, source_target_pairs={{0,2},{1,3},{2,0},{3,1},{4,6},{5,7},{6,4},{7,5},{8,10},{9,11},{10,... | collective-permute-start | bytes 184328 | tf_op jit(solution)/shard_map/ppermute | solution.py:41
  10.3 0.7 xor_multiply_fusion
  11.9 0.6 reshape_reshape.3
  13.3 0.6 reshape.411.refs_4_
  15.2 3.5 %collective-permute-start.1 = (bf16[24,96]{1,0:T(8,128)(2,1)S(1)}, bf16[24,96]{1,0:T(8,128)(2,1)S(1)}, u32[]{:S(2)}, u32[]{:S(2)}) collective-permute-start(bf16[24,96]{1,0:T(8,128)(2,1)S(1)} %get-tuple-element.41), channel_id=1, source_target_pairs={{0,4},{4,8},{8,12},{12,16},{16,20},{20,24},{24,28},{28,32},{32,36}... | collective-permute-start | bytes 13832 | tf_op jit(solution)/shard_map/ppermute | solution.py:20
  18.7 7.2 %collective-permute-start.2 = (bf16[24,96]{1,0:T(8,128)(2,1)S(1)}, bf16[24,96]{1,0:T(8,128)(2,1)S(1)}, u32[]{:S(2)}, u32[]{:S(2)}) collective-permute-start(bf16[24,96]{1,0:T(8,128)(2,1)S(1)} %get-tuple-element.42), channel_id=1, source_target_pairs={{4,0},{8,4},{12,8},{16,12},{20,16},{24,20},{28,24},{32,28},{36,32}... | collective-permute-start | bytes 13832 | tf_op jit(solution)/shard_map/ppermute | solution.py:20
  25.9 1.3 %collective-permute-done.2 = bf16[24,96]{1,0:T(8,128)(2,1)S(1)} collective-permute-done((bf16[24,96]{1,0:T(8,128)(2,1)S(1)}, bf16[24,96]{1,0:T(8,128)(2,1)S(1)}, u32[]{:S(2)}, u32[]{:S(2)}) %collective-permute-start.2) | collective-permute-done | bytes 4640 | tf_op jit(solution)/shard_map/ppermute | solution.py:20
  28.7 3.2 %shard_map.149 = (bf16[10,512]{1,0:T(8,128)(2,1)S(1)}, bf16[8,256]{1,0:T(8,128)(2,1)S(1)}) custom-call(s32[2]{0:T(128)S(1)} %pad_add_fusion.refs_0_, bf16[48,768]{1,0:T(8,128)(2,1)S(1)} %pad_maximum_fusion.3.refs_1_, bf16[256,432]{1,0:T(8,128)(2,1)S(1)} %copy.57.refs_2_, bf16[256,2304]{1,0:T(8,128)(2,1)S(1)} %shard_map.148.refs_3_, ...), custom_call_target="tpu_custom_call" | custom-call | tf_op jit(solution)/shard_map/pallas_call | solution.py:293
  31.9 1.9 %collective-permute-start.5 = (bf16[48,2048]{1,0:T(8,128)(2,1)S(1)}, bf16[48,2048]{1,0:T(8,128)(2,1)S(1)}, u32[]{:S(2)}, u32[]{:S(2)}) collective-permute-start(bf16[48,2048]{1,0:T(8,128)(2,1)S(1)} %pad_maximum_fusion.1.refs_5_), channel_id=1, source_target_pairs={{0,4},{2,6},{4,8},{5,1},{6,10},{7,3},{8,12},{9,5},{10,14},{11,7},{... | collective-permute-start | bytes 589832 | tf_op jit(solution)/shard_map/ppermute | solution.py:36
  33.9 4.6 %collective-permute-start.6 = (bf16[48,1024]{1,0:T(8,128)(2,1)S(1)}, bf16[48,1024]{1,0:T(8,128)(2,1)S(1)}, u32[]{:S(2)}, u32[]{:S(2)}) collective-permute-start(bf16[48,1024]{1,0:T(8,128)(2,1)S(1)} %slice_select_fusion), channel_id=1, source_target_pairs={{0,8},{2,10},{4,12},{6,14},{8,16},{9,1},{10,18},{11,3},{12,20},{13... | collective-permute-start | bytes 294920 | tf_op jit(solution)/shard_map/ppermute | solution.py:36
  38.5 0.7 broadcast_in_dim.20
  39.2 11.0 %all-to-all-start = ((bf16[64,8,256]{2,1,0:T(8,128)(2,1)}), bf16[64,8,256]{2,1,0:T(8,128)(2,1)S(1)}, u32[]{:S(2)}, u32[]{:S(2)}) async-start(bf16[64,8,256]{2,1,0:T(8,128)(2,1)} %broadcast_in_dim.20), calls=%async_computation | async-start | bytes 524288 | tf_op jit(solution)/shard_map/all_to_all | solution.py:366
  52.5 0.8 shard_map.151.refs_9_
  55.0 7.7 %all-to-all-done = bf16[64,8,256]{2,1,0:T(8,128)(2,1)S(1)} async-done(((bf16[64,8,256]{2,1,0:T(8,128)(2,1)}), bf16[64,8,256]{2,1,0:T(8,128)(2,1)S(1)}, u32[]{:S(2)}, u32[]{:S(2)}) %all-to-all-start) | async-done | bytes 262176 | tf_op jit(solution)/shard_map/all_to_all | solution.py:366
  63.5 1.2 %collective-permute-done.7.refs_3_ = bf16[512,256]{1,0:T(8,128)(2,1)S(1)} collective-permute-done((bf16[512,256]{1,0:T(8,128)(2,1)S(1)}, bf16[512,256]{1,0:T(8,128)(2,1)S(1)}, u32[]{:S(2)}, u32[]{:S(2)}) %collective-permute-start.7) | collective-permute-done | bytes 262176 | tf_op jit(solution)/shard_map/ppermute | solution.py:41
  64.7 14.2 %shard_map.152 = (bf16[2,10,1024]{2,1,0:T(8,128)(2,1)S(1)}, bf16[128,128]{1,0:T(8,128)(2,1)}) custom-call(s32[2]{0:T(128)S(1)} %pad_add_fusion.refs_0_, s32[64,8]{1,0:T(8,128)S(1)} %bitcast.92, bf16[512,256]{1,0:T(8,128)(2,1)S(1)} %bitcast.90, bf16[512,256]{1,0:T(8,128)(2,1)S(1)} %collective-permute-done.7.refs_3_, bf16[512,512]{1,0:T(8,128)(2,1)S(1)} %shard_map.150.refs_4_, ...), custom_call_target="tpu_custom_call" | custom-call | tf_op jit(solution)/shard_map/pallas_call | solution.py:293
  78.8 6.5 %all-to-all-start.1 = ((bf16[64,2,128]{2,1,0:T(2,128)(2,1)}), bf16[64,2,128]{2,1,0:T(2,128)(2,1)S(1)}, u32[]{:S(2)}, u32[]{:S(2)}) async-start(bf16[64,2,128]{2,1,0:T(2,128)(2,1)} %bitcast.39), calls=%async_computation.1 | async-start | bytes 65536 | tf_op jit(solution)/shard_map/all_to_all | solution.py:424
  85.4 0.6 reshape.412
  86.1 0.7 copy.69
  86.7 7.7 %all-to-all-done.1 = bf16[64,2,128]{2,1,0:T(2,128)(2,1)S(1)} async-done(((bf16[64,2,128]{2,1,0:T(2,128)(2,1)}), bf16[64,2,128]{2,1,0:T(2,128)(2,1)S(1)}, u32[]{:S(2)}, u32[]{:S(2)}) %all-to-all-start.1) | async-done | bytes 32800 | tf_op jit(solution)/shard_map/all_to_all | solution.py:424
  94.5 3.2 %shard_map.153 = f32[2,512]{1,0:T(2,128)} custom-call(bf16[128,128]{1,0:T(8,128)(2,1)S(1)} %bitcast.93, f32[128,512]{1,0:T(8,128)S(1)} %add_add_fusion.refs_1_), custom_call_target="tpu_custom_call" | custom-call | tf_op jit(solution)/shard_map/pallas_call | solution.py:293
  (99 shorter events, 9.1 us)
Async XLA Ops:
  0.6 10.6 %copy-start = (bf16[3,3,3,6,32]{4,3,2,1,0:T(8,128)(2,1)S(1)}, bf16[3,3,3,6,32]{4,3,2,1,0:T(8,128)(2,1)}, u32[]{:S(2)}) copy-start(bf16[3,3,3,6,32]{4,3,2,1,0:T(8,128)(2,1)} %param.18) | copy-start | bytes 31108
  3.1 12.1 %collective-permute-start = (bf16[12,2560]{1,0:T(8,128)(2,1)S(1)}, bf16[12,2560]{1,0:T(8,128)(2,1)S(1)}, u32[]{:S(2)}, u32[]{:S(2)}) collective-permute-start(bf16[12,2560]{1,0:T(8,128)(2,1)S(1)} %constant_dynamic-update-slice_fusion), channel_id=1, source_target_pairs={{0,2},{1,3},{2,0},{3,1},{4,6},{5,7},{6,4},{7,5},{8,10},{9,11},{10,... | collective-permute-start | bytes 184328 | tf_op jit(solution)/shard_map/ppermute | solution.py:41
  11.9 0.8 copy-start.5
  13.1 0.9 copy-start.1
  15.2 10.7 %collective-permute-start.1 = (bf16[24,96]{1,0:T(8,128)(2,1)S(1)}, bf16[24,96]{1,0:T(8,128)(2,1)S(1)}, u32[]{:S(2)}, u32[]{:S(2)}) collective-permute-start(bf16[24,96]{1,0:T(8,128)(2,1)S(1)} %get-tuple-element.41), channel_id=1, source_target_pairs={{0,4},{4,8},{8,12},{12,16},{16,20},{20,24},{24,28},{28,32},{32,36}... | collective-permute-start | bytes 13832 | tf_op jit(solution)/shard_map/ppermute | solution.py:20
  18.7 8.5 %collective-permute-start.2 = (bf16[24,96]{1,0:T(8,128)(2,1)S(1)}, bf16[24,96]{1,0:T(8,128)(2,1)S(1)}, u32[]{:S(2)}, u32[]{:S(2)}) collective-permute-start(bf16[24,96]{1,0:T(8,128)(2,1)S(1)} %get-tuple-element.42), channel_id=1, source_target_pairs={{4,0},{8,4},{12,8},{16,12},{20,16},{24,20},{28,24},{32,28},{36,32}... | collective-permute-start | bytes 13832 | tf_op jit(solution)/shard_map/ppermute | solution.py:20
  27.3 1.3 %collective-permute-start.3 = (bf16[24,768]{1,0:T(8,128)(2,1)S(1)}, bf16[24,768]{1,0:T(8,128)(2,1)S(1)}, u32[]{:S(2)}, u32[]{:S(2)}) collective-permute-start(bf16[24,768]{1,0:T(8,128)(2,1)S(1)} %pad_maximum_fusion.5), channel_id=1, source_target_pairs={{0,1},{1,0},{2,3},{3,2},{4,5},{5,4},{6,7},{7,6},{8,9},{9,8},{10,11... | collective-permute-start | bytes 110600 | tf_op jit(solution)/shard_map/ppermute | solution.py:41
  27.4 4.5 %collective-permute-start.4 = (bf16[24,2048]{1,0:T(8,128)(2,1)S(1)}, bf16[24,2048]{1,0:T(8,128)(2,1)S(1)}, u32[]{:S(2)}, u32[]{:S(2)}) collective-permute-start(bf16[24,2048]{1,0:T(8,128)(2,1)S(1)} %pad_maximum_fusion.2), channel_id=1, source_target_pairs={{0,1},{1,0},{2,3},{3,2},{4,5},{5,4},{6,7},{7,6},{8,9},{9,8},{10,11... | collective-permute-start | bytes 294920 | tf_op jit(solution)/shard_map/ppermute | solution.py:41
  31.9 18.4 %copy-start.3 = (bf16[3,3,3,7,32]{4,3,2,1,0:T(8,128)(2,1)S(1)}, bf16[3,3,3,7,32]{4,3,2,1,0:T(8,128)(2,1)}, u32[]{:S(2)}) copy-start(bf16[3,3,3,7,32]{4,3,2,1,0:T(8,128)(2,1)} %param.21) | copy-start | bytes 36292
  31.9 18.3 %collective-permute-start.5 = (bf16[48,2048]{1,0:T(8,128)(2,1)S(1)}, bf16[48,2048]{1,0:T(8,128)(2,1)S(1)}, u32[]{:S(2)}, u32[]{:S(2)}) collective-permute-start(bf16[48,2048]{1,0:T(8,128)(2,1)S(1)} %pad_maximum_fusion.1.refs_5_), channel_id=1, source_target_pairs={{0,4},{2,6},{4,8},{5,1},{6,10},{7,3},{8,12},{9,5},{10,14},{11,7},{... | collective-permute-start | bytes 589832 | tf_op jit(solution)/shard_map/ppermute | solution.py:36
  33.9 16.3 %collective-permute-start.6 = (bf16[48,1024]{1,0:T(8,128)(2,1)S(1)}, bf16[48,1024]{1,0:T(8,128)(2,1)S(1)}, u32[]{:S(2)}, u32[]{:S(2)}) collective-permute-start(bf16[48,1024]{1,0:T(8,128)(2,1)S(1)} %slice_select_fusion), channel_id=1, source_target_pairs={{0,8},{2,10},{4,12},{6,14},{8,16},{9,1},{10,18},{11,3},{12,20},{13... | collective-permute-start | bytes 294920 | tf_op jit(solution)/shard_map/ppermute | solution.py:36
  39.2 23.5 %all-to-all-start = ((bf16[64,8,256]{2,1,0:T(8,128)(2,1)}), bf16[64,8,256]{2,1,0:T(8,128)(2,1)S(1)}, u32[]{:S(2)}, u32[]{:S(2)}) async-start(bf16[64,8,256]{2,1,0:T(8,128)(2,1)} %broadcast_in_dim.20), calls=%async_computation | async-start | bytes 524288 | tf_op jit(solution)/shard_map/all_to_all | solution.py:366
  51.1 1.0 %copy-start.2 = (bf16[3,3,3,32,32]{4,3,2,1,0:T(8,128)(2,1)S(1)}, bf16[3,3,3,32,32]{4,3,2,1,0:T(8,128)(2,1)}, u32[]{:S(2)}) copy-start(bf16[3,3,3,32,32]{4,3,2,1,0:T(8,128)(2,1)} %param.22) | copy-start | bytes 165892
  52.0 1.7 %copy-start.7 = (bf16[3,3,3,32,5]{3,2,4,1,0:T(4,128)(2,1)S(1)}, bf16[3,3,3,32,5]{3,2,4,1,0:T(4,128)(2,1)}, u32[]{:S(2)}) copy-start(bf16[3,3,3,32,5]{3,2,4,1,0:T(4,128)(2,1)} %param.23) | copy-start | bytes 25924
  52.1 1.9 %copy-start.6 = (s32[64,128]{1,0:T(8,128)S(1)}, s32[64,128]{1,0:T(8,128)}, u32[]{:S(2)}) copy-start(s32[64,128]{1,0:T(8,128)} %param.17) | copy-start | bytes 98308
  53.4 10.0 %copy-start.4 = (bf16[5,2,2,1024]{3,2,1,0:T(2,128)(2,1)S(1)}, bf16[5,2,2,1024]{3,2,1,0:T(2,128)(2,1)}, u32[]{:S(2)}) copy-start(bf16[5,2,2,1024]{3,2,1,0:T(2,128)(2,1)} %param.15) | copy-start | bytes 122884
  62.7 2.0 %collective-permute-start.8 = (bf16[48,3072]{1,0:T(8,128)(2,1)S(1)}, bf16[48,3072]{1,0:T(8,128)(2,1)S(1)}, u32[]{:S(2)}, u32[]{:S(2)}) collective-permute-start(bf16[48,3072]{1,0:T(8,128)(2,1)S(1)} %pad_maximum_fusion.refs_6_), channel_id=1, source_target_pairs={{0,1},{1,0},{2,3},{3,2},{4,5},{5,4},{6,7},{7,6},{8,9},{9,8},{10,11... | collective-permute-start | bytes 884744 | tf_op jit(solution)/shard_map/ppermute | solution.py:41
  62.8 1.8 %collective-permute-start.7 = (bf16[512,256]{1,0:T(8,128)(2,1)S(1)}, bf16[512,256]{1,0:T(8,128)(2,1)S(1)}, u32[]{:S(2)}, u32[]{:S(2)}) collective-permute-start(bf16[512,256]{1,0:T(8,128)(2,1)S(1)} %bitcast.89), channel_id=1, source_target_pairs={{0,1},{1,0},{2,3},{3,2},{4,5},{5,4},{6,7},{7,6},{8,9},{9,8},{10,11... | collective-permute-start | bytes 786440 | tf_op jit(solution)/shard_map/ppermute | solution.py:41
  78.8 15.6 %all-to-all-start.1 = ((bf16[64,2,128]{2,1,0:T(2,128)(2,1)}), bf16[64,2,128]{2,1,0:T(2,128)(2,1)S(1)}, u32[]{:S(2)}, u32[]{:S(2)}) async-start(bf16[64,2,128]{2,1,0:T(2,128)(2,1)} %bitcast.39), calls=%async_computation.1 | async-start | bytes 65536 | tf_op jit(solution)/shard_map/all_to_all | solution.py:424

commit v5 on v4

--- a/solution.py
+++ b/solution.py
@@ -153,7 +153,9 @@
     lead = jnp.concatenate([total[i * per : i * per + 2] for i in range(4)], axis=0)
     lead = jnp.where((scal_ref[1] & 1) == 0, lead, pltpu.roll(lead, 4, 0))
     half = TX * NY // 2
-    lead_ref[...] = jnp.where((scal_ref[1] & 1) == 0, lead[:, :half], lead[:, half:]).astype(BF)
+    lead = jnp.where((scal_ref[1] & 1) == 0, lead[:, :half], lead[:, half:]).astype(BF)
+    for tile in range(lead_ref.shape[0]):
+        lead_ref[tile] = lead
     own_ref[...] = total[: own_ref.shape[0]].astype(BF)
 
 
@@ -201,7 +203,7 @@
             pj[a][q + 1] = hi
         return 0
 
-    lax.fori_loop(0, tiles, place, 0)
+    lax.fori_loop(0, tiles, place, 0, unroll=4)
 
     low_core = (scal_ref[1] & 1) == 0
     for a in range(8):
@@ -266,7 +268,7 @@
         pc[pl.ds(pl.multiple_of(g * 8, 8), 8), :] = full
         return 0
 
-    lax.fori_loop(0, tiles // 4, cut, 0)
+    lax.fori_loop(0, tiles // 4, cut, 0, unroll=4)
     piece_ref[...] = pc[...].astype(BF)
 
 
@@ -354,7 +356,7 @@
     )
     own, lead = call(
         lambda *refs: primal_kernel(wide_count * TX, *refs),
-        [jax.ShapeDtypeStruct((mem * zl, pix), BF), jax.ShapeDtypeStruct((nz, pix // 2), BF)],
+        [jax.ShapeDtypeStruct((mem * zl, pix), BF), jax.ShapeDtypeStruct((wide_count, nz, pix // 2), BF)],
         [
             pltpu.VMEM((9 * xg.shape[0], xg.shape[1]), BF),
             pltpu.VMEM((9 * nz * hid, xg.shape[1]), BF),
@@ -362,8 +364,7 @@
         (scal, xg, pw1, pw2, pw3), 1,
     )
 
-    sent = jnp.broadcast_to(lead[None], (wide_count, nz, pix // 2))
-    gv = lax.all_to_all(sent, "wide", split_axis=0, concat_axis=0, tiled=True)
+    gv = lax.all_to_all(lead, "wide", split_axis=0, concat_axis=0, tiled=True)
     gv = gv.reshape(wide_count * nz, pix // 2)
 
     xd, _ = lax.optimization_barrier((xd, lead))

time: 98.7 us -> 94.8 us (0.960)
  Pallas kernels: 21.7 us -> 18.5 us
    pallas_call x6, Pallas kernels: 21.7 us -> 18.5 us  [call(): pl.pallas_call(kernel, out_shape=outs, in_specs=[sm] * smem + [vm] * (len...]
  transfers between devices with their start and end apart: 11 -> 11, of which waited for: 5 -> 5; matrix products, arithmetic and copies ran while one was open for 11% -> 10% of each run, Pallas kernels for 4% -> 5%
where the time goes in v5:
time: 94.8 us; the launch traced here: 93.7 us
  starting transfers between devices  43.1 us (45%)
  Pallas kernels  18.5 us (20%)
  waiting for transfers between devices  18.5 us (20%)
  local copies, waits for them, and re-layouts  6.16 us (6%)
  other arithmetic  4.37 us (5%)
  matrix products  1.83 us (2%)
  between operations  1.24 us (1%)
    pallas_call x6, Pallas kernels, call(): pl.pallas_call(kernel, out_shape=outs, in_specs=[sm] * smem + [vm] * (len...  18.5 us
    all_to_all x1, starting transfers between devices, body(): gv = lax.all_to_all(lead, 'wide', split_axis=0, concat_axis=0, tiled=True)  11 us
    ppermute x2, starting transfers between devices, shifted(): lax.ppermute(value, axis, [(i, i + delta) for i in range(size) if 0 <= i...  10.6 us
    ppermute x5, starting transfers between devices, swapped(): return lax.ppermute(value, 'slab', [(i, i ^ mask) for i in range(size)])  8.46 us
    all_to_all x1, waiting for transfers between devices, body(): lax.all_to_all(pieces.reshape(wide_count, zl, 128), 'wide', split_axis=0,...  7.74 us
    all_to_all x1, waiting for transfers between devices, body(): gv = lax.all_to_all(lead, 'wide', split_axis=0, concat_axis=0, tiled=True)  7.69 us
    ppermute x2, starting transfers between devices, from_sides(): return lax.ppermute(value, ('wide', 'slab'), pairs)  6.53 us
    all_to_all x1, starting transfers between devices, body(): lax.all_to_all(pieces.reshape(wide_count, zl, 128), 'wide', split_axis=0,...  6.47 us
  transfers between devices with their start and end apart: 11, of which 5 were waited for; matrix products, arithmetic and copies ran while one was open for 10% of the time, Pallas kernels for 5%

profile of v5, /device:TPU:2, one launch (start us, length us, event | category | flops | bytes accessed | tf_op | source)
XLA Modules:
  0.0 93.7 jit_solution(4617939455683577047)
XLA Ops:
  0.6 0.9 pad_maximum_fusion.4
  1.6 0.7 convert_bitcast_fusion
  2.3 0.7 pad_maximum_fusion.7
  3.1 7.3 %collective-permute-start = (bf16[12,2560]{1,0:T(8,128)(2,1)S(1)}, bf16[12,2560]{1,0:T(8,128)(2,1)S(1)}, u32[]{:S(2)}, u32[]{:S(2)}) collective-permute-start(bf16[12,2560]{1,0:T(8,128)(2,1)S(1)} %constant_dynamic-update-slice_fusion), channel_id=1, source_target_pairs={{0,2},{1,3},{2,0},{3,1},{4,6},{5,7},{6,4},{7,5},{8,10},{9,11},{10,... | collective-permute-start | bytes 184328 | tf_op jit(solution)/shard_map/ppermute | solution.py:41
  10.3 0.7 xor_multiply_fusion
  11.9 0.6 reshape_reshape.3
  13.3 0.6 reshape.410.refs_4_
  15.2 3.5 %collective-permute-start.1 = (bf16[24,96]{1,0:T(8,128)(2,1)S(1)}, bf16[24,96]{1,0:T(8,128)(2,1)S(1)}, u32[]{:S(2)}, u32[]{:S(2)}) collective-permute-start(bf16[24,96]{1,0:T(8,128)(2,1)S(1)} %get-tuple-element.41), channel_id=1, source_target_pairs={{0,4},{4,8},{8,12},{12,16},{16,20},{20,24},{24,28},{28,32},{32,36}... | collective-permute-start | bytes 13832 | tf_op jit(solution)/shard_map/ppermute | solution.py:20
  18.7 7.2 %collective-permute-start.2 = (bf16[24,96]{1,0:T(8,128)(2,1)S(1)}, bf16[24,96]{1,0:T(8,128)(2,1)S(1)}, u32[]{:S(2)}, u32[]{:S(2)}) collective-permute-start(bf16[24,96]{1,0:T(8,128)(2,1)S(1)} %get-tuple-element.42), channel_id=1, source_target_pairs={{4,0},{8,4},{12,8},{16,12},{20,16},{24,20},{28,24},{32,28},{36,32}... | collective-permute-start | bytes 13832 | tf_op jit(solution)/shard_map/ppermute | solution.py:20
  25.9 1.3 %collective-permute-done.2 = bf16[24,96]{1,0:T(8,128)(2,1)S(1)} collective-permute-done((bf16[24,96]{1,0:T(8,128)(2,1)S(1)}, bf16[24,96]{1,0:T(8,128)(2,1)S(1)}, u32[]{:S(2)}, u32[]{:S(2)}) %collective-permute-start.2) | collective-permute-done | bytes 4640 | tf_op jit(solution)/shard_map/ppermute | solution.py:20
  28.0 0.6 collective-permute-done.3
  28.7 3.9 %shard_map.149 = (bf16[10,512]{1,0:T(8,128)(2,1)S(1)}, bf16[64,8,256]{2,1,0:T(8,128)(2,1)}) custom-call(s32[2]{0:T(128)S(1)} %pad_add_fusion.refs_0_, bf16[48,768]{1,0:T(8,128)(2,1)S(1)} %pad_maximum_fusion.3.refs_1_, bf16[256,432]{1,0:T(8,128)(2,1)S(1)} %copy.57.refs_2_, bf16[256,2304]{1,0:T(8,128)(2,1)S(1)} %shard_map.148.refs_3_, ...), custom_call_target="tpu_custom_call" | custom-call | tf_op jit(solution)/shard_map/pallas_call | solution.py:295
  32.6 1.9 %collective-permute-start.5 = (bf16[48,2048]{1,0:T(8,128)(2,1)S(1)}, bf16[48,2048]{1,0:T(8,128)(2,1)S(1)}, u32[]{:S(2)}, u32[]{:S(2)}) collective-permute-start(bf16[48,2048]{1,0:T(8,128)(2,1)S(1)} %pad_maximum_fusion.1.refs_5_), channel_id=1, source_target_pairs={{0,4},{2,6},{4,8},{5,1},{6,10},{7,3},{8,12},{9,5},{10,14},{11,7},{... | collective-permute-start | bytes 589832 | tf_op jit(solution)/shard_map/ppermute | solution.py:36
  34.6 4.6 %collective-permute-start.6 = (bf16[48,1024]{1,0:T(8,128)(2,1)S(1)}, bf16[48,1024]{1,0:T(8,128)(2,1)S(1)}, u32[]{:S(2)}, u32[]{:S(2)}) collective-permute-start(bf16[48,1024]{1,0:T(8,128)(2,1)S(1)} %slice_select_fusion), channel_id=1, source_target_pairs={{0,8},{2,10},{4,12},{6,14},{8,16},{9,1},{10,18},{11,3},{12,20},{13... | collective-permute-start | bytes 294920 | tf_op jit(solution)/shard_map/ppermute | solution.py:36
  39.2 11.0 %all-to-all-start = ((bf16[64,8,256]{2,1,0:T(8,128)(2,1)}), bf16[64,8,256]{2,1,0:T(8,128)(2,1)S(1)}, u32[]{:S(2)}, u32[]{:S(2)}) async-start(bf16[64,8,256]{2,1,0:T(8,128)(2,1)} %get-tuple-element.23), calls=%async_computation | async-start | bytes 524288 | tf_op jit(solution)/shard_map/all_to_all | solution.py:367
  52.5 0.8 shard_map.151.refs_9_
  55.0 7.7 %all-to-all-done = bf16[64,8,256]{2,1,0:T(8,128)(2,1)S(1)} async-done(((bf16[64,8,256]{2,1,0:T(8,128)(2,1)}), bf16[64,8,256]{2,1,0:T(8,128)(2,1)S(1)}, u32[]{:S(2)}, u32[]{:S(2)}) %all-to-all-start) | async-done | bytes 262176 | tf_op jit(solution)/shard_map/all_to_all | solution.py:367
  63.5 1.2 %collective-permute-done.7.refs_3_ = bf16[512,256]{1,0:T(8,128)(2,1)S(1)} collective-permute-done((bf16[512,256]{1,0:T(8,128)(2,1)S(1)}, bf16[512,256]{1,0:T(8,128)(2,1)S(1)}, u32[]{:S(2)}, u32[]{:S(2)}) %collective-permute-start.7) | collective-permute-done | bytes 262176 | tf_op jit(solution)/shard_map/ppermute | solution.py:41
  64.6 10.3 %shard_map.152 = (bf16[2,10,1024]{2,1,0:T(8,128)(2,1)S(1)}, bf16[128,128]{1,0:T(8,128)(2,1)}) custom-call(s32[2]{0:T(128)S(1)} %pad_add_fusion.refs_0_, s32[64,8]{1,0:T(8,128)S(1)} %bitcast.92, bf16[512,256]{1,0:T(8,128)(2,1)S(1)} %bitcast.90, bf16[512,256]{1,0:T(8,128)(2,1)S(1)} %collective-permute-done.7.refs_3_, bf16[512,512]{1,0:T(8,128)(2,1)S(1)} %shard_map.150.refs_4_, ...), custom_call_target="tpu_custom_call" | custom-call | tf_op jit(solution)/shard_map/pallas_call | solution.py:295
  74.9 6.5 %all-to-all-start.1 = ((bf16[64,2,128]{2,1,0:T(2,128)(2,1)}), bf16[64,2,128]{2,1,0:T(2,128)(2,1)S(1)}, u32[]{:S(2)}, u32[]{:S(2)}) async-start(bf16[64,2,128]{2,1,0:T(2,128)(2,1)} %bitcast.39), calls=%async_computation.1 | async-start | bytes 65536 | tf_op jit(solution)/shard_map/all_to_all | solution.py:425
  81.5 0.6 reshape.411
  82.2 0.7 copy.69
  82.8 7.7 %all-to-all-done.1 = bf16[64,2,128]{2,1,0:T(2,128)(2,1)S(1)} async-done(((bf16[64,2,128]{2,1,0:T(2,128)(2,1)}), bf16[64,2,128]{2,1,0:T(2,128)(2,1)S(1)}, u32[]{:S(2)}, u32[]{:S(2)}) %all-to-all-start.1) | async-done | bytes 32800 | tf_op jit(solution)/shard_map/all_to_all | solution.py:425
  90.6 3.2 %shard_map.153 = f32[2,512]{1,0:T(2,128)} custom-call(bf16[128,128]{1,0:T(8,128)(2,1)S(1)} %bitcast.93, f32[128,512]{1,0:T(8,128)S(1)} %add_add_fusion.refs_1_), custom_call_target="tpu_custom_call" | custom-call | tf_op jit(solution)/shard_map/pallas_call | solution.py:295
  (98 shorter events, 8.5 us)
Async XLA Ops:
  0.6 10.6 %copy-start = (bf16[3,3,3,6,32]{4,3,2,1,0:T(8,128)(2,1)S(1)}, bf16[3,3,3,6,32]{4,3,2,1,0:T(8,128)(2,1)}, u32[]{:S(2)}) copy-start(bf16[3,3,3,6,32]{4,3,2,1,0:T(8,128)(2,1)} %param.18) | copy-start | bytes 31108
  3.1 12.1 %collective-permute-start = (bf16[12,2560]{1,0:T(8,128)(2,1)S(1)}, bf16[12,2560]{1,0:T(8,128)(2,1)S(1)}, u32[]{:S(2)}, u32[]{:S(2)}) collective-permute-start(bf16[12,2560]{1,0:T(8,128)(2,1)S(1)} %constant_dynamic-update-slice_fusion), channel_id=1, source_target_pairs={{0,2},{1,3},{2,0},{3,1},{4,6},{5,7},{6,4},{7,5},{8,10},{9,11},{10,... | collective-permute-start | bytes 184328 | tf_op jit(solution)/shard_map/ppermute | solution.py:41
  11.9 0.8 copy-start.5
  13.1 0.9 %copy-start.1 = (bf16[3,3,3,32,32]{4,3,2,1,0:T(8,128)(2,1)S(1)}, bf16[3,3,3,32,32]{4,3,2,1,0:T(8,128)(2,1)}, u32[]{:S(2)}) copy-start(bf16[3,3,3,32,32]{4,3,2,1,0:T(8,128)(2,1)} %param.19) | copy-start | bytes 165892
  15.2 10.7 %collective-permute-start.1 = (bf16[24,96]{1,0:T(8,128)(2,1)S(1)}, bf16[24,96]{1,0:T(8,128)(2,1)S(1)}, u32[]{:S(2)}, u32[]{:S(2)}) collective-permute-start(bf16[24,96]{1,0:T(8,128)(2,1)S(1)} %get-tuple-element.41), channel_id=1, source_target_pairs={{0,4},{4,8},{8,12},{12,16},{16,20},{20,24},{24,28},{28,32},{32,36}... | collective-permute-start | bytes 13832 | tf_op jit(solution)/shard_map/ppermute | solution.py:20
  18.7 8.5 %collective-permute-start.2 = (bf16[24,96]{1,0:T(8,128)(2,1)S(1)}, bf16[24,96]{1,0:T(8,128)(2,1)S(1)}, u32[]{:S(2)}, u32[]{:S(2)}) collective-permute-start(bf16[24,96]{1,0:T(8,128)(2,1)S(1)} %get-tuple-element.42), channel_id=1, source_target_pairs={{4,0},{8,4},{12,8},{16,12},{20,16},{24,20},{28,24},{32,28},{36,32}... | collective-permute-start | bytes 13832 | tf_op jit(solution)/shard_map/ppermute | solution.py:20
  27.3 1.3 %collective-permute-start.3 = (bf16[24,768]{1,0:T(8,128)(2,1)S(1)}, bf16[24,768]{1,0:T(8,128)(2,1)S(1)}, u32[]{:S(2)}, u32[]{:S(2)}) collective-permute-start(bf16[24,768]{1,0:T(8,128)(2,1)S(1)} %pad_maximum_fusion.5), channel_id=1, source_target_pairs={{0,1},{1,0},{2,3},{3,2},{4,5},{5,4},{6,7},{7,6},{8,9},{9,8},{10,11... | collective-permute-start | bytes 110600 | tf_op jit(solution)/shard_map/ppermute | solution.py:41
  27.4 5.2 %collective-permute-start.4 = (bf16[24,2048]{1,0:T(8,128)(2,1)S(1)}, bf16[24,2048]{1,0:T(8,128)(2,1)S(1)}, u32[]{:S(2)}, u32[]{:S(2)}) collective-permute-start(bf16[24,2048]{1,0:T(8,128)(2,1)S(1)} %pad_maximum_fusion.2), channel_id=1, source_target_pairs={{0,1},{1,0},{2,3},{3,2},{4,5},{5,4},{6,7},{7,6},{8,9},{9,8},{10,11... | collective-permute-start | bytes 294920 | tf_op jit(solution)/shard_map/ppermute | solution.py:41
  32.6 17.7 %copy-start.3 = (bf16[3,3,3,7,32]{4,3,2,1,0:T(8,128)(2,1)S(1)}, bf16[3,3,3,7,32]{4,3,2,1,0:T(8,128)(2,1)}, u32[]{:S(2)}) copy-start(bf16[3,3,3,7,32]{4,3,2,1,0:T(8,128)(2,1)} %param.21) | copy-start | bytes 36292
  32.6 17.6 %collective-permute-start.5 = (bf16[48,2048]{1,0:T(8,128)(2,1)S(1)}, bf16[48,2048]{1,0:T(8,128)(2,1)S(1)}, u32[]{:S(2)}, u32[]{:S(2)}) collective-permute-start(bf16[48,2048]{1,0:T(8,128)(2,1)S(1)} %pad_maximum_fusion.1.refs_5_), channel_id=1, source_target_pairs={{0,4},{2,6},{4,8},{5,1},{6,10},{7,3},{8,12},{9,5},{10,14},{11,7},{... | collective-permute-start | bytes 589832 | tf_op jit(solution)/shard_map/ppermute | solution.py:36
  34.6 15.6 %collective-permute-start.6 = (bf16[48,1024]{1,0:T(8,128)(2,1)S(1)}, bf16[48,1024]{1,0:T(8,128)(2,1)S(1)}, u32[]{:S(2)}, u32[]{:S(2)}) collective-permute-start(bf16[48,1024]{1,0:T(8,128)(2,1)S(1)} %slice_select_fusion), channel_id=1, source_target_pairs={{0,8},{2,10},{4,12},{6,14},{8,16},{9,1},{10,18},{11,3},{12,20},{13... | collective-permute-start | bytes 294920 | tf_op jit(solution)/shard_map/ppermute | solution.py:36
  39.2 23.5 %all-to-all-start = ((bf16[64,8,256]{2,1,0:T(8,128)(2,1)}), bf16[64,8,256]{2,1,0:T(8,128)(2,1)S(1)}, u32[]{:S(2)}, u32[]{:S(2)}) async-start(bf16[64,8,256]{2,1,0:T(8,128)(2,1)} %get-tuple-element.23), calls=%async_computation | async-start | bytes 524288 | tf_op jit(solution)/shard_map/all_to_all | solution.py:367
  51.1 1.0 %copy-start.2 = (bf16[3,3,3,32,32]{4,3,2,1,0:T(8,128)(2,1)S(1)}, bf16[3,3,3,32,32]{4,3,2,1,0:T(8,128)(2,1)}, u32[]{:S(2)}) copy-start(bf16[3,3,3,32,32]{4,3,2,1,0:T(8,128)(2,1)} %param.22) | copy-start | bytes 165892
  51.9 1.7 %copy-start.7 = (bf16[3,3,3,32,5]{3,2,4,1,0:T(4,128)(2,1)S(1)}, bf16[3,3,3,32,5]{3,2,4,1,0:T(4,128)(2,1)}, u32[]{:S(2)}) copy-start(bf16[3,3,3,32,5]{3,2,4,1,0:T(4,128)(2,1)} %param.23) | copy-start | bytes 25924
  52.1 1.9 %copy-start.6 = (s32[64,128]{1,0:T(8,128)S(1)}, s32[64,128]{1,0:T(8,128)}, u32[]{:S(2)}) copy-start(s32[64,128]{1,0:T(8,128)} %param.17) | copy-start | bytes 98308
  53.4 10.0 %copy-start.4 = (bf16[5,2,2,1024]{3,2,1,0:T(2,128)(2,1)S(1)}, bf16[5,2,2,1024]{3,2,1,0:T(2,128)(2,1)}, u32[]{:S(2)}) copy-start(bf16[5,2,2,1024]{3,2,1,0:T(2,128)(2,1)} %param.15) | copy-start | bytes 122884
  62.7 2.0 %collective-permute-start.8 = (bf16[48,3072]{1,0:T(8,128)(2,1)S(1)}, bf16[48,3072]{1,0:T(8,128)(2,1)S(1)}, u32[]{:S(2)}, u32[]{:S(2)}) collective-permute-start(bf16[48,3072]{1,0:T(8,128)(2,1)S(1)} %pad_maximum_fusion.refs_6_), channel_id=1, source_target_pairs={{0,1},{1,0},{2,3},{3,2},{4,5},{5,4},{6,7},{7,6},{8,9},{9,8},{10,11... | collective-permute-start | bytes 884744 | tf_op jit(solution)/shard_map/ppermute | solution.py:41
  62.8 1.8 %collective-permute-start.7 = (bf16[512,256]{1,0:T(8,128)(2,1)S(1)}, bf16[512,256]{1,0:T(8,128)(2,1)S(1)}, u32[]{:S(2)}, u32[]{:S(2)}) collective-permute-start(bf16[512,256]{1,0:T(8,128)(2,1)S(1)} %bitcast.89), channel_id=1, source_target_pairs={{0,1},{1,0},{2,3},{3,2},{4,5},{5,4},{6,7},{7,6},{8,9},{9,8},{10,11... | collective-permute-start | bytes 786440 | tf_op jit(solution)/shard_map/ppermute | solution.py:41
  74.9 15.6 %all-to-all-start.1 = ((bf16[64,2,128]{2,1,0:T(2,128)(2,1)}), bf16[64,2,128]{2,1,0:T(2,128)(2,1)S(1)}, u32[]{:S(2)}, u32[]{:S(2)}) async-start(bf16[64,2,128]{2,1,0:T(2,128)(2,1)} %bitcast.39), calls=%async_computation.1 | async-start | bytes 65536 | tf_op jit(solution)/shard_map/all_to_all | solution.py:425

commit v6 on v5

--- a/solution.py
+++ b/solution.py
@@ -203,7 +203,7 @@
             pj[a][q + 1] = hi
         return 0
 
-    lax.fori_loop(0, tiles, place, 0, unroll=4)
+    lax.fori_loop(0, tiles, place, 0, unroll=8)
 
     low_core = (scal_ref[1] & 1) == 0
     for a in range(8):
@@ -268,7 +268,7 @@
         pc[pl.ds(pl.multiple_of(g * 8, 8), 8), :] = full
         return 0
 
-    lax.fori_loop(0, tiles // 4, cut, 0, unroll=4)
+    lax.fori_loop(0, tiles // 4, cut, 0, unroll=8)
     piece_ref[...] = pc[...].astype(BF)
 
 

time: 94.8 us -> 94.7 us (level)
  no operation moved by 1% of the time
where the time goes in v6:
time: 94.7 us; the launch traced here: 93.7 us
  starting transfers between devices  43.1 us (46%)
  Pallas kernels  18.5 us (20%)
  waiting for transfers between devices  18.5 us (20%)
  local copies, waits for them, and re-layouts  6.16 us (7%)
  other arithmetic  4.37 us (5%)
  matrix products  1.83 us (2%)
  between operations  1.24 us (1%)
    pallas_call x6, Pallas kernels, call(): pl.pallas_call(kernel, out_shape=outs, in_specs=[sm] * smem + [vm] * (len...  18.5 us
    all_to_all x1, starting transfers between devices, body(): gv = lax.all_to_all(lead, 'wide', split_axis=0, concat_axis=0, tiled=True)  11 us
    ppermute x2, starting transfers between devices, shifted(): lax.ppermute(value, axis, [(i, i + delta) for i in range(size) if 0 <= i...  10.6 us
    ppermute x5, starting transfers between devices, swapped(): return lax.ppermute(value, 'slab', [(i, i ^ mask) for i in range(size)])  8.46 us
    all_to_all x1, waiting for transfers between devices, body(): lax.all_to_all(pieces.reshape(wide_count, zl, 128), 'wide', split_axis=0,...  7.74 us
    all_to_all x1, waiting for transfers between devices, body(): gv = lax.all_to_all(lead, 'wide', split_axis=0, concat_axis=0, tiled=True)  7.69 us
    ppermute x2, starting transfers between devices, from_sides(): return lax.ppermute(value, ('wide', 'slab'), pairs)  6.53 us
    all_to_all x1, starting transfers between devices, body(): lax.all_to_all(pieces.reshape(wide_count, zl, 128), 'wide', split_axis=0,...  6.47 us
  transfers between devices with their start and end apart: 11, of which 5 were waited for; matrix products, arithmetic and copies ran while one was open for 10% of the time, Pallas kernels for 5%

profile of v6, /device:TPU:2, one launch (start us, length us, event | category | flops | bytes accessed | tf_op | source)
XLA Modules:
  0.0 93.7 jit_solution(8775925280122991930)
XLA Ops:
  0.6 0.9 pad_maximum_fusion.4
  1.6 0.7 convert_bitcast_fusion
  2.3 0.7 pad_maximum_fusion.7
  3.1 7.3 %collective-permute-start = (bf16[12,2560]{1,0:T(8,128)(2,1)S(1)}, bf16[12,2560]{1,0:T(8,128)(2,1)S(1)}, u32[]{:S(2)}, u32[]{:S(2)}) collective-permute-start(bf16[12,2560]{1,0:T(8,128)(2,1)S(1)} %constant_dynamic-update-slice_fusion), channel_id=1, source_target_pairs={{0,2},{1,3},{2,0},{3,1},{4,6},{5,7},{6,4},{7,5},{8,10},{9,11},{10,... | collective-permute-start | bytes 184328 | tf_op jit(solution)/shard_map/ppermute | solution.py:41
  10.3 0.7 xor_multiply_fusion
  11.9 0.6 reshape_reshape.3
  13.3 0.6 reshape.410.refs_4_
  15.2 3.5 %collective-permute-start.1 = (bf16[24,96]{1,0:T(8,128)(2,1)S(1)}, bf16[24,96]{1,0:T(8,128)(2,1)S(1)}, u32[]{:S(2)}, u32[]{:S(2)}) collective-permute-start(bf16[24,96]{1,0:T(8,128)(2,1)S(1)} %get-tuple-element.41), channel_id=1, source_target_pairs={{0,4},{4,8},{8,12},{12,16},{16,20},{20,24},{24,28},{28,32},{32,36}... | collective-permute-start | bytes 13832 | tf_op jit(solution)/shard_map/ppermute | solution.py:20
  18.7 7.2 %collective-permute-start.2 = (bf16[24,96]{1,0:T(8,128)(2,1)S(1)}, bf16[24,96]{1,0:T(8,128)(2,1)S(1)}, u32[]{:S(2)}, u32[]{:S(2)}) collective-permute-start(bf16[24,96]{1,0:T(8,128)(2,1)S(1)} %get-tuple-element.42), channel_id=1, source_target_pairs={{4,0},{8,4},{12,8},{16,12},{20,16},{24,20},{28,24},{32,28},{36,32}... | collective-permute-start | bytes 13832 | tf_op jit(solution)/shard_map/ppermute | solution.py:20
  25.9 1.3 %collective-permute-done.2 = bf16[24,96]{1,0:T(8,128)(2,1)S(1)} collective-permute-done((bf16[24,96]{1,0:T(8,128)(2,1)S(1)}, bf16[24,96]{1,0:T(8,128)(2,1)S(1)}, u32[]{:S(2)}, u32[]{:S(2)}) %collective-permute-start.2) | collective-permute-done | bytes 4640 | tf_op jit(solution)/shard_map/ppermute | solution.py:20
  28.0 0.6 collective-permute-done.3
  28.7 3.9 %shard_map.149 = (bf16[10,512]{1,0:T(8,128)(2,1)S(1)}, bf16[64,8,256]{2,1,0:T(8,128)(2,1)}) custom-call(s32[2]{0:T(128)S(1)} %pad_add_fusion.refs_0_, bf16[48,768]{1,0:T(8,128)(2,1)S(1)} %pad_maximum_fusion.3.refs_1_, bf16[256,432]{1,0:T(8,128)(2,1)S(1)} %copy.57.refs_2_, bf16[256,2304]{1,0:T(8,128)(2,1)S(1)} %shard_map.148.refs_3_, ...), custom_call_target="tpu_custom_call" | custom-call | tf_op jit(solution)/shard_map/pallas_call | solution.py:295
  32.6 1.9 %collective-permute-start.5 = (bf16[48,2048]{1,0:T(8,128)(2,1)S(1)}, bf16[48,2048]{1,0:T(8,128)(2,1)S(1)}, u32[]{:S(2)}, u32[]{:S(2)}) collective-permute-start(bf16[48,2048]{1,0:T(8,128)(2,1)S(1)} %pad_maximum_fusion.1.refs_5_), channel_id=1, source_target_pairs={{0,4},{2,6},{4,8},{5,1},{6,10},{7,3},{8,12},{9,5},{10,14},{11,7},{... | collective-permute-start | bytes 589832 | tf_op jit(solution)/shard_map/ppermute | solution.py:36
  34.6 4.6 %collective-permute-start.6 = (bf16[48,1024]{1,0:T(8,128)(2,1)S(1)}, bf16[48,1024]{1,0:T(8,128)(2,1)S(1)}, u32[]{:S(2)}, u32[]{:S(2)}) collective-permute-start(bf16[48,1024]{1,0:T(8,128)(2,1)S(1)} %slice_select_fusion), channel_id=1, source_target_pairs={{0,8},{2,10},{4,12},{6,14},{8,16},{9,1},{10,18},{11,3},{12,20},{13... | collective-permute-start | bytes 294920 | tf_op jit(solution)/shard_map/ppermute | solution.py:36
  39.2 11.0 %all-to-all-start = ((bf16[64,8,256]{2,1,0:T(8,128)(2,1)}), bf16[64,8,256]{2,1,0:T(8,128)(2,1)S(1)}, u32[]{:S(2)}, u32[]{:S(2)}) async-start(bf16[64,8,256]{2,1,0:T(8,128)(2,1)} %get-tuple-element.23), calls=%async_computation | async-start | bytes 524288 | tf_op jit(solution)/shard_map/all_to_all | solution.py:367
  52.5 0.8 shard_map.151.refs_9_
  55.0 7.7 %all-to-all-done = bf16[64,8,256]{2,1,0:T(8,128)(2,1)S(1)} async-done(((bf16[64,8,256]{2,1,0:T(8,128)(2,1)}), bf16[64,8,256]{2,1,0:T(8,128)(2,1)S(1)}, u32[]{:S(2)}, u32[]{:S(2)}) %all-to-all-start) | async-done | bytes 262176 | tf_op jit(solution)/shard_map/all_to_all | solution.py:367
  63.5 1.2 %collective-permute-done.7.refs_3_ = bf16[512,256]{1,0:T(8,128)(2,1)S(1)} collective-permute-done((bf16[512,256]{1,0:T(8,128)(2,1)S(1)}, bf16[512,256]{1,0:T(8,128)(2,1)S(1)}, u32[]{:S(2)}, u32[]{:S(2)}) %collective-permute-start.7) | collective-permute-done | bytes 262176 | tf_op jit(solution)/shard_map/ppermute | solution.py:41
  64.6 10.2 %shard_map.152 = (bf16[2,10,1024]{2,1,0:T(8,128)(2,1)S(1)}, bf16[128,128]{1,0:T(8,128)(2,1)}) custom-call(s32[2]{0:T(128)S(1)} %pad_add_fusion.refs_0_, s32[64,8]{1,0:T(8,128)S(1)} %bitcast.92, bf16[512,256]{1,0:T(8,128)(2,1)S(1)} %bitcast.90, bf16[512,256]{1,0:T(8,128)(2,1)S(1)} %collective-permute-done.7.refs_3_, bf16[512,512]{1,0:T(8,128)(2,1)S(1)} %shard_map.150.refs_4_, ...), custom_call_target="tpu_custom_call" | custom-call | tf_op jit(solution)/shard_map/pallas_call | solution.py:295
  74.9 6.5 %all-to-all-start.1 = ((bf16[64,2,128]{2,1,0:T(2,128)(2,1)}), bf16[64,2,128]{2,1,0:T(2,128)(2,1)S(1)}, u32[]{:S(2)}, u32[]{:S(2)}) async-start(bf16[64,2,128]{2,1,0:T(2,128)(2,1)} %bitcast.39), calls=%async_computation.1 | async-start | bytes 65536 | tf_op jit(solution)/shard_map/all_to_all | solution.py:425
  81.5 0.6 reshape.411
  82.1 0.7 copy.69
  82.8 7.7 %all-to-all-done.1 = bf16[64,2,128]{2,1,0:T(2,128)(2,1)S(1)} async-done(((bf16[64,2,128]{2,1,0:T(2,128)(2,1)}), bf16[64,2,128]{2,1,0:T(2,128)(2,1)S(1)}, u32[]{:S(2)}, u32[]{:S(2)}) %all-to-all-start.1) | async-done | bytes 32800 | tf_op jit(solution)/shard_map/all_to_all | solution.py:425
  90.5 3.2 %shard_map.153 = f32[2,512]{1,0:T(2,128)} custom-call(bf16[128,128]{1,0:T(8,128)(2,1)S(1)} %bitcast.93, f32[128,512]{1,0:T(8,128)S(1)} %add_add_fusion.refs_1_), custom_call_target="tpu_custom_call" | custom-call | tf_op jit(solution)/shard_map/pallas_call | solution.py:295
  (98 shorter events, 8.5 us)
Async XLA Ops:
  0.6 10.6 %copy-start = (bf16[3,3,3,6,32]{4,3,2,1,0:T(8,128)(2,1)S(1)}, bf16[3,3,3,6,32]{4,3,2,1,0:T(8,128)(2,1)}, u32[]{:S(2)}) copy-start(bf16[3,3,3,6,32]{4,3,2,1,0:T(8,128)(2,1)} %param.18) | copy-start | bytes 31108
  3.1 12.1 %collective-permute-start = (bf16[12,2560]{1,0:T(8,128)(2,1)S(1)}, bf16[12,2560]{1,0:T(8,128)(2,1)S(1)}, u32[]{:S(2)}, u32[]{:S(2)}) collective-permute-start(bf16[12,2560]{1,0:T(8,128)(2,1)S(1)} %constant_dynamic-update-slice_fusion), channel_id=1, source_target_pairs={{0,2},{1,3},{2,0},{3,1},{4,6},{5,7},{6,4},{7,5},{8,10},{9,11},{10,... | collective-permute-start | bytes 184328 | tf_op jit(solution)/shard_map/ppermute | solution.py:41
  11.9 0.8 copy-start.5
  13.1 0.9 %copy-start.1 = (bf16[3,3,3,32,32]{4,3,2,1,0:T(8,128)(2,1)S(1)}, bf16[3,3,3,32,32]{4,3,2,1,0:T(8,128)(2,1)}, u32[]{:S(2)}) copy-start(bf16[3,3,3,32,32]{4,3,2,1,0:T(8,128)(2,1)} %param.19) | copy-start | bytes 165892
  15.2 10.7 %collective-permute-start.1 = (bf16[24,96]{1,0:T(8,128)(2,1)S(1)}, bf16[24,96]{1,0:T(8,128)(2,1)S(1)}, u32[]{:S(2)}, u32[]{:S(2)}) collective-permute-start(bf16[24,96]{1,0:T(8,128)(2,1)S(1)} %get-tuple-element.41), channel_id=1, source_target_pairs={{0,4},{4,8},{8,12},{12,16},{16,20},{20,24},{24,28},{28,32},{32,36}... | collective-permute-start | bytes 13832 | tf_op jit(solution)/shard_map/ppermute | solution.py:20
  18.7 8.5 %collective-permute-start.2 = (bf16[24,96]{1,0:T(8,128)(2,1)S(1)}, bf16[24,96]{1,0:T(8,128)(2,1)S(1)}, u32[]{:S(2)}, u32[]{:S(2)}) collective-permute-start(bf16[24,96]{1,0:T(8,128)(2,1)S(1)} %get-tuple-element.42), channel_id=1, source_target_pairs={{4,0},{8,4},{12,8},{16,12},{20,16},{24,20},{28,24},{32,28},{36,32}... | collective-permute-start | bytes 13832 | tf_op jit(solution)/shard_map/ppermute | solution.py:20
  27.3 1.3 %collective-permute-start.3 = (bf16[24,768]{1,0:T(8,128)(2,1)S(1)}, bf16[24,768]{1,0:T(8,128)(2,1)S(1)}, u32[]{:S(2)}, u32[]{:S(2)}) collective-permute-start(bf16[24,768]{1,0:T(8,128)(2,1)S(1)} %pad_maximum_fusion.5), channel_id=1, source_target_pairs={{0,1},{1,0},{2,3},{3,2},{4,5},{5,4},{6,7},{7,6},{8,9},{9,8},{10,11... | collective-permute-start | bytes 110600 | tf_op jit(solution)/shard_map/ppermute | solution.py:41
  27.4 5.2 %collective-permute-start.4 = (bf16[24,2048]{1,0:T(8,128)(2,1)S(1)}, bf16[24,2048]{1,0:T(8,128)(2,1)S(1)}, u32[]{:S(2)}, u32[]{:S(2)}) collective-permute-start(bf16[24,2048]{1,0:T(8,128)(2,1)S(1)} %pad_maximum_fusion.2), channel_id=1, source_target_pairs={{0,1},{1,0},{2,3},{3,2},{4,5},{5,4},{6,7},{7,6},{8,9},{9,8},{10,11... | collective-permute-start | bytes 294920 | tf_op jit(solution)/shard_map/ppermute | solution.py:41
  32.6 17.7 %copy-start.3 = (bf16[3,3,3,7,32]{4,3,2,1,0:T(8,128)(2,1)S(1)}, bf16[3,3,3,7,32]{4,3,2,1,0:T(8,128)(2,1)}, u32[]{:S(2)}) copy-start(bf16[3,3,3,7,32]{4,3,2,1,0:T(8,128)(2,1)} %param.21) | copy-start | bytes 36292
  32.6 17.6 %collective-permute-start.5 = (bf16[48,2048]{1,0:T(8,128)(2,1)S(1)}, bf16[48,2048]{1,0:T(8,128)(2,1)S(1)}, u32[]{:S(2)}, u32[]{:S(2)}) collective-permute-start(bf16[48,2048]{1,0:T(8,128)(2,1)S(1)} %pad_maximum_fusion.1.refs_5_), channel_id=1, source_target_pairs={{0,4},{2,6},{4,8},{5,1},{6,10},{7,3},{8,12},{9,5},{10,14},{11,7},{... | collective-permute-start | bytes 589832 | tf_op jit(solution)/shard_map/ppermute | solution.py:36
  34.6 15.6 %collective-permute-start.6 = (bf16[48,1024]{1,0:T(8,128)(2,1)S(1)}, bf16[48,1024]{1,0:T(8,128)(2,1)S(1)}, u32[]{:S(2)}, u32[]{:S(2)}) collective-permute-start(bf16[48,1024]{1,0:T(8,128)(2,1)S(1)} %slice_select_fusion), channel_id=1, source_target_pairs={{0,8},{2,10},{4,12},{6,14},{8,16},{9,1},{10,18},{11,3},{12,20},{13... | collective-permute-start | bytes 294920 | tf_op jit(solution)/shard_map/ppermute | solution.py:36
  39.2 23.5 %all-to-all-start = ((bf16[64,8,256]{2,1,0:T(8,128)(2,1)}), bf16[64,8,256]{2,1,0:T(8,128)(2,1)S(1)}, u32[]{:S(2)}, u32[]{:S(2)}) async-start(bf16[64,8,256]{2,1,0:T(8,128)(2,1)} %get-tuple-element.23), calls=%async_computation | async-start | bytes 524288 | tf_op jit(solution)/shard_map/all_to_all | solution.py:367
  51.1 1.0 %copy-start.2 = (bf16[3,3,3,32,32]{4,3,2,1,0:T(8,128)(2,1)S(1)}, bf16[3,3,3,32,32]{4,3,2,1,0:T(8,128)(2,1)}, u32[]{:S(2)}) copy-start(bf16[3,3,3,32,32]{4,3,2,1,0:T(8,128)(2,1)} %param.22) | copy-start | bytes 165892
  51.9 1.7 %copy-start.7 = (bf16[3,3,3,32,5]{3,2,4,1,0:T(4,128)(2,1)S(1)}, bf16[3,3,3,32,5]{3,2,4,1,0:T(4,128)(2,1)}, u32[]{:S(2)}) copy-start(bf16[3,3,3,32,5]{3,2,4,1,0:T(4,128)(2,1)} %param.23) | copy-start | bytes 25924
  52.1 1.9 %copy-start.6 = (s32[64,128]{1,0:T(8,128)S(1)}, s32[64,128]{1,0:T(8,128)}, u32[]{:S(2)}) copy-start(s32[64,128]{1,0:T(8,128)} %param.17) | copy-start | bytes 98308
  53.4 10.0 %copy-start.4 = (bf16[5,2,2,1024]{3,2,1,0:T(2,128)(2,1)S(1)}, bf16[5,2,2,1024]{3,2,1,0:T(2,128)(2,1)}, u32[]{:S(2)}) copy-start(bf16[5,2,2,1024]{3,2,1,0:T(2,128)(2,1)} %param.15) | copy-start | bytes 122884
  62.7 2.0 %collective-permute-start.8 = (bf16[48,3072]{1,0:T(8,128)(2,1)S(1)}, bf16[48,3072]{1,0:T(8,128)(2,1)S(1)}, u32[]{:S(2)}, u32[]{:S(2)}) collective-permute-start(bf16[48,3072]{1,0:T(8,128)(2,1)S(1)} %pad_maximum_fusion.refs_6_), channel_id=1, source_target_pairs={{0,1},{1,0},{2,3},{3,2},{4,5},{5,4},{6,7},{7,6},{8,9},{9,8},{10,11... | collective-permute-start | bytes 884744 | tf_op jit(solution)/shard_map/ppermute | solution.py:41
  62.8 1.8 %collective-permute-start.7 = (bf16[512,256]{1,0:T(8,128)(2,1)S(1)}, bf16[512,256]{1,0:T(8,128)(2,1)S(1)}, u32[]{:S(2)}, u32[]{:S(2)}) collective-permute-start(bf16[512,256]{1,0:T(8,128)(2,1)S(1)} %bitcast.89), channel_id=1, source_target_pairs={{0,1},{1,0},{2,3},{3,2},{4,5},{5,4},{6,7},{7,6},{8,9},{9,8},{10,11... | collective-permute-start | bytes 786440 | tf_op jit(solution)/shard_map/ppermute | solution.py:41
  74.9 15.6 %all-to-all-start.1 = ((bf16[64,2,128]{2,1,0:T(2,128)(2,1)}), bf16[64,2,128]{2,1,0:T(2,128)(2,1)S(1)}, u32[]{:S(2)}, u32[]{:S(2)}) async-start(bf16[64,2,128]{2,1,0:T(2,128)(2,1)} %bitcast.39), calls=%async_computation.1 | async-start | bytes 65536 | tf_op jit(solution)/shard_map/all_to_all | solution.py:425
